TPU v7x, 512 devices: a whole 4x8x8 slice. The times are simulated.
512 devices in a mesh: group: 4 (over z_hi), ctx: 8 (over y), sample: 16 (over z_lo, x, core).
Axes of the slice: x: 4, y: 8, z: 8 (z_hi: 4, z_lo: 2; z = z_hi * 2 + z_lo), core: 2. Of those that a mesh axis runs over, the one named last changes fastest.
Arguments:
- q_nope: bfloat16 [8192, 16384], P(('group', 'sample'), 'ctx'), parts along dimension 0, may hold values from -6 to 6
- q_rope: bfloat16 [8192, 8192], P(('group', 'sample'), 'ctx'), parts along dimension 0, may hold values from -400 to 400
- prompt_latent: bfloat16 [1024, 512], P(('group', 'ctx')), parts along dimension 0, may hold values from -6 to 6
- prompt_rope: bfloat16 [1024, 64], P(('group', 'ctx')), parts along dimension 0, may hold values from -4.5 to 4.5
- resp_latent: bfloat16 [8192, 512], P(('group', 'sample')), parts along dimension 0, may hold values from -6 to 6
- resp_rope: bfloat16 [8192, 64], P(('group', 'sample')), parts along dimension 0, may hold values from -6 to 6
- w_key: bfloat16 [512, 16384], P('sample', 'ctx'), may hold values from -0.25 to 0.25
- w_value: bfloat16 [512, 16384], P('sample', 'ctx'), may hold values from -0.25 to 0.25
- out_grad: bfloat16 [8192, 16384], P(('group', 'sample'), 'ctx'), parts along dimension 0, may hold values from -6 to 6
- lengths: int32 [64], P(('group', 'sample')), parts along dimension 0, may hold values from 16 to 128, as said below
- offsets: int32 [64], P(('group', 'sample')), parts along dimension 0, may hold values from 128 to 256, as said below
Outputs:
- attn_out: bfloat16 [8192, 16384], P(('group', 'sample'), 'ctx'), parts along dimension 0
- grad_query_nope: bfloat16 [8192, 16384], P(('group', 'sample'), 'ctx'), parts along dimension 0
- grad_query_rope: bfloat16 [8192, 8192], P(('group', 'sample'), 'ctx'), parts along dimension 0
- grad_prompt_latent: float32 [1024, 512], P(('group', 'ctx')), parts along dimension 0
- grad_prompt_rope: float32 [1024, 64], P(('group', 'ctx')), parts along dimension 0
- grad_resp_latent: float32 [8192, 512], P(('group', 'sample')), parts along dimension 0
- grad_resp_rope: float32 [8192, 64], P(('group', 'sample')), parts along dimension 0
There are 4 independent parts, one for each index of `group`. A program takes and returns all parts, laid end to end along the dimension named above; an argument that names none is the same for every part. Nothing has to cross between parts.
Inputs may be any that keep to these rules, and one draw needn't show every extreme that they name: `lengths`: one response has exactly 128 live slots and one exactly 16. `offsets`: one response follows all 256 prompt rows and one exactly 128.
All inputs are finite; a program needn't handle non-finite values.
Results may differ from a plain program's by a relative error of at most 0.017.
Values may be sent and summed in bfloat16 or wider, within the bound.
No kernel may reach another device: no remote copies, remote signals or barrier semaphores. Data moves between devices by JAX's collectives and lax.ppermute only.
A program may use at most 64 MiB of HBM per device.

v0:
```python
import math

import jax
import jax.numpy as jnp
from jax import lax
from jax.sharding import PartitionSpec as P

NEG_FILL = -1e30


def per_device(
    q_nope,
    q_rope,
    prompt_latent,
    prompt_rope,
    resp_latent,
    resp_rope,
    w_key,
    w_value,
    out_grad,
    lengths,
    offsets,
):
    row_count = q_nope.shape[0]
    rope_width = prompt_rope.shape[1]
    head_count = q_rope.shape[1] // rope_width
    nope_width = q_nope.shape[1] // head_count
    value_width = out_grad.shape[1] // head_count
    score_scale = 1.0 / math.sqrt(nope_width + rope_width)
    query_nope = q_nope.reshape(row_count, head_count, nope_width)
    query_rope = q_rope.reshape(row_count, head_count, rope_width)
    prompt_lat, prompt_rot = (
        lax.all_gather(prompt_latent, "ctx", axis=0, tiled=True),
        lax.all_gather(prompt_rope, "ctx", axis=0, tiled=True),
    )
    prompt_count = prompt_lat.shape[0]
    keys_lat = jnp.concatenate([prompt_lat, resp_latent], axis=0)
    keys_rot = jnp.concatenate([prompt_rot, resp_rope], axis=0)
    slot_index = jnp.arange(row_count, dtype=jnp.int32)
    key_index = jnp.arange(prompt_count + row_count, dtype=jnp.int32)
    live_rows = slot_index < lengths[0]
    visible = jnp.where(
        key_index[None, :] < prompt_count,
        key_index[None, :] < offsets[0],
        key_index[None, :] - prompt_count <= slot_index[:, None],
    )
    grad_rows = jnp.where(live_rows[:, None], out_grad, jnp.zeros_like(out_grad)).reshape(
        row_count, head_count, value_width
    )
    key_all, value_all = (
        lax.all_gather(w_key, "sample", axis=0, tiled=True),
        lax.all_gather(w_value, "sample", axis=0, tiled=True),
    )
    key_all = key_all.reshape(key_all.shape[0], head_count, nope_width)
    value_all = value_all.reshape(value_all.shape[0], head_count, value_width)
    absorbed = jnp.einsum(
        "rhn,lhn->rhl", query_nope, key_all, preferred_element_type=jnp.float32
    ).astype(jnp.bfloat16)
    scores = jnp.einsum("rhl,kl->rhk", absorbed, keys_lat, preferred_element_type=jnp.float32)
    scores = (
        scores + jnp.einsum("rhe,ke->rhk", query_rope, keys_rot, preferred_element_type=jnp.float32)
    ) * score_scale
    scores = jnp.where(visible[:, None, :], scores, NEG_FILL)
    row_max = jnp.max(scores, axis=-1, keepdims=True)
    raised = jnp.exp(scores - row_max)
    probability = raised / jnp.sum(raised, axis=-1, keepdims=True)
    prob_half = probability.astype(jnp.bfloat16)
    latent_out = jnp.einsum(
        "rhk,kl->rhl", prob_half, keys_lat, preferred_element_type=jnp.float32
    ).astype(jnp.bfloat16)
    projected = jnp.einsum(
        "rhl,lhv->rhv", latent_out, value_all, preferred_element_type=jnp.float32
    )
    attn_out = (
        jnp.where(live_rows[:, None, None], projected, 0.0)
        .astype(jnp.bfloat16)
        .reshape(row_count, head_count * value_width)
    )
    grad_latent = jnp.einsum(
        "rhv,lhv->rhl", grad_rows, value_all, preferred_element_type=jnp.float32
    ).astype(jnp.bfloat16)
    grad_probs = jnp.einsum(
        "rhl,kl->rhk", grad_latent, keys_lat, preferred_element_type=jnp.float32
    )
    inner_sum = jnp.sum(probability * grad_probs, axis=-1, keepdims=True)
    grad_scores = (probability * (grad_probs - inner_sum) * score_scale).astype(jnp.bfloat16)
    grad_absorbed = jnp.einsum(
        "rhk,kl->rhl", grad_scores, keys_lat, preferred_element_type=jnp.float32
    ).astype(jnp.bfloat16)
    grad_query_rope = jnp.einsum(
        "rhk,ke->rhe", grad_scores, keys_rot, preferred_element_type=jnp.float32
    ).astype(jnp.bfloat16)
    grad_query_rope = grad_query_rope.reshape(row_count, head_count * rope_width)
    grad_qnope = jnp.einsum(
        "rhl,lhn->rhn", grad_absorbed, key_all, preferred_element_type=jnp.float32
    )
    grad_query_nope = grad_qnope.astype(jnp.bfloat16).reshape(row_count, head_count * nope_width)
    grad_keys_lat = jnp.einsum(
        "rhk,rhl->kl", grad_scores, absorbed, preferred_element_type=jnp.float32
    )
    grad_keys_lat = grad_keys_lat + jnp.einsum(
        "rhk,rhl->kl", prob_half, grad_latent, preferred_element_type=jnp.float32
    )
    grad_keys_rot = jnp.einsum(
        "rhk,rhe->ke", grad_scores, query_rope, preferred_element_type=jnp.float32
    )
    prompt_term_lat = grad_keys_lat[:prompt_count]
    prompt_term_rot = grad_keys_rot[:prompt_count]
    total_lat, total_rot = lax.psum((prompt_term_lat, prompt_term_rot), ("ctx", "sample"))
    owner_count = prompt_count // lax.axis_size("ctx")
    first_owned = lax.axis_index("ctx") * owner_count
    grad_prompt_latent = lax.dynamic_slice_in_dim(total_lat, first_owned, owner_count, 0)
    grad_prompt_rope = lax.dynamic_slice_in_dim(total_rot, first_owned, owner_count, 0)
    grad_resp_latent, grad_resp_rope = (
        lax.psum(grad_keys_lat[prompt_count:].astype(jnp.bfloat16), "ctx").astype(jnp.float32),
        lax.psum(grad_keys_rot[prompt_count:].astype(jnp.bfloat16), "ctx").astype(jnp.float32),
    )
    return (
        attn_out,
        grad_query_nope,
        grad_query_rope,
        grad_prompt_latent,
        grad_prompt_rope,
        grad_resp_latent,
        grad_resp_rope,
    )


def solution(mesh):
    placed = (
        P(("group", "sample"), "ctx"),
        P(("group", "sample"), "ctx"),
        P(("group", "ctx"), None),
        P(("group", "ctx"), None),
        P(("group", "sample"), None),
        P(("group", "sample"), None),
        P("sample", "ctx"),
        P("sample", "ctx"),
        P(("group", "sample"), "ctx"),
        P(("group", "sample")),
        P(("group", "sample")),
    )
    return jax.shard_map(
        per_device,
        mesh=mesh,
        in_specs=placed,
        out_specs=(
            P(("group", "sample"), "ctx"),
            P(("group", "sample"), "ctx"),
            P(("group", "sample"), "ctx"),
            P(("group", "ctx"), None),
            P(("group", "ctx"), None),
            P(("group", "sample"), None),
            P(("group", "sample"), None),
        ),
        check_vma=False,
    )
```

profile of v0, /device:TPU:1, one launch (start us, length us, event | category | flops | bytes accessed | tf_op | source)
XLA Modules:
  0.0 1244.0 jit_solution(14912622951282392525)
XLA Ops:
  11.1 20.8 %all_gather.14 = bf16[256,64]{1,0:T(8,128)(2,1)S(1)} all-gather(bf16[32,64]{1,0:T(8,128)(2,1)} %param.14), channel_id=1, replica_groups=mesh['group'=4,'ctx'=8,'sample'=16] {'ctx'}, dimensions={0}, use_global_device_ids=true | all-gather | bytes 36864 | tf_op jit(solution)/shard_map/all_gather | solution.py:34
  32.1 19.4 %all_gather.13 = bf16[256,512]{1,0:T(8,128)(2,1)S(1)} all-gather(bf16[32,512]{1,0:T(8,128)(2,1)} %param.13), channel_id=1, replica_groups=mesh['group'=4,'ctx'=8,'sample'=16] {'ctx'}, dimensions={0}, use_global_device_ids=true | all-gather | bytes 294912 | tf_op jit(solution)/shard_map/all_gather | solution.py:33
  51.6 4.0 all-gather.3.cloned.1.call-done
  55.5 2.9 copy.52
  59.5 1.3 fusion.13
  61.6 1.7 copy-done.1
  63.3 2.2 fusion.83
  65.5 31.6 %all-gather.5.cloned.1.call-done = bf16[512,2048]{1,0:T(8,128)(2,1)} async-done(((bf16[32,2048]{1,0:T(8,128)(2,1)}), bf16[512,2048]{1,0:T(8,128)(2,1)}) %all-gather.5.cloned.1.call-update) | async-done | bytes 2097168 | tf_op jit(solution)/shard_map/all_gather | solution.py:52
  97.1 2.9 copy.59
  99.9 1.8 convolution_convert_fusion
  103.0 3.0 fusion.9
  106.0 18.4 %fusion.41 = f32[384,512]{1,0:T(8,128)} fusion(bf16[16,512,128]{2,1,0:T(8,128)(2,1)} %copy-done.4, f32[128,16,384]{2,0,1:T(8,128)} %fusion.9, f32[128,16,384]{2,0,1:T(8,128)} %get-tuple-element.31, f32[128,16]{0,1:T(8,128)S(1)} %get-tuple-element.30), kind=kOutput, calls=%fused_computation.30 | convolution fusion | flops 810813824 | bytes 9183232 | tf_op jit(solution)/shard_map/rhk,rhl->kl/dot_general | solution.py:98
  124.4 8.9 fusion.54
  133.3 1.9 slice.18
  135.2 1.6 slice.24
  137.0 15.9 %fusion.60 = f32[384,64]{0,1:T(8,128)S(1)} fusion(bf16[128,16,64]{0,2,1:T(8,128)(2,1)S(1)} %bitcast.84, f32[128,16,384]{2,0,1:T(8,128)} %fusion.9, f32[128,16,384]{2,0,1:T(8,128)} %get-tuple-element.31, f32[128,16]{0,1:T(8,128)S(1)} %get-tuple-element.30), kind=kOutput, calls=%fused_computation.35 | convolution fusion | flops 106170752 | bytes 6660096 | tf_op jit(solution)/shard_map/rhk,rhe->ke/dot_general | solution.py:104
  153.6 8.5 fusion.46
  162.2 2.0 copy.65
  164.2 15.2 %fusion.49 = bf16[16,128,128]{1,2,0:T(8,128)(2,1)S(1)} fusion(bf16[512,16,128]{0,2,1:T(8,128)(2,1)} %bitcast.82, f32[128,16,384]{2,0,1:T(8,128)} %fusion.9, bf16[128,512]{1,0:T(8,128)(2,1)S(1)} %copy-done.5, bf16[256,512]{1,0:T(8,128)(2,1)S(1)} %all_gather.13, f32[128,16,384]{2,0,1:T(8,128)} %get-tuple-element.31, f32[128,16]{0,1:T(8,128)S(1)} %get-tuple-element.30), kind=kOutput, calls=%fused_computation.32 | convolution fusion | flops 1081346432 | bytes 9314304 | tf_op jit(solution)/shard_map/rhl,lhn->rhn/dot_general | solution.py:94
  180.5 15.9 %fusion.57 = bf16[128,16,64]{0,2,1:T(8,128)(2,1)S(1)} fusion(f32[128,16,384]{2,0,1:T(8,128)} %fusion.9, bf16[128,64]{0,1:T(8,128)(2,1)S(1)} %copy-done.6, bf16[256,64]{0,1:T(8,128)(2,1)S(1)} %copy.56, f32[128,16,384]{2,0,1:T(8,128)} %get-tuple-element.31, f32[128,16]{0,1:T(8,128)S(1)} %get-tuple-element.30), kind=kOutput, calls=%fused_computation.34 | convolution fusion | flops 106400128 | bytes 6610944 | tf_op jit(solution)/shard_map/rhk,ke->rhe/dot_general | solution.py:90
  197.2 23.8 %psum.31 = bf16[128,64]{0,1:T(8,128)(2,1)S(1)} all-reduce(bf16[128,64]{0,1:T(8,128)(2,1)S(1)} %slice.25), channel_id=1, replica_groups=mesh['group'=4,'ctx'=8,'sample'=16] {'ctx'}, use_global_device_ids=true, to_apply=%region_6.7 | all-reduce | flops 8192 | bytes 32768 | tf_op jit(solution)/shard_map/psum | solution.py:116
  221.7 1.6 convert_element_type.60
  223.3 1011.2 %all-reduce.6.cloned.1.call-done = (f32[256,512]{1,0:T(8,128)}, f32[256,64]{0,1:T(8,128)}) async-done(((f32[256,512]{1,0:T(8,128)}, f32[256,64]{0,1:T(8,128)}), (f32[256,512]{1,0:T(8,128)}, f32[256,64]{0,1:T(8,128)})) %all-reduce.6.cloned.1.call-update) | async-done | bytes 589840 | tf_op jit(solution)/shard_map/psum | solution.py:109
  1234.5 1.5 constant_dynamic-slice_fusion.1
  (37 shorter events, 10.7 us)
Async XLA Ops:
  7.2 51.3 %copy-start = (bf16[128,2048]{1,0:T(8,128)(2,1)S(1)}, bf16[128,2048]{1,0:T(8,128)(2,1)}, u32[]{:S(2)}) copy-start(bf16[128,2048]{1,0:T(8,128)(2,1)} %param.11) | copy-start | bytes 1572868
  7.2 48.3 %all-gather.3.cloned.1.call-start = ((), (), s32[]{:S(2)}) async-start(), calls=%async_computation | async-start | bytes 2228224 | tf_op jit(solution)/shard_map/all_gather | solution.py:51
  7.9 89.1 %all-gather.5.cloned.1.call-start = ((), (), s32[]{:S(2)}) async-start(), calls=%async_computation.1 | async-start | bytes 2228224 | tf_op jit(solution)/shard_map/all_gather | solution.py:52
  8.7 213.0 %all-reduce.4.cloned.1.call-start = ((), (), s32[]{:S(2)}) async-start(), calls=%async_computation.2 | async-start | bytes 262144 | tf_op jit(solution)/shard_map/psum | solution.py:115
  58.4 2.4 copy-start.2
  58.4 1.0 copy-start.5
  59.5 2.1 copy-start.4
  59.5 1.3 copy-start.6
  61.6 1.7 copy-start.1
  101.7 1.3 copy-start.3
  136.8 1097.7 %all-reduce.6.cloned.1.call-start = ((), (), s32[]{:S(2)}) async-start(), calls=%async_computation.3 | async-start | bytes 1179648 | tf_op jit(solution)/shard_map/psum | solution.py:109
Sparse Core Ops, SparseCore 0:
  10.2 45.3 all-gather.2
  57.7 39.3 all-gather.4
  136.9 71.8 all-reduce.3
  212.5 1021.9 all-reduce.5
where the time goes:
time: 1240 us
  waiting for transfers between devices  1050 us (85%)
  matrix products  90.5 us (7%)
  blocking collectives  64 us (5%)
  local copies, waits for them, and re-layouts  21.2 us (2%)
  between operations  15.3 us (1%)
    psum x1, waiting for transfers between devices, per_device(): lax.psum((prompt_term_lat, prompt_term_rot), ('ctx', 'sample'))  1010 us
    all_gather x1, waiting for transfers between devices, per_device(): lax.all_gather(w_value, 'sample', axis=0, tiled=True)  31.6 us
  transfers between devices with their start and end apart: 4, of which 3 were waited for; matrix products, arithmetic and copies ran while one was open for 6% of the time, Pallas kernels for 0%

commit v1 on v0

v1 whole, which is shorter than its diff:
```python
import math

import jax
import jax.numpy as jnp
from jax import lax
from jax.experimental import pallas as pl
from jax.experimental.pallas import tpu as pltpu
from jax.sharding import PartitionSpec as P

NEG_FILL = -1e30
HEADS_PER_STEP = 4
LAT = 512
WIDE = 640
BF = jnp.bfloat16
F32 = jnp.float32


def spread_weights(w_key, w_value, copies):
    rows, cols = w_key.shape

    def kernel(key_ref, value_ref, out_ref, sems):
        moves = []
        for j in range(copies):
            moves.append(pltpu.make_async_copy(key_ref, out_ref.at[j, pl.ds(0, rows)], sems.at[2 * j]))
            moves.append(pltpu.make_async_copy(value_ref, out_ref.at[j, pl.ds(rows, rows)], sems.at[2 * j + 1]))
        for move in moves:
            move.start()
        for move in moves:
            move.wait()

    return pl.pallas_call(
        kernel,
        out_shape=pltpu.HBM((copies, 2 * rows, cols), BF),
        in_specs=[pl.BlockSpec(memory_space=pltpu.VMEM)] * 2,
        out_specs=pl.BlockSpec(memory_space=pl.ANY),
        scratch_shapes=[pltpu.SemaphoreType.DMA((2 * copies,))],
        name="spread_weights",
    )(w_key, w_value)


def dot(left, right, dims):
    return lax.dot_general(left, right, (dims, ((), ())), preferred_element_type=F32)


def attention(facts, q_nope, q_rope, out_grad, keys, w_own, w_other):
    row_count = q_nope.shape[0]
    key_count = keys.shape[0]
    prompt_count = key_count - row_count
    head_count = q_nope.shape[1] // 128
    hps = HEADS_PER_STEP
    steps = head_count // hps
    chips, two_rows, _ = w_own.shape
    w_rows = two_rows // 2
    ctx_count = 8
    owned = prompt_count // ctx_count
    resp_owned = row_count // ctx_count
    scale = 1.0 / math.sqrt(192.0)
    exp_scale = scale * math.log2(math.e)

    def kernel(facts_ref, qn_ref, qr_ref, og_ref, keys_ref, wk_own, wv_own, wk_oth, wv_oth,
               out_ref, gqn_ref, gqr_ref, prompt_ref, resp_ref, w_all, bias, live, acc, acc_rope):
        step = pl.program_id(0)
        length, offset, ctx, core = facts_ref[0], facts_ref[1], facts_ref[2], facts_ref[3]

        @pl.when(step == 0)
        def _():
            key = lax.broadcasted_iota(jnp.int32, (key_count, row_count), 0)
            slot = lax.broadcasted_iota(jnp.int32, (key_count, row_count), 1)
            block = lax.shift_right_logical(key, 5)
            place = jnp.bitwise_xor(block, ctx) * owned + jnp.bitwise_and(key, owned - 1)
            bias[...] = jnp.where(
                key < prompt_count,
                jnp.where(place < offset, 0.0, NEG_FILL),
                jnp.where(key - prompt_count <= slot, 0.0, NEG_FILL))
            row = lax.broadcasted_iota(jnp.int32, (row_count, 128), 0)
            live[...] = jnp.where(row < length, 1.0, 0.0)
            acc[...] = jnp.zeros_like(acc)
            acc_rope[...] = jnp.zeros_like(acc_rope)

        for j in range(chips):
            own_at = pl.ds(pl.multiple_of(j * 2 * w_rows + core * w_rows, w_rows), w_rows)
            oth_at = pl.ds(pl.multiple_of(j * 2 * w_rows + (1 - core) * w_rows, w_rows), w_rows)
            for h in range(hps):
                src = slice(128 * h, 128 * h + 128)
                w_all[own_at, 256 * h:256 * h + 128] = wk_own[j, :, src]
                w_all[own_at, 256 * h + 128:256 * h + 256] = wv_own[j, :, src]
                w_all[oth_at, 256 * h:256 * h + 128] = wk_oth[j, :, src]
                w_all[oth_at, 256 * h + 128:256 * h + 256] = wv_oth[j, :, src]

        keys_lat = keys_ref[:, :LAT]
        keys_rot = keys_ref[:, LAT:]
        alive = live[...]
        lane = lax.broadcasted_iota(jnp.int32, (row_count, 128), 1)
        grads = []
        rope_pair = []
        rope_sum = None
        for h in range(hps):
            col = slice(128 * h, 128 * h + 128)
            both = dot(keys_lat, w_all[:, 256 * h:256 * h + 256], ((1,), (0,))).astype(BF)
            value = both[:, 128:]
            key_full = jnp.concatenate([both[:, :128], keys_rot], axis=1)
            mine = (lane < 64) if h % 2 == 0 else (lane >= 64)
            rope = jnp.where(mine, qr_ref[:, 128 * (h // 2):128 * (h // 2) + 128].astype(F32), 0.0).astype(BF)
            query = jnp.concatenate([qn_ref[:, col], rope], axis=1)
            grad_out = (og_ref[:, col].astype(F32) * alive).astype(BF)
            scores = dot(key_full, query, ((1,), (1,))) + bias[...]
            top = jnp.max(scores, axis=0, keepdims=True)
            raised = jnp.exp2((scores - top) * exp_scale)
            prob = raised * (1.0 / jnp.sum(raised, axis=0, keepdims=True))
            prob_half = prob.astype(BF)
            grad_prob = dot(value, grad_out, ((1,), (1,)))
            weighed = prob * grad_prob
            inner = jnp.sum(weighed, axis=0, keepdims=True)
            grad_score = ((weighed - prob * inner) * scale).astype(BF)
            attn = dot(prob_half, value, ((0,), (0,)))
            out_ref[:, col] = (attn * alive).astype(BF)
            grad_query = dot(grad_score, key_full, ((0,), (0,)))
            gqn_ref[:, col] = grad_query[:, :128].astype(BF)
            rope_pair.append(grad_query[:, 128:])
            if h % 2 == 1:
                gqr_ref[:, 128 * (h // 2):128 * (h // 2) + 128] = jnp.where(
                    lane < 64, rope_pair[h - 1], rope_pair[h]).astype(BF)
            grad_key = dot(grad_score, query, ((1,), (0,)))
            grad_value = dot(prob_half, grad_out, ((1,), (0,)))
            grads += [grad_key[:, :128].astype(BF), grad_value.astype(BF)]
            rope_sum = grad_key[:, 128:] if rope_sum is None else rope_sum + grad_key[:, 128:]
        acc[...] += dot(jnp.concatenate(grads, axis=1), w_all[...], ((1,), (1,)))
        acc_rope[...] += rope_sum

        @pl.when(step == steps - 1)
        def _():
            for owner in range(ctx_count):
                at = pl.ds(pl.multiple_of(jnp.bitwise_xor(ctx, owner) * owned, owned), owned)
                prompt_ref[owner, :, :LAT] = acc[at, :].astype(BF)
                prompt_ref[owner, :, LAT:] = acc_rope[at, :].astype(BF)
                at = slice(prompt_count + owner * resp_owned, prompt_count + (owner + 1) * resp_owned)
                resp_ref[owner, :, :LAT] = acc[at, :].astype(BF)
                resp_ref[owner, :, LAT:] = acc_rope[at, :].astype(BF)

    wide = 128 * hps
    return pl.pallas_call(
        kernel,
        grid=(steps,),
        in_specs=[
            pl.BlockSpec(memory_space=pltpu.SMEM),
            pl.BlockSpec((row_count, wide), lambda i: (0, i)),
            pl.BlockSpec((row_count, wide // 2), lambda i: (0, i)),
            pl.BlockSpec((row_count, wide), lambda i: (0, i)),
            pl.BlockSpec((key_count, WIDE), lambda i: (0, 0)),
            pl.BlockSpec((chips, w_rows, wide), lambda i: (0, 0, i)),
            pl.BlockSpec((chips, w_rows, wide), lambda i: (0, 1, i)),
            pl.BlockSpec((chips, w_rows, wide), lambda i: (0, 0, i)),
            pl.BlockSpec((chips, w_rows, wide), lambda i: (0, 1, i)),
        ],
        out_specs=[
            pl.BlockSpec((row_count, wide), lambda i: (0, i)),
            pl.BlockSpec((row_count, wide), lambda i: (0, i)),
            pl.BlockSpec((row_count, wide // 2), lambda i: (0, i)),
            pl.BlockSpec((ctx_count, owned, WIDE), lambda i: (0, 0, 0)),
            pl.BlockSpec((ctx_count, resp_owned, WIDE), lambda i: (0, 0, 0)),
        ],
        out_shape=[
            jax.ShapeDtypeStruct(q_nope.shape, BF),
            jax.ShapeDtypeStruct(q_nope.shape, BF),
            jax.ShapeDtypeStruct(q_rope.shape, BF),
            pltpu.HBM((ctx_count, owned, WIDE), BF),
            pltpu.HBM((ctx_count, resp_owned, WIDE), BF),
        ],
        scratch_shapes=[
            pltpu.VMEM((LAT, 256 * hps), BF),
            pltpu.VMEM((key_count, row_count), F32),
            pltpu.VMEM((row_count, 128), F32),
            pltpu.VMEM((key_count, LAT), F32),
            pltpu.VMEM((key_count, 128), F32),
        ],
        compiler_params=pltpu.CompilerParams(vmem_limit_bytes=40 * 2**20),
        cost_estimate=pl.CostEstimate(flops=6 * 10**9, bytes_accessed=8 * 2**20, transcendentals=2048 * 384),
        name="attention",
    )(facts, q_nope, q_rope, out_grad, keys, w_own, w_own, w_other, w_other)


def add_resp(terms, prompt_terms):
    def kernel(terms_ref, through_ref, resp_ref, out_ref):
        del through_ref, out_ref
        total = terms_ref[0].astype(F32)
        for j in range(1, terms.shape[0]):
            total = total + terms_ref[j].astype(F32)
        resp_ref[...] = total.astype(BF)

    return pl.pallas_call(
        kernel,
        in_specs=[pl.BlockSpec(memory_space=pltpu.VMEM), pl.BlockSpec(memory_space=pl.ANY)],
        out_specs=[pl.BlockSpec(memory_space=pltpu.VMEM), pl.BlockSpec(memory_space=pl.ANY)],
        out_shape=[
            jax.ShapeDtypeStruct(terms.shape[1:], BF),
            pltpu.HBM(prompt_terms.shape, BF),
        ],
        input_output_aliases={1: 1},
        name="add_resp",
    )(terms, prompt_terms)


def add_prompt(terms, copies):
    owned = terms.shape[1]

    def kernel(terms_ref, prompt_ref, held, sems):
        total = terms_ref[0].astype(F32)
        for j in range(1, terms.shape[0]):
            total = total + terms_ref[j].astype(F32)
        held[...] = total.astype(BF)
        moves = [pltpu.make_async_copy(held, prompt_ref.at[j], sems.at[j]) for j in range(copies)]
        for move in moves:
            move.start()
        for move in moves:
            move.wait()

    return pl.pallas_call(
        kernel,
        in_specs=[pl.BlockSpec(memory_space=pltpu.VMEM)],
        out_specs=pl.BlockSpec(memory_space=pl.ANY),
        out_shape=pltpu.HBM((copies, owned, WIDE), BF),
        scratch_shapes=[pltpu.VMEM((owned, WIDE), BF), pltpu.SemaphoreType.DMA((copies,))],
        name="add_prompt",
    )(terms)


def finish(facts, prompt_terms, resp_sum):
    samples, owned, _ = prompt_terms.shape
    row_count = resp_sum.shape[0]
    resp_owned = row_count // 8

    def kernel(facts_ref, prompt_ref, resp_ref, plat_ref, prot_ref, rlat_ref, rrot_ref, held):
        ctx = facts_ref[2]
        total = prompt_ref[0].astype(F32)
        for j in range(1, samples):
            total = total + prompt_ref[j].astype(F32)
        plat_ref[...] = total[:, :LAT]
        prot_ref[...] = total[:, LAT:LAT + 64] + total[:, LAT + 64:]
        for owner in range(8):
            at = pl.ds(pl.multiple_of(jnp.bitwise_xor(ctx, owner) * resp_owned, resp_owned), resp_owned)
            rows = resp_ref[at, :].astype(F32)
            to = slice(owner * resp_owned, (owner + 1) * resp_owned)
            rlat_ref[to, :] = rows[:, :LAT]
            held[to, :] = rows[:, LAT:]
        turned = jnp.swapaxes(held[...], 0, 1)
        rrot_ref[...] = turned[:64] + turned[64:]

    vm = pl.BlockSpec(memory_space=pltpu.VMEM)
    return pl.pallas_call(
        kernel,
        in_specs=[pl.BlockSpec(memory_space=pltpu.SMEM), vm, vm],
        out_specs=[vm] * 4,
        out_shape=[
            jax.ShapeDtypeStruct((owned, LAT), F32),
            jax.ShapeDtypeStruct((owned, 64), F32),
            jax.ShapeDtypeStruct((row_count, LAT), F32),
            jax.ShapeDtypeStruct((64, row_count), F32),
        ],
        scratch_shapes=[pltpu.VMEM((row_count, 128), F32)],
        name="finish",
    )(facts, prompt_terms, resp_sum)


def butterfly(block, distances=(1, 2, 4)):
    for k in distances:
        block = jnp.concatenate([block, lax.ppermute(block, "ctx", [(i, i ^ k) for i in range(8)])], axis=0)
    return block


def per_device(
    q_nope,
    q_rope,
    prompt_latent,
    prompt_rope,
    resp_latent,
    resp_rope,
    w_key,
    w_value,
    out_grad,
    lengths,
    offsets,
):
    ctx = lax.axis_index("ctx").astype(jnp.int32)
    core = jnp.bitwise_and(lax.axis_index("sample").astype(jnp.int32), 1)
    facts = jnp.concatenate([lengths, offsets, ctx[None], core[None]])
    same_core = [[2 * chip + c for chip in range(8)] for c in range(2)]
    w_own = lax.all_to_all(
        spread_weights(w_key, w_value, 8), "sample", 0, 0, tiled=True, axis_index_groups=same_core)
    prompt_keys = butterfly(jnp.concatenate([prompt_latent, prompt_rope, prompt_rope], axis=1))
    keys = jnp.concatenate(
        [prompt_keys, jnp.concatenate([resp_latent, resp_rope, resp_rope], axis=1)], axis=0)
    w_own, keys = lax.optimization_barrier((w_own, keys))
    w_other = lax.ppermute(w_own, "sample", [(i, i ^ 1) for i in range(16)])
    attn_out, grad_query_nope, grad_query_rope, prompt_terms, resp_terms = attention(
        facts, q_nope, q_rope, out_grad, keys, w_own, w_other)
    resp_terms = lax.all_to_all(resp_terms, "ctx", 0, 0, tiled=True)
    resp_part, prompt_terms = add_resp(resp_terms, prompt_terms)
    prompt_terms = lax.all_to_all(prompt_terms, "ctx", 0, 0, tiled=True)
    resp_half, prompt_terms = lax.optimization_barrier((butterfly(resp_part, (1, 2)), prompt_terms))
    resp_sum = butterfly(resp_half, (4,))
    prompt_part = lax.all_to_all(add_prompt(prompt_terms, 16), "sample", 0, 0, tiled=True)
    prompt_lat, prompt_rot, resp_lat, resp_rot = finish(facts, prompt_part, resp_sum)
    return (attn_out, grad_query_nope, grad_query_rope, prompt_lat, prompt_rot, resp_lat, resp_rot.T)


def solution(mesh):
    placed = (
        P(("group", "sample"), "ctx"),
        P(("group", "sample"), "ctx"),
        P(("group", "ctx"), None),
        P(("group", "ctx"), None),
        P(("group", "sample"), None),
        P(("group", "sample"), None),
        P("sample", "ctx"),
        P("sample", "ctx"),
        P(("group", "sample"), "ctx"),
        P(("group", "sample")),
        P(("group", "sample")),
    )
    return jax.shard_map(
        per_device,
        mesh=mesh,
        in_specs=placed,
        out_specs=(
            P(("group", "sample"), "ctx"),
            P(("group", "sample"), "ctx"),
            P(("group", "sample"), "ctx"),
            P(("group", "ctx"), None),
            P(("group", "ctx"), None),
            P(("group", "sample"), None),
            P(("group", "sample"), None),
        ),
        check_vma=False,
    )
```

time: 1240 us -> 127 us (0.10)
  waiting for transfers between devices: 1050 us -> 20.4 us
  matrix products: 90.5 us -> 0 us
  starting transfers between devices: 0.34 us -> 57.4 us
  blocking collectives: 64 us -> 12.9 us
  Pallas kernels: 0 us -> 25.6 us
  local copies, waits for them, and re-layouts: 21.2 us -> 3.42 us
  between operations: 15.3 us -> 2.12 us
    psum x2 -> x0, waiting for transfers between devices: 1010 us -> none  [the longest x1 1010 us: per_device(): lax.psum((prompt_term_lat, prompt_term_rot), ('ctx', 'sample'))]
    dot_general x11 -> x0, matrix products: 90.5 us -> none  [the longest x1 18.4 us: per_device(): jnp.einsum('rhk,rhl->kl', grad_scores, absorbed, preferred_element_type=j...]
    all_gather x2 -> x0, blocking collectives: 40.2 us -> none  [the longest x1 20.8 us: per_device(): lax.all_gather(prompt_rope, 'ctx', axis=0, tiled=True)]
    ppermute x0 -> x7, starting transfers between devices: none -> 37.6 us  [the longest x6 28.6 us: butterfly(): lax.ppermute(block, 'ctx', [(i, i ^ k) for i in range(8)])]
    all_gather x2 -> x0, waiting for transfers between devices: 35.5 us -> none  [the longest x1 31.6 us: per_device(): lax.all_gather(w_value, 'sample', axis=0, tiled=True)]
    pallas_call x0 -> x5, Pallas kernels: none -> 25.6 us  [the longest x1 17.6 us: attention(): pl.pallas_call(kernel, grid=(steps,), in_specs=[pl.BlockSpec(memory_space...]
    psum x1 -> x0, blocking collectives: 23.8 us -> none  [per_device(): lax.psum(grad_keys_rot[prompt_count:].astype(jnp.bfloat16), 'ctx')]
    all_to_all x0 -> x3, starting transfers between devices: none -> 19.8 us  [the longest x1 9.53 us: per_device(): lax.all_to_all(add_prompt(prompt_terms, 16), 'sample', 0, 0, tiled=True)]
  transfers between devices with their start and end apart: 4 -> 10, of which waited for: 3 -> 9; matrix products, arithmetic and copies ran while one was open for 6% -> 4% of each run, Pallas kernels for 0% -> 0%
where the time goes in v1:
time: 127 us; the launch traced here: 126 us
  starting transfers between devices  57.4 us (45%)
  Pallas kernels  25.6 us (20%)
  waiting for transfers between devices  20.4 us (16%)
  blocking collectives  12.9 us (10%)
  other arithmetic  4.14 us (3%)
  local copies, waits for them, and re-layouts  3.42 us (3%)
  between operations  2.12 us (2%)
    ppermute x6, starting transfers between devices, butterfly(): lax.ppermute(block, 'ctx', [(i, i ^ k) for i in range(8)])  28.6 us
    pallas_call x1, Pallas kernels, attention(): pl.pallas_call(kernel, grid=(steps,), in_specs=[pl.BlockSpec(memory_space...  17.6 us
    ppermute x6, waiting for transfers between devices, butterfly(): lax.ppermute(block, 'ctx', [(i, i ^ k) for i in range(8)])  16.3 us
    all_to_all x1, blocking collectives, per_device(): resp_terms = lax.all_to_all(resp_terms, 'ctx', 0, 0, tiled=True)  12.9 us
    all_to_all x1, starting transfers between devices, per_device(): lax.all_to_all(add_prompt(prompt_terms, 16), 'sample', 0, 0, tiled=True)  9.53 us
    ppermute x1, starting transfers between devices, per_device(): w_other = lax.ppermute(w_own, 'sample', [(i, i ^ 1) for i in range(16)])  9.04 us
    all_to_all x1, starting transfers between devices, per_device(): lax.all_to_all(spread_weights(w_key, w_value, 8), 'sample', 0, 0, tiled=T...  6.8 us
    all_to_all x1, starting transfers between devices, per_device(): prompt_terms = lax.all_to_all(prompt_terms, 'ctx', 0, 0, tiled=True)  3.43 us
  transfers between devices with their start and end apart: 10, of which 9 were waited for; matrix products, arithmetic and copies ran while one was open for 4% of the time, Pallas kernels for 0%

profile of v1, /device:TPU:1, one launch (start us, length us, event | category | flops | bytes accessed | tf_op | source)
XLA Modules:
  0.0 125.9 jit_solution(9726758929901920062)
XLA Ops:
  0.6 2.4 %spread_weights.1 = bf16[8,64,2048]{2,1,0:T(8,128)(2,1)} custom-call(bf16[32,2048]{1,0:T(8,128)(2,1)} %key_ref.1, bf16[32,2048]{1,0:T(8,128)(2,1)} %value_ref.1), custom_call_target="tpu_custom_call" | custom-call | tf_op jit(solution)/shard_map/spread_weights/pallas_call | solution.py:31
  3.1 6.8 %all-to-all-start = ((bf16[8,64,2048]{2,1,0:T(8,128)(2,1)}), bf16[8,64,2048]{2,1,0:T(8,128)(2,1)S(1)}, u32[]{:S(2)}, u32[]{:S(2)}) async-start(bf16[8,64,2048]{2,1,0:T(8,128)(2,1)} %spread_weights.1), calls=%async_computation | async-start | bytes 4194304 | tf_op jit(solution)/shard_map/all_to_all | solution.py:287
  10.0 3.2 %collective-permute-start = (bf16[32,640]{1,0:T(8,128)(2,1)S(1)}, bf16[32,640]{1,0:T(8,128)(2,1)S(1)}, u32[]{:S(2)}, u32[]{:S(2)}) collective-permute-start(bf16[32,640]{1,0:T(8,128)(2,1)S(1)} %get-tuple-element.37), channel_id=1, source_target_pairs={{0,16},{16,0},{32,48},{48,32},{64,80},{80,64},{96,112},{112,96},{1... | collective-permute-start | bytes 122888 | tf_op jit(solution)/shard_map/ppermute | solution.py:266
  13.2 1.5 %collective-permute-done = bf16[32,640]{1,0:T(8,128)(2,1)S(1)} collective-permute-done((bf16[32,640]{1,0:T(8,128)(2,1)S(1)}, bf16[32,640]{1,0:T(8,128)(2,1)S(1)}, u32[]{:S(2)}, u32[]{:S(2)}) %collective-permute-start) | collective-permute-done | bytes 40992 | tf_op jit(solution)/shard_map/ppermute | solution.py:266
  15.5 4.2 %collective-permute-start.1 = (bf16[64,640]{1,0:T(8,128)(2,1)}, bf16[64,640]{1,0:T(8,128)(2,1)S(1)}, u32[]{:S(2)}, u32[]{:S(2)}) collective-permute-start(bf16[64,640]{1,0:T(8,128)(2,1)} %pad_maximum_fusion.2), channel_id=1, source_target_pairs={{0,32},{16,48},{32,0},{48,16},{64,96},{80,112},{96,64},{112,80},{1... | collective-permute-start | bytes 245768 | tf_op jit(solution)/shard_map/ppermute | solution.py:266
  20.4 1.6 %collective-permute-done.1 = bf16[64,640]{1,0:T(8,128)(2,1)S(1)} collective-permute-done((bf16[64,640]{1,0:T(8,128)(2,1)}, bf16[64,640]{1,0:T(8,128)(2,1)S(1)}, u32[]{:S(2)}, u32[]{:S(2)}) %collective-permute-start.1) | collective-permute-done | bytes 81952 | tf_op jit(solution)/shard_map/ppermute | solution.py:266
  22.2 8.3 %collective-permute-start.2 = (bf16[128,640]{1,0:T(8,128)(2,1)S(1)}, bf16[128,640]{1,0:T(8,128)(2,1)S(1)}, u32[]{:S(2)}, u32[]{:S(2)}) collective-permute-start(bf16[128,640]{1,0:T(8,128)(2,1)S(1)} %pad_maximum_fusion), channel_id=1, source_target_pairs={{0,64},{16,80},{32,96},{48,112},{64,0},{80,16},{96,32},{112,48},{1... | collective-permute-start | bytes 491528 | tf_op jit(solution)/shard_map/ppermute | solution.py:266
  30.5 2.8 %collective-permute-done.2 = bf16[128,640]{1,0:T(8,128)(2,1)S(1)} collective-permute-done((bf16[128,640]{1,0:T(8,128)(2,1)S(1)}, bf16[128,640]{1,0:T(8,128)(2,1)S(1)}, u32[]{:S(2)}, u32[]{:S(2)}) %collective-permute-start.2) | collective-permute-done | bytes 163872 | tf_op jit(solution)/shard_map/ppermute | solution.py:266
  35.1 9.0 %collective-permute-start.3 = (bf16[8,64,2048]{2,1,0:T(8,128)(2,1)S(1)}, bf16[8,64,2048]{2,1,0:T(8,128)(2,1)}, u32[]{:S(2)}, u32[]{:S(2)}) collective-permute-start(bf16[8,64,2048]{2,1,0:T(8,128)(2,1)S(1)} %all-to-all-done.wk_own.wv_own), channel_id=1, source_target_pairs={{0,1},{1,0},{2,3},{3,2},{4,5},{5,4},{6,7},{7,6},{8,9},{9,8},{10,11... | collective-permute-start | bytes 6291464 | tf_op jit(solution)/shard_map/ppermute | solution.py:293
  45.6 2.5 %collective-permute-done.3.wk_oth.wv_oth = bf16[8,64,2048]{2,1,0:T(8,128)(2,1)} collective-permute-done((bf16[8,64,2048]{2,1,0:T(8,128)(2,1)S(1)}, bf16[8,64,2048]{2,1,0:T(8,128)(2,1)}, u32[]{:S(2)}, u32[]{:S(2)}) %collective-permute-start.3) | collective-permute-done | bytes 2097184 | tf_op jit(solution)/shard_map/ppermute | solution.py:293
  48.1 1.0 copy-done.2
  49.1 17.6 %attention.1 = (bf16[128,2048]{1,0:T(8,128)(2,1)}, bf16[128,2048]{1,0:T(8,128)(2,1)}, bf16[128,1024]{1,0:T(8,128)(2,1)}, bf16[8,32,640]{2,1,0:T(8,128)(2,1)}, bf16[8,16,640]{2,1,0:T(8,128)(2,1)}) custom-call(s32[4]{0:T(128)S(1)} %pad_add_fusion.facts_ref, bf16[128,2048]{1,0:T(8,128)(2,1)S(1)} %copy-done.1, bf16[128,1024]{1,0:T(8,128)(2,1)S(1)} %copy-done.3, ...), custom_call_target="tpu_custom_call" | custom-call | flops 6000000000 | bytes 8388608 | tf_op jit(solution)/shard_map/attention/pallas_call | solution.py:141
  66.7 12.9 %all_to_all.20.terms_ref = bf16[8,16,640]{2,1,0:T(8,128)(2,1)} all-to-all(bf16[8,16,640]{2,1,0:T(8,128)(2,1)} %get-tuple-element.27), channel_id=1, replica_groups=mesh['group'=4,'ctx'=8,'sample'=16] {'ctx'}, dimensions={0} | all-to-all | bytes 327680 | tf_op jit(solution)/shard_map/all_to_all | solution.py:296
  79.6 1.5 %add_resp.1 = (bf16[16,640]{1,0:T(8,128)(2,1)}, bf16[8,32,640]{2,1,0:T(8,128)(2,1)}) custom-call(bf16[8,16,640]{2,1,0:T(8,128)(2,1)} %all_to_all.20.terms_ref, bf16[8,32,640]{2,1,0:T(8,128)(2,1)} %get-tuple-element.28.through_ref), custom_call_target="tpu_custom_call", output_to_operand_aliasing={{1}: (1, {})} | custom-call | tf_op jit(solution)/shard_map/add_resp/pallas_call | solution.py:190
  81.1 3.4 %all-to-all-start.2 = ((bf16[8,32,640]{2,1,0:T(8,128)(2,1)}), bf16[8,32,640]{2,1,0:T(8,128)(2,1)S(1)}, u32[]{:S(2)}, u32[]{:S(2)}) async-start(bf16[8,32,640]{2,1,0:T(8,128)(2,1)} %get-tuple-element.30), calls=%async_computation.2 | async-start | bytes 655360 | tf_op jit(solution)/shard_map/all_to_all | solution.py:298
  84.6 3.3 %collective-permute-start.4 = (bf16[16,640]{1,0:T(8,128)(2,1)}, bf16[16,640]{1,0:T(8,128)(2,1)S(1)}, u32[]{:S(2)}, u32[]{:S(2)}) collective-permute-start(bf16[16,640]{1,0:T(8,128)(2,1)} %get-tuple-element.29), channel_id=1, source_target_pairs={{0,16},{16,0},{32,48},{48,32},{64,80},{80,64},{96,112},{112,96},{1... | collective-permute-start | bytes 61448 | tf_op jit(solution)/shard_map/ppermute | solution.py:266
  87.8 4.6 %collective-permute-done.4 = bf16[16,640]{1,0:T(8,128)(2,1)S(1)} collective-permute-done((bf16[16,640]{1,0:T(8,128)(2,1)}, bf16[16,640]{1,0:T(8,128)(2,1)S(1)}, u32[]{:S(2)}, u32[]{:S(2)}) %collective-permute-start.4) | collective-permute-done | bytes 20512 | tf_op jit(solution)/shard_map/ppermute | solution.py:266
  93.2 3.4 %collective-permute-start.5 = (bf16[32,640]{1,0:T(8,128)(2,1)S(1)}, bf16[32,640]{1,0:T(8,128)(2,1)S(1)}, u32[]{:S(2)}, u32[]{:S(2)}) collective-permute-start(bf16[32,640]{1,0:T(8,128)(2,1)S(1)} %pad_maximum_fusion.5), channel_id=1, source_target_pairs={{0,32},{16,48},{32,0},{48,16},{64,96},{80,112},{96,64},{112,80},{1... | collective-permute-start | bytes 122888 | tf_op jit(solution)/shard_map/ppermute | solution.py:266
  96.6 2.2 %collective-permute-done.5 = bf16[32,640]{1,0:T(8,128)(2,1)S(1)} collective-permute-done((bf16[32,640]{1,0:T(8,128)(2,1)S(1)}, bf16[32,640]{1,0:T(8,128)(2,1)S(1)}, u32[]{:S(2)}, u32[]{:S(2)}) %collective-permute-start.5) | collective-permute-done | bytes 40992 | tf_op jit(solution)/shard_map/ppermute | solution.py:266
  100.3 2.0 %add_prompt.1 = bf16[16,32,640]{2,1,0:T(8,128)(2,1)} custom-call(bf16[8,32,640]{2,1,0:T(8,128)(2,1)} %copy-done.5), custom_call_target="tpu_custom_call" | custom-call | tf_op jit(solution)/shard_map/add_prompt/pallas_call | solution.py:217
  102.3 9.5 %all-to-all-start.3 = ((bf16[16,32,640]{2,1,0:T(8,128)(2,1)}), bf16[16,32,640]{2,1,0:T(8,128)(2,1)S(1)}, u32[]{:S(2)}, u32[]{:S(2)}) async-start(bf16[16,32,640]{2,1,0:T(8,128)(2,1)} %add_prompt.1), calls=%async_computation.3 | async-start | bytes 1310720 | tf_op jit(solution)/shard_map/all_to_all | solution.py:301
  111.8 6.2 %collective-permute-start.6 = (bf16[64,640]{1,0:T(8,128)(2,1)S(1)}, bf16[64,640]{1,0:T(8,128)(2,1)S(1)}, u32[]{:S(2)}, u32[]{:S(2)}) collective-permute-start(bf16[64,640]{1,0:T(8,128)(2,1)S(1)} %pad_maximum_fusion.3), channel_id=1, source_target_pairs={{0,64},{16,80},{32,96},{48,112},{64,0},{80,16},{96,32},{112,48},{1... | collective-permute-start | bytes 245768 | tf_op jit(solution)/shard_map/ppermute | solution.py:266
  118.0 3.6 %collective-permute-done.6 = bf16[64,640]{1,0:T(8,128)(2,1)S(1)} collective-permute-done((bf16[64,640]{1,0:T(8,128)(2,1)S(1)}, bf16[64,640]{1,0:T(8,128)(2,1)S(1)}, u32[]{:S(2)}, u32[]{:S(2)}) %collective-permute-start.6) | collective-permute-done | bytes 81952 | tf_op jit(solution)/shard_map/ppermute | solution.py:266
  123.9 2.0 %finish.1 = (f32[32,512]{1,0:T(8,128)}, f32[32,64]{1,0:T(8,128)}, f32[128,512]{1,0:T(8,128)}, f32[64,128]{1,0:T(8,128)}) custom-call(s32[4]{0:T(128)} %copy-done, bf16[16,32,640]{2,1,0:T(8,128)(2,1)} %copy-done.4, bf16[128,640]{1,0:T(8,128)(2,1)} %pad_maximum_fusion.1.resp_ref), custom_call_target="tpu_custom_call" | custom-call | tf_op jit(solution)/shard_map/finish/pallas_call | solution.py:249
  (32 shorter events, 8.1 us)
Async XLA Ops:
  3.1 6.9 %copy-start.6 = (bf16[32,512]{1,0:T(8,128)(2,1)S(1)}, bf16[32,512]{1,0:T(8,128)(2,1)}, u32[]{:S(2)}) copy-start(bf16[32,512]{1,0:T(8,128)(2,1)} %param.13) | copy-start | bytes 98308
  3.1 6.9 %copy-start.7 = (bf16[32,64]{1,0:T(8,128)(2,1)S(1)}, bf16[32,64]{1,0:T(8,128)(2,1)}, u32[]{:S(2)}) copy-start(bf16[32,64]{1,0:T(8,128)(2,1)} %param.14) | copy-start | bytes 12292
  3.1 16.6 %copy-start.8 = (bf16[128,64]{0,1:T(8,128)(2,1)S(1)}, bf16[128,64]{0,1:T(8,128)(2,1)}, u32[]{:S(2)}) copy-start(bf16[128,64]{0,1:T(8,128)(2,1)} %param.16) | copy-start | bytes 49156
  3.1 45.0 %copy-start.1 = (bf16[128,2048]{1,0:T(8,128)(2,1)S(1)}, bf16[128,2048]{1,0:T(8,128)(2,1)}, u32[]{:S(2)}) copy-start(bf16[128,2048]{1,0:T(8,128)(2,1)} %qn_ref.1) | copy-start | bytes 1572868
  3.1 44.9 %copy-start.3 = (bf16[128,1024]{1,0:T(8,128)(2,1)S(1)}, bf16[128,1024]{1,0:T(8,128)(2,1)}, u32[]{:S(2)}) copy-start(bf16[128,1024]{1,0:T(8,128)(2,1)} %qr_ref.1) | copy-start | bytes 786436
  3.1 32.0 %all-to-all-start = ((bf16[8,64,2048]{2,1,0:T(8,128)(2,1)}), bf16[8,64,2048]{2,1,0:T(8,128)(2,1)S(1)}, u32[]{:S(2)}, u32[]{:S(2)}) async-start(bf16[8,64,2048]{2,1,0:T(8,128)(2,1)} %spread_weights.1), calls=%async_computation | async-start | bytes 4194304 | tf_op jit(solution)/shard_map/all_to_all | solution.py:287
  10.0 4.7 %collective-permute-start = (bf16[32,640]{1,0:T(8,128)(2,1)S(1)}, bf16[32,640]{1,0:T(8,128)(2,1)S(1)}, u32[]{:S(2)}, u32[]{:S(2)}) collective-permute-start(bf16[32,640]{1,0:T(8,128)(2,1)S(1)} %get-tuple-element.37), channel_id=1, source_target_pairs={{0,16},{16,0},{32,48},{48,32},{64,80},{80,64},{96,112},{112,96},{1... | collective-permute-start | bytes 122888 | tf_op jit(solution)/shard_map/ppermute | solution.py:266
  15.5 6.6 %collective-permute-start.1 = (bf16[64,640]{1,0:T(8,128)(2,1)}, bf16[64,640]{1,0:T(8,128)(2,1)S(1)}, u32[]{:S(2)}, u32[]{:S(2)}) collective-permute-start(bf16[64,640]{1,0:T(8,128)(2,1)} %pad_maximum_fusion.2), channel_id=1, source_target_pairs={{0,32},{16,48},{32,0},{48,16},{64,96},{80,112},{96,64},{112,80},{1... | collective-permute-start | bytes 245768 | tf_op jit(solution)/shard_map/ppermute | solution.py:266
  22.2 11.1 %collective-permute-start.2 = (bf16[128,640]{1,0:T(8,128)(2,1)S(1)}, bf16[128,640]{1,0:T(8,128)(2,1)S(1)}, u32[]{:S(2)}, u32[]{:S(2)}) collective-permute-start(bf16[128,640]{1,0:T(8,128)(2,1)S(1)} %pad_maximum_fusion), channel_id=1, source_target_pairs={{0,64},{16,80},{32,96},{48,112},{64,0},{80,16},{96,32},{112,48},{1... | collective-permute-start | bytes 491528 | tf_op jit(solution)/shard_map/ppermute | solution.py:266
  35.1 12.9 %collective-permute-start.3 = (bf16[8,64,2048]{2,1,0:T(8,128)(2,1)S(1)}, bf16[8,64,2048]{2,1,0:T(8,128)(2,1)}, u32[]{:S(2)}, u32[]{:S(2)}) collective-permute-start(bf16[8,64,2048]{2,1,0:T(8,128)(2,1)S(1)} %all-to-all-done.wk_own.wv_own), channel_id=1, source_target_pairs={{0,1},{1,0},{2,3},{3,2},{4,5},{5,4},{6,7},{7,6},{8,9},{9,8},{10,11... | collective-permute-start | bytes 6291464 | tf_op jit(solution)/shard_map/ppermute | solution.py:293
  45.6 21.2 %copy-start = (s32[4]{0:T(128)}, s32[4]{0:T(128)S(1)}, u32[]{:S(2)}) copy-start(s32[4]{0:T(128)S(1)} %pad_add_fusion.facts_ref) | copy-start | bytes 52
  48.1 1.0 copy-start.2
  81.1 18.4 %all-to-all-start.2 = ((bf16[8,32,640]{2,1,0:T(8,128)(2,1)}), bf16[8,32,640]{2,1,0:T(8,128)(2,1)S(1)}, u32[]{:S(2)}, u32[]{:S(2)}) async-start(bf16[8,32,640]{2,1,0:T(8,128)(2,1)} %get-tuple-element.30), calls=%async_computation.2 | async-start | bytes 655360 | tf_op jit(solution)/shard_map/all_to_all | solution.py:298
  84.6 7.9 %collective-permute-start.4 = (bf16[16,640]{1,0:T(8,128)(2,1)}, bf16[16,640]{1,0:T(8,128)(2,1)S(1)}, u32[]{:S(2)}, u32[]{:S(2)}) collective-permute-start(bf16[16,640]{1,0:T(8,128)(2,1)} %get-tuple-element.29), channel_id=1, source_target_pairs={{0,16},{16,0},{32,48},{48,32},{64,80},{80,64},{96,112},{112,96},{1... | collective-permute-start | bytes 61448 | tf_op jit(solution)/shard_map/ppermute | solution.py:266
  93.2 5.6 %collective-permute-start.5 = (bf16[32,640]{1,0:T(8,128)(2,1)S(1)}, bf16[32,640]{1,0:T(8,128)(2,1)S(1)}, u32[]{:S(2)}, u32[]{:S(2)}) collective-permute-start(bf16[32,640]{1,0:T(8,128)(2,1)S(1)} %pad_maximum_fusion.5), channel_id=1, source_target_pairs={{0,32},{16,48},{32,0},{48,16},{64,96},{80,112},{96,64},{112,80},{1... | collective-permute-start | bytes 122888 | tf_op jit(solution)/shard_map/ppermute | solution.py:266
  99.5 0.7 copy-start.5
  102.3 20.8 %all-to-all-start.3 = ((bf16[16,32,640]{2,1,0:T(8,128)(2,1)}), bf16[16,32,640]{2,1,0:T(8,128)(2,1)S(1)}, u32[]{:S(2)}, u32[]{:S(2)}) async-start(bf16[16,32,640]{2,1,0:T(8,128)(2,1)} %add_prompt.1), calls=%async_computation.3 | async-start | bytes 1310720 | tf_op jit(solution)/shard_map/all_to_all | solution.py:301
  111.8 9.8 %collective-permute-start.6 = (bf16[64,640]{1,0:T(8,128)(2,1)S(1)}, bf16[64,640]{1,0:T(8,128)(2,1)S(1)}, u32[]{:S(2)}, u32[]{:S(2)}) collective-permute-start(bf16[64,640]{1,0:T(8,128)(2,1)S(1)} %pad_maximum_fusion.3), channel_id=1, source_target_pairs={{0,64},{16,80},{32,96},{48,112},{64,0},{80,16},{96,32},{112,48},{1... | collective-permute-start | bytes 245768 | tf_op jit(solution)/shard_map/ppermute | solution.py:266
  123.1 0.9 copy-start.4

commit v2 on v1

--- a/solution.py
+++ b/solution.py
@@ -8,7 +8,7 @@
 from jax.sharding import PartitionSpec as P
 
 NEG_FILL = -1e30
-HEADS_PER_STEP = 4
+HEADS_PER_STEP = 8
 LAT = 512
 WIDE = 640
 BF = jnp.bfloat16
@@ -34,8 +34,14 @@
         in_specs=[pl.BlockSpec(memory_space=pltpu.VMEM)] * 2,
         out_specs=pl.BlockSpec(memory_space=pl.ANY),
         scratch_shapes=[pltpu.SemaphoreType.DMA((2 * copies,))],
+        compiler_params=pltpu.CompilerParams(vmem_limit_bytes=2 * 2**20),
         name="spread_weights",
     )(w_key, w_value)
+
+
+def turn3(number):
+    low = lax.shift_left(jnp.bitwise_and(number, 1), 2)
+    return low + jnp.bitwise_and(number, 2) + lax.shift_right_logical(number, 2)
 
 
 def dot(left, right, dims):
@@ -67,7 +73,7 @@
             key = lax.broadcasted_iota(jnp.int32, (key_count, row_count), 0)
             slot = lax.broadcasted_iota(jnp.int32, (key_count, row_count), 1)
             block = lax.shift_right_logical(key, 5)
-            place = jnp.bitwise_xor(block, ctx) * owned + jnp.bitwise_and(key, owned - 1)
+            place = jnp.bitwise_xor(turn3(block), ctx) * owned + jnp.bitwise_and(key, owned - 1)
             bias[...] = jnp.where(
                 key < prompt_count,
                 jnp.where(place < offset, 0.0, NEG_FILL),
@@ -91,46 +97,49 @@
         keys_rot = keys_ref[:, LAT:]
         alive = live[...]
         lane = lax.broadcasted_iota(jnp.int32, (row_count, 128), 1)
-        grads = []
-        rope_pair = []
-        rope_sum = None
-        for h in range(hps):
-            col = slice(128 * h, 128 * h + 128)
-            both = dot(keys_lat, w_all[:, 256 * h:256 * h + 256], ((1,), (0,))).astype(BF)
-            value = both[:, 128:]
-            key_full = jnp.concatenate([both[:, :128], keys_rot], axis=1)
+        heads = range(hps)
+        cols = [slice(128 * h, 128 * h + 128) for h in heads]
+        both = [dot(keys_lat, w_all[:, 256 * h:256 * h + 256], ((1,), (0,))).astype(BF) for h in heads]
+        value = [b[:, 128:] for b in both]
+        key_full = [jnp.concatenate([b[:, :128], keys_rot], axis=1) for b in both]
+        query = []
+        for h in heads:
             mine = (lane < 64) if h % 2 == 0 else (lane >= 64)
             rope = jnp.where(mine, qr_ref[:, 128 * (h // 2):128 * (h // 2) + 128].astype(F32), 0.0).astype(BF)
-            query = jnp.concatenate([qn_ref[:, col], rope], axis=1)
-            grad_out = (og_ref[:, col].astype(F32) * alive).astype(BF)
-            scores = dot(key_full, query, ((1,), (1,))) + bias[...]
-            top = jnp.max(scores, axis=0, keepdims=True)
-            raised = jnp.exp2((scores - top) * exp_scale)
+            query.append(jnp.concatenate([qn_ref[:, cols[h]], rope], axis=1))
+        grad_out = [(og_ref[:, c].astype(F32) * alive).astype(BF) for c in cols]
+        scores = [dot(key_full[h], query[h], ((1,), (1,))) + bias[...] for h in heads]
+        grad_prob = [dot(value[h], grad_out[h], ((1,), (1,))) for h in heads]
+        prob_half, grad_score = [], []
+        for h in heads:
+            top = jnp.max(scores[h], axis=0, keepdims=True)
+            raised = jnp.exp2((scores[h] - top) * exp_scale)
             prob = raised * (1.0 / jnp.sum(raised, axis=0, keepdims=True))
-            prob_half = prob.astype(BF)
-            grad_prob = dot(value, grad_out, ((1,), (1,)))
-            weighed = prob * grad_prob
+            prob_half.append(prob.astype(BF))
+            weighed = prob * grad_prob[h]
             inner = jnp.sum(weighed, axis=0, keepdims=True)
-            grad_score = ((weighed - prob * inner) * scale).astype(BF)
-            attn = dot(prob_half, value, ((0,), (0,)))
-            out_ref[:, col] = (attn * alive).astype(BF)
-            grad_query = dot(grad_score, key_full, ((0,), (0,)))
-            gqn_ref[:, col] = grad_query[:, :128].astype(BF)
-            rope_pair.append(grad_query[:, 128:])
+            grad_score.append(((weighed - prob * inner) * scale).astype(BF))
+        attn = [dot(prob_half[h], value[h], ((0,), (0,))) for h in heads]
+        grad_query = [dot(grad_score[h], key_full[h], ((0,), (0,))) for h in heads]
+        grad_key = [dot(grad_score[h], query[h], ((1,), (0,))) for h in heads]
+        grad_value = [dot(prob_half[h], grad_out[h], ((1,), (0,))) for h in heads]
+        grads = []
+        rope_sum = None
+        for h in heads:
+            out_ref[:, cols[h]] = (attn[h] * alive).astype(BF)
+            gqn_ref[:, cols[h]] = grad_query[h][:, :128].astype(BF)
             if h % 2 == 1:
-                gqr_ref[:, 128 * (h // 2):128 * (h // 2) + 128] = jnp.where(
-                    lane < 64, rope_pair[h - 1], rope_pair[h]).astype(BF)
-            grad_key = dot(grad_score, query, ((1,), (0,)))
-            grad_value = dot(prob_half, grad_out, ((1,), (0,)))
-            grads += [grad_key[:, :128].astype(BF), grad_value.astype(BF)]
-            rope_sum = grad_key[:, 128:] if rope_sum is None else rope_sum + grad_key[:, 128:]
+                gqr_ref[:, cols[h // 2]] = jnp.where(
+                    lane < 64, grad_query[h - 1][:, 128:], grad_query[h][:, 128:]).astype(BF)
+            grads += [grad_key[h][:, :128].astype(BF), grad_value[h].astype(BF)]
+            rope_sum = grad_key[h][:, 128:] if rope_sum is None else rope_sum + grad_key[h][:, 128:]
         acc[...] += dot(jnp.concatenate(grads, axis=1), w_all[...], ((1,), (1,)))
         acc_rope[...] += rope_sum
 
         @pl.when(step == steps - 1)
         def _():
             for owner in range(ctx_count):
-                at = pl.ds(pl.multiple_of(jnp.bitwise_xor(ctx, owner) * owned, owned), owned)
+                at = pl.ds(pl.multiple_of(turn3(jnp.bitwise_xor(ctx, owner)) * owned, owned), owned)
                 prompt_ref[owner, :, :LAT] = acc[at, :].astype(BF)
                 prompt_ref[owner, :, LAT:] = acc_rope[at, :].astype(BF)
                 at = slice(prompt_count + owner * resp_owned, prompt_count + (owner + 1) * resp_owned)
@@ -173,7 +182,7 @@
             pltpu.VMEM((key_count, LAT), F32),
             pltpu.VMEM((key_count, 128), F32),
         ],
-        compiler_params=pltpu.CompilerParams(vmem_limit_bytes=40 * 2**20),
+        compiler_params=pltpu.CompilerParams(vmem_limit_bytes=28 * 2**20),
         cost_estimate=pl.CostEstimate(flops=6 * 10**9, bytes_accessed=8 * 2**20, transcendentals=2048 * 384),
         name="attention",
     )(facts, q_nope, q_rope, out_grad, keys, w_own, w_own, w_other, w_other)
@@ -196,6 +205,7 @@
             pltpu.HBM(prompt_terms.shape, BF),
         ],
         input_output_aliases={1: 1},
+        compiler_params=pltpu.CompilerParams(vmem_limit_bytes=4 * 2**20),
         name="add_resp",
     )(terms, prompt_terms)
 
@@ -220,6 +230,7 @@
         out_specs=pl.BlockSpec(memory_space=pl.ANY),
         out_shape=pltpu.HBM((copies, owned, WIDE), BF),
         scratch_shapes=[pltpu.VMEM((owned, WIDE), BF), pltpu.SemaphoreType.DMA((copies,))],
+        compiler_params=pltpu.CompilerParams(vmem_limit_bytes=4 * 2**20),
         name="add_prompt",
     )(terms)
 
@@ -237,7 +248,7 @@
         plat_ref[...] = total[:, :LAT]
         prot_ref[...] = total[:, LAT:LAT + 64] + total[:, LAT + 64:]
         for owner in range(8):
-            at = pl.ds(pl.multiple_of(jnp.bitwise_xor(ctx, owner) * resp_owned, resp_owned), resp_owned)
+            at = pl.ds(pl.multiple_of(turn3(jnp.bitwise_xor(ctx, owner)) * resp_owned, resp_owned), resp_owned)
             rows = resp_ref[at, :].astype(F32)
             to = slice(owner * resp_owned, (owner + 1) * resp_owned)
             rlat_ref[to, :] = rows[:, :LAT]
@@ -257,11 +268,12 @@
             jax.ShapeDtypeStruct((64, row_count), F32),
         ],
         scratch_shapes=[pltpu.VMEM((row_count, 128), F32)],
+        compiler_params=pltpu.CompilerParams(vmem_limit_bytes=4 * 2**20),
         name="finish",
     )(facts, prompt_terms, resp_sum)
 
 
-def butterfly(block, distances=(1, 2, 4)):
+def butterfly(block, distances=(4, 2, 1)):
     for k in distances:
         block = jnp.concatenate([block, lax.ppermute(block, "ctx", [(i, i ^ k) for i in range(8)])], axis=0)
     return block
@@ -296,8 +308,8 @@
     resp_terms = lax.all_to_all(resp_terms, "ctx", 0, 0, tiled=True)
     resp_part, prompt_terms = add_resp(resp_terms, prompt_terms)
     prompt_terms = lax.all_to_all(prompt_terms, "ctx", 0, 0, tiled=True)
-    resp_half, prompt_terms = lax.optimization_barrier((butterfly(resp_part, (1, 2)), prompt_terms))
-    resp_sum = butterfly(resp_half, (4,))
+    resp_half, prompt_terms = lax.optimization_barrier((butterfly(resp_part, (4,)), prompt_terms))
+    resp_sum = butterfly(resp_half, (2, 1))
     prompt_part = lax.all_to_all(add_prompt(prompt_terms, 16), "sample", 0, 0, tiled=True)
     prompt_lat, prompt_rot, resp_lat, resp_rot = finish(facts, prompt_part, resp_sum)
     return (attn_out, grad_query_nope, grad_query_rope, prompt_lat, prompt_rot, resp_lat, resp_rot.T)

time: 127 us -> 113 us (0.89)
  Pallas kernels: 25.6 us -> 15.4 us
  starting transfers between devices: 57.4 us -> 51 us
  waiting for transfers between devices: 20.4 us -> 23.7 us
  other arithmetic: 4.14 us -> 2.02 us
    pallas_call x1, Pallas kernels: 17.6 us -> 11.4 us  [attention(): pl.pallas_call(kernel, grid=(steps,), in_specs=[pl.BlockSpec(memory_space...]
    ppermute x6, waiting for transfers between devices: 16.3 us -> 20.9 us  [butterfly(): lax.ppermute(block, 'ctx', [(i, i ^ k) for i in range(8)])]
    ppermute x6, starting transfers between devices: 28.6 us -> 25 us  [butterfly(): lax.ppermute(block, 'ctx', [(i, i ^ k) for i in range(8)])]
    concatenate x5, other arithmetic: 2.94 us -> 0.82 us  [butterfly(): jnp.concatenate([block, lax.ppermute(block, 'ctx', [(i, i ^ k) for i in r...]
    ppermute x1, starting transfers between devices: 9.04 us -> 6.95 us  [per_device(): w_other = lax.ppermute(w_own, 'sample', [(i, i ^ 1) for i in range(16)])]
    pallas_call x1, Pallas kernels: 1.55 us -> 0.03 us  [add_resp(): pl.pallas_call(kernel, in_specs=[pl.BlockSpec(memory_space=pltpu.VMEM), p...]
    unnamed x22 -> x20, local copies, waits for them, and re-layouts: 3.42 us -> 3.65 us
  transfers between devices with their start and end apart: 10 -> 10, of which waited for: 9 -> 8; matrix products, arithmetic and copies ran while one was open for 4% -> 3% of each run, Pallas kernels for 0% -> 0%
where the time goes in v2:
time: 113 us; the launch traced here: 112 us
  starting transfers between devices  51 us (45%)
  waiting for transfers between devices  23.7 us (21%)
  Pallas kernels  15.4 us (14%)
  blocking collectives  13.6 us (12%)
  local copies, waits for them, and re-layouts  3.65 us (3%)
  between operations  2.13 us (2%)
  other arithmetic  2.02 us (2%)
    ppermute x6, starting transfers between devices, butterfly(): lax.ppermute(block, 'ctx', [(i, i ^ k) for i in range(8)])  25 us
    ppermute x6, waiting for transfers between devices, butterfly(): lax.ppermute(block, 'ctx', [(i, i ^ k) for i in range(8)])  20.9 us
    all_to_all x1, blocking collectives, per_device(): resp_terms = lax.all_to_all(resp_terms, 'ctx', 0, 0, tiled=True)  13.6 us
    pallas_call x1, Pallas kernels, attention(): pl.pallas_call(kernel, grid=(steps,), in_specs=[pl.BlockSpec(memory_space...  11.4 us
    all_to_all x1, starting transfers between devices, per_device(): lax.all_to_all(add_prompt(prompt_terms, 16), 'sample', 0, 0, tiled=True)  8.82 us
    ppermute x1, starting transfers between devices, per_device(): w_other = lax.ppermute(w_own, 'sample', [(i, i ^ 1) for i in range(16)])  6.95 us
    all_to_all x1, starting transfers between devices, per_device(): lax.all_to_all(spread_weights(w_key, w_value, 8), 'sample', 0, 0, tiled=T...  6.8 us
    unnamed x20, local copies, waits for them, and re-layouts  3.65 us
  transfers between devices with their start and end apart: 10, of which 8 were waited for; matrix products, arithmetic and copies ran while one was open for 3% of the time, Pallas kernels for 0%

profile of v2, /device:TPU:1, one launch (start us, length us, event | category | flops | bytes accessed | tf_op | source)
XLA Modules:
  0.0 111.6 jit_solution(14799506895805802540)
XLA Ops:
  2.4 1.5 %spread_weights.1 = bf16[8,64,2048]{2,1,0:T(8,128)(2,1)} custom-call(bf16[32,2048]{1,0:T(8,128)(2,1)S(1)} %copy-done, bf16[32,2048]{1,0:T(8,128)(2,1)S(1)} %copy-done.1), custom_call_target="tpu_custom_call" | custom-call | tf_op jit(solution)/shard_map/spread_weights/pallas_call | solution.py:31
  4.0 6.8 %all-to-all-start = ((bf16[8,64,2048]{2,1,0:T(8,128)(2,1)}), bf16[8,64,2048]{2,1,0:T(8,128)(2,1)S(1)}, u32[]{:S(2)}, u32[]{:S(2)}) async-start(bf16[8,64,2048]{2,1,0:T(8,128)(2,1)} %spread_weights.1), calls=%async_computation | async-start | bytes 4194304 | tf_op jit(solution)/shard_map/all_to_all | solution.py:299
  10.9 7.4 %collective-permute-start = (bf16[32,640]{1,0:T(8,128)(2,1)S(1)}, bf16[32,640]{1,0:T(8,128)(2,1)S(1)}, u32[]{:S(2)}, u32[]{:S(2)}) collective-permute-start(bf16[32,640]{1,0:T(8,128)(2,1)S(1)} %get-tuple-element.37), channel_id=1, source_target_pairs={{0,64},{16,80},{32,96},{48,112},{64,0},{80,16},{96,32},{112,48},{1... | collective-permute-start | bytes 122888 | tf_op jit(solution)/shard_map/ppermute | solution.py:278
  18.3 1.4 %collective-permute-done = bf16[32,640]{1,0:T(8,128)(2,1)S(1)} collective-permute-done((bf16[32,640]{1,0:T(8,128)(2,1)S(1)}, bf16[32,640]{1,0:T(8,128)(2,1)S(1)}, u32[]{:S(2)}, u32[]{:S(2)}) %collective-permute-start) | collective-permute-done | bytes 40992 | tf_op jit(solution)/shard_map/ppermute | solution.py:278
  20.5 4.5 %collective-permute-start.1 = (bf16[64,640]{1,0:T(8,128)(2,1)}, bf16[64,640]{1,0:T(8,128)(2,1)S(1)}, u32[]{:S(2)}, u32[]{:S(2)}) collective-permute-start(bf16[64,640]{1,0:T(8,128)(2,1)} %pad_maximum_fusion.2), channel_id=1, source_target_pairs={{0,32},{16,48},{32,0},{48,16},{64,96},{80,112},{96,64},{112,80},{1... | collective-permute-start | bytes 245768 | tf_op jit(solution)/shard_map/ppermute | solution.py:278
  25.7 2.5 %collective-permute-done.1 = bf16[64,640]{1,0:T(8,128)(2,1)S(1)} collective-permute-done((bf16[64,640]{1,0:T(8,128)(2,1)}, bf16[64,640]{1,0:T(8,128)(2,1)S(1)}, u32[]{:S(2)}, u32[]{:S(2)}) %collective-permute-start.1) | collective-permute-done | bytes 81952 | tf_op jit(solution)/shard_map/ppermute | solution.py:278
  28.2 2.1 %collective-permute-start.2 = (bf16[128,640]{1,0:T(8,128)(2,1)S(1)}, bf16[128,640]{1,0:T(8,128)(2,1)S(1)}, u32[]{:S(2)}, u32[]{:S(2)}) collective-permute-start(bf16[128,640]{1,0:T(8,128)(2,1)S(1)} %pad_maximum_fusion), channel_id=1, source_target_pairs={{0,16},{16,0},{32,48},{48,32},{64,80},{80,64},{96,112},{112,96},{1... | collective-permute-start | bytes 491528 | tf_op jit(solution)/shard_map/ppermute | solution.py:278
  30.4 4.2 %collective-permute-done.2 = bf16[128,640]{1,0:T(8,128)(2,1)S(1)} collective-permute-done((bf16[128,640]{1,0:T(8,128)(2,1)S(1)}, bf16[128,640]{1,0:T(8,128)(2,1)S(1)}, u32[]{:S(2)}, u32[]{:S(2)}) %collective-permute-start.2) | collective-permute-done | bytes 163872 | tf_op jit(solution)/shard_map/ppermute | solution.py:278
  34.6 1.0 maximum_dynamic-update-slice_fusion.keys_ref
  36.0 7.0 %collective-permute-start.3 = (bf16[8,64,2048]{2,1,0:T(8,128)(2,1)S(1)}, bf16[8,64,2048]{2,1,0:T(8,128)(2,1)}, u32[]{:S(2)}, u32[]{:S(2)}) collective-permute-start(bf16[8,64,2048]{2,1,0:T(8,128)(2,1)S(1)} %all-to-all-done.wk_own.wv_own), channel_id=1, source_target_pairs={{0,1},{1,0},{2,3},{3,2},{4,5},{5,4},{6,7},{7,6},{8,9},{9,8},{10,11... | collective-permute-start | bytes 6291464 | tf_op jit(solution)/shard_map/ppermute | solution.py:305
  44.3 2.5 %collective-permute-done.3.wk_oth.wv_oth = bf16[8,64,2048]{2,1,0:T(8,128)(2,1)} collective-permute-done((bf16[8,64,2048]{2,1,0:T(8,128)(2,1)S(1)}, bf16[8,64,2048]{2,1,0:T(8,128)(2,1)}, u32[]{:S(2)}, u32[]{:S(2)}) %collective-permute-start.3) | collective-permute-done | bytes 2097184 | tf_op jit(solution)/shard_map/ppermute | solution.py:305
  46.8 1.0 copy-done.3
  47.9 11.4 %attention.1 = (bf16[128,2048]{1,0:T(8,128)(2,1)}, bf16[128,2048]{1,0:T(8,128)(2,1)}, bf16[128,1024]{1,0:T(8,128)(2,1)}, bf16[8,32,640]{2,1,0:T(8,128)(2,1)}, bf16[8,16,640]{2,1,0:T(8,128)(2,1)}) custom-call(s32[4]{0:T(128)S(1)} %pad_add_fusion.facts_ref, bf16[128,2048]{1,0:T(8,128)(2,1)S(1)} %copy-done.2, bf16[128,1024]{1,0:T(8,128)(2,1)S(1)} %copy-done.4, ...), custom_call_target="tpu_custom_call" | custom-call | flops 6000000000 | bytes 8388608 | tf_op jit(solution)/shard_map/attention/pallas_call | solution.py:150
  59.3 13.6 %all_to_all.20.terms_ref = bf16[8,16,640]{2,1,0:T(8,128)(2,1)S(1)} all-to-all(bf16[8,16,640]{2,1,0:T(8,128)(2,1)} %get-tuple-element.27), channel_id=1, replica_groups=mesh['group'=4,'ctx'=8,'sample'=16] {'ctx'}, dimensions={0} | all-to-all | bytes 327680 | tf_op jit(solution)/shard_map/all_to_all | solution.py:308
  73.0 3.4 %all-to-all-start.2 = ((bf16[8,32,640]{2,1,0:T(8,128)(2,1)}), bf16[8,32,640]{2,1,0:T(8,128)(2,1)S(1)}, u32[]{:S(2)}, u32[]{:S(2)}) async-start(bf16[8,32,640]{2,1,0:T(8,128)(2,1)} %get-tuple-element.30), calls=%async_computation.2 | async-start | bytes 655360 | tf_op jit(solution)/shard_map/all_to_all | solution.py:310
  76.4 7.2 %collective-permute-start.4 = (bf16[16,640]{1,0:T(8,128)(2,1)S(1)}, bf16[16,640]{1,0:T(8,128)(2,1)S(1)}, u32[]{:S(2)}, u32[]{:S(2)}) collective-permute-start(bf16[16,640]{1,0:T(8,128)(2,1)S(1)} %get-tuple-element.29), channel_id=1, source_target_pairs={{0,64},{16,80},{32,96},{48,112},{64,0},{80,16},{96,32},{112,48},{1... | collective-permute-start | bytes 61448 | tf_op jit(solution)/shard_map/ppermute | solution.py:278
  83.6 4.5 %collective-permute-done.4 = bf16[16,640]{1,0:T(8,128)(2,1)S(1)} collective-permute-done((bf16[16,640]{1,0:T(8,128)(2,1)S(1)}, bf16[16,640]{1,0:T(8,128)(2,1)S(1)}, u32[]{:S(2)}, u32[]{:S(2)}) %collective-permute-start.4) | collective-permute-done | bytes 20512 | tf_op jit(solution)/shard_map/ppermute | solution.py:278
  88.1 1.1 add_prompt.1
  89.2 8.8 %all-to-all-start.3 = ((bf16[16,32,640]{2,1,0:T(8,128)(2,1)}), bf16[16,32,640]{2,1,0:T(8,128)(2,1)S(1)}, u32[]{:S(2)}, u32[]{:S(2)}) async-start(bf16[16,32,640]{2,1,0:T(8,128)(2,1)} %add_prompt.1), calls=%async_computation.3 | async-start | bytes 1310720 | tf_op jit(solution)/shard_map/all_to_all | solution.py:313
  98.0 1.9 %collective-permute-start.5 = (bf16[32,640]{1,0:T(8,128)(2,1)S(1)}, bf16[32,640]{1,0:T(8,128)(2,1)S(1)}, u32[]{:S(2)}, u32[]{:S(2)}) collective-permute-start(bf16[32,640]{1,0:T(8,128)(2,1)S(1)} %pad_maximum_fusion.5), channel_id=1, source_target_pairs={{0,32},{16,48},{32,0},{48,16},{64,96},{80,112},{96,64},{112,80},{1... | collective-permute-start | bytes 122888 | tf_op jit(solution)/shard_map/ppermute | solution.py:278
  99.9 5.0 %collective-permute-done.5 = bf16[32,640]{1,0:T(8,128)(2,1)S(1)} collective-permute-done((bf16[32,640]{1,0:T(8,128)(2,1)S(1)}, bf16[32,640]{1,0:T(8,128)(2,1)S(1)}, u32[]{:S(2)}, u32[]{:S(2)}) %collective-permute-start.5) | collective-permute-done | bytes 40992 | tf_op jit(solution)/shard_map/ppermute | solution.py:278
  105.0 1.9 %collective-permute-start.6 = (bf16[64,640]{1,0:T(8,128)(2,1)S(1)}, bf16[64,640]{1,0:T(8,128)(2,1)S(1)}, u32[]{:S(2)}, u32[]{:S(2)}) collective-permute-start(bf16[64,640]{1,0:T(8,128)(2,1)S(1)} %pad_maximum_fusion.3), channel_id=1, source_target_pairs={{0,16},{16,0},{32,48},{48,32},{64,80},{80,64},{96,112},{112,96},{1... | collective-permute-start | bytes 245768 | tf_op jit(solution)/shard_map/ppermute | solution.py:278
  106.9 3.3 %collective-permute-done.6 = bf16[64,640]{1,0:T(8,128)(2,1)S(1)} collective-permute-done((bf16[64,640]{1,0:T(8,128)(2,1)S(1)}, bf16[64,640]{1,0:T(8,128)(2,1)S(1)}, u32[]{:S(2)}, u32[]{:S(2)}) %collective-permute-start.6) | collective-permute-done | bytes 81952 | tf_op jit(solution)/shard_map/ppermute | solution.py:278
  110.2 1.4 %finish.1 = (f32[32,512]{1,0:T(8,128)}, f32[32,64]{1,0:T(8,128)}, f32[128,512]{1,0:T(8,128)}, f32[64,128]{1,0:T(8,128)}) custom-call(s32[4]{0:T(128)S(1)} %pad_add_fusion.facts_ref, bf16[16,32,640]{2,1,0:T(8,128)(2,1)S(1)} %all-to-all-done.3.prompt_ref, bf16[128,640]{1,0:T(8,128)(2,1)S(1)} %pad_maximum_fusion.1.resp_ref), custom_call_target="tpu_custom_call" | custom-call | tf_op jit(solution)/shard_map/finish/pallas_call | solution.py:260
  (30 shorter events, 3.9 us)
Async XLA Ops:
  0.6 0.9 copy-start
  1.5 0.9 copy-start.1
  3.9 6.9 %copy-start.5 = (bf16[32,512]{1,0:T(8,128)(2,1)S(1)}, bf16[32,512]{1,0:T(8,128)(2,1)}, u32[]{:S(2)}) copy-start(bf16[32,512]{1,0:T(8,128)(2,1)} %param.13) | copy-start | bytes 98308
  3.9 6.9 %copy-start.6 = (bf16[32,64]{1,0:T(8,128)(2,1)S(1)}, bf16[32,64]{1,0:T(8,128)(2,1)}, u32[]{:S(2)}) copy-start(bf16[32,64]{1,0:T(8,128)(2,1)} %param.14) | copy-start | bytes 12292
  4.0 21.0 %copy-start.7 = (bf16[128,64]{0,1:T(8,128)(2,1)S(1)}, bf16[128,64]{0,1:T(8,128)(2,1)}, u32[]{:S(2)}) copy-start(bf16[128,64]{0,1:T(8,128)(2,1)} %param.16) | copy-start | bytes 49156
  4.0 42.9 %copy-start.2 = (bf16[128,2048]{1,0:T(8,128)(2,1)S(1)}, bf16[128,2048]{1,0:T(8,128)(2,1)}, u32[]{:S(2)}) copy-start(bf16[128,2048]{1,0:T(8,128)(2,1)} %qn_ref.1) | copy-start | bytes 1572868
  4.0 42.9 %copy-start.4 = (bf16[128,1024]{1,0:T(8,128)(2,1)S(1)}, bf16[128,1024]{1,0:T(8,128)(2,1)}, u32[]{:S(2)}) copy-start(bf16[128,1024]{1,0:T(8,128)(2,1)} %qr_ref.1) | copy-start | bytes 786436
  4.0 32.0 %all-to-all-start = ((bf16[8,64,2048]{2,1,0:T(8,128)(2,1)}), bf16[8,64,2048]{2,1,0:T(8,128)(2,1)S(1)}, u32[]{:S(2)}, u32[]{:S(2)}) async-start(bf16[8,64,2048]{2,1,0:T(8,128)(2,1)} %spread_weights.1), calls=%async_computation | async-start | bytes 4194304 | tf_op jit(solution)/shard_map/all_to_all | solution.py:299
  10.9 8.9 %collective-permute-start = (bf16[32,640]{1,0:T(8,128)(2,1)S(1)}, bf16[32,640]{1,0:T(8,128)(2,1)S(1)}, u32[]{:S(2)}, u32[]{:S(2)}) collective-permute-start(bf16[32,640]{1,0:T(8,128)(2,1)S(1)} %get-tuple-element.37), channel_id=1, source_target_pairs={{0,64},{16,80},{32,96},{48,112},{64,0},{80,16},{96,32},{112,48},{1... | collective-permute-start | bytes 122888 | tf_op jit(solution)/shard_map/ppermute | solution.py:278
  20.5 7.7 %collective-permute-start.1 = (bf16[64,640]{1,0:T(8,128)(2,1)}, bf16[64,640]{1,0:T(8,128)(2,1)S(1)}, u32[]{:S(2)}, u32[]{:S(2)}) collective-permute-start(bf16[64,640]{1,0:T(8,128)(2,1)} %pad_maximum_fusion.2), channel_id=1, source_target_pairs={{0,32},{16,48},{32,0},{48,16},{64,96},{80,112},{96,64},{112,80},{1... | collective-permute-start | bytes 245768 | tf_op jit(solution)/shard_map/ppermute | solution.py:278
  28.2 6.3 %collective-permute-start.2 = (bf16[128,640]{1,0:T(8,128)(2,1)S(1)}, bf16[128,640]{1,0:T(8,128)(2,1)S(1)}, u32[]{:S(2)}, u32[]{:S(2)}) collective-permute-start(bf16[128,640]{1,0:T(8,128)(2,1)S(1)} %pad_maximum_fusion), channel_id=1, source_target_pairs={{0,16},{16,0},{32,48},{48,32},{64,80},{80,64},{96,112},{112,96},{1... | collective-permute-start | bytes 491528 | tf_op jit(solution)/shard_map/ppermute | solution.py:278
  36.0 10.9 %collective-permute-start.3 = (bf16[8,64,2048]{2,1,0:T(8,128)(2,1)S(1)}, bf16[8,64,2048]{2,1,0:T(8,128)(2,1)}, u32[]{:S(2)}, u32[]{:S(2)}) collective-permute-start(bf16[8,64,2048]{2,1,0:T(8,128)(2,1)S(1)} %all-to-all-done.wk_own.wv_own), channel_id=1, source_target_pairs={{0,1},{1,0},{2,3},{3,2},{4,5},{5,4},{6,7},{7,6},{8,9},{9,8},{10,11... | collective-permute-start | bytes 6291464 | tf_op jit(solution)/shard_map/ppermute | solution.py:305
  46.8 1.0 copy-start.3
  73.0 15.2 %all-to-all-start.2 = ((bf16[8,32,640]{2,1,0:T(8,128)(2,1)}), bf16[8,32,640]{2,1,0:T(8,128)(2,1)S(1)}, u32[]{:S(2)}, u32[]{:S(2)}) async-start(bf16[8,32,640]{2,1,0:T(8,128)(2,1)} %get-tuple-element.30), calls=%async_computation.2 | async-start | bytes 655360 | tf_op jit(solution)/shard_map/all_to_all | solution.py:310
  76.4 11.7 %collective-permute-start.4 = (bf16[16,640]{1,0:T(8,128)(2,1)S(1)}, bf16[16,640]{1,0:T(8,128)(2,1)S(1)}, u32[]{:S(2)}, u32[]{:S(2)}) collective-permute-start(bf16[16,640]{1,0:T(8,128)(2,1)S(1)} %get-tuple-element.29), channel_id=1, source_target_pairs={{0,64},{16,80},{32,96},{48,112},{64,0},{80,16},{96,32},{112,48},{1... | collective-permute-start | bytes 61448 | tf_op jit(solution)/shard_map/ppermute | solution.py:278
  89.2 21.0 %all-to-all-start.3 = ((bf16[16,32,640]{2,1,0:T(8,128)(2,1)}), bf16[16,32,640]{2,1,0:T(8,128)(2,1)S(1)}, u32[]{:S(2)}, u32[]{:S(2)}) async-start(bf16[16,32,640]{2,1,0:T(8,128)(2,1)} %add_prompt.1), calls=%async_computation.3 | async-start | bytes 1310720 | tf_op jit(solution)/shard_map/all_to_all | solution.py:313
  98.0 6.9 %collective-permute-start.5 = (bf16[32,640]{1,0:T(8,128)(2,1)S(1)}, bf16[32,640]{1,0:T(8,128)(2,1)S(1)}, u32[]{:S(2)}, u32[]{:S(2)}) collective-permute-start(bf16[32,640]{1,0:T(8,128)(2,1)S(1)} %pad_maximum_fusion.5), channel_id=1, source_target_pairs={{0,32},{16,48},{32,0},{48,16},{64,96},{80,112},{96,64},{112,80},{1... | collective-permute-start | bytes 122888 | tf_op jit(solution)/shard_map/ppermute | solution.py:278
  105.0 5.2 %collective-permute-start.6 = (bf16[64,640]{1,0:T(8,128)(2,1)S(1)}, bf16[64,640]{1,0:T(8,128)(2,1)S(1)}, u32[]{:S(2)}, u32[]{:S(2)}) collective-permute-start(bf16[64,640]{1,0:T(8,128)(2,1)S(1)} %pad_maximum_fusion.3), channel_id=1, source_target_pairs={{0,16},{16,0},{32,48},{48,32},{64,80},{80,64},{96,112},{112,96},{1... | collective-permute-start | bytes 245768 | tf_op jit(solution)/shard_map/ppermute | solution.py:278

commit v3 on v2

--- a/solution.py
+++ b/solution.py
@@ -18,34 +18,61 @@
 def spread_weights(w_key, w_value, copies):
     rows, cols = w_key.shape
 
-    def kernel(key_ref, value_ref, out_ref, sems):
-        moves = []
-        for j in range(copies):
-            moves.append(pltpu.make_async_copy(key_ref, out_ref.at[j, pl.ds(0, rows)], sems.at[2 * j]))
-            moves.append(pltpu.make_async_copy(value_ref, out_ref.at[j, pl.ds(rows, rows)], sems.at[2 * j + 1]))
+    def kernel(key_ref, value_ref, out_ref, held, sems):
+        moves = [
+            pltpu.make_async_copy(key_ref, held.at[pl.ds(0, rows)], sems.at[0]),
+            pltpu.make_async_copy(value_ref, held.at[pl.ds(rows, rows)], sems.at[1]),
+        ]
         for move in moves:
             move.start()
         for move in moves:
             move.wait()
+        moves = [pltpu.make_async_copy(held, out_ref.at[j], sems.at[j]) for j in range(copies)]
+        for move in moves:
+            move.start()
+        for move in moves:
+            move.wait()
 
     return pl.pallas_call(
         kernel,
         out_shape=pltpu.HBM((copies, 2 * rows, cols), BF),
-        in_specs=[pl.BlockSpec(memory_space=pltpu.VMEM)] * 2,
+        in_specs=[pl.BlockSpec(memory_space=pltpu.HBM)] * 2,
         out_specs=pl.BlockSpec(memory_space=pl.ANY),
-        scratch_shapes=[pltpu.SemaphoreType.DMA((2 * copies,))],
-        compiler_params=pltpu.CompilerParams(vmem_limit_bytes=2 * 2**20),
+        scratch_shapes=[pltpu.VMEM((2 * rows, cols), BF), pltpu.SemaphoreType.DMA((copies,))],
+        compiler_params=pltpu.CompilerParams(vmem_limit_bytes=58 * 2**20),
         name="spread_weights",
     )(w_key, w_value)
 
 
-def turn3(number):
-    low = lax.shift_left(jnp.bitwise_and(number, 1), 2)
-    return low + jnp.bitwise_and(number, 2) + lax.shift_right_logical(number, 2)
+def block_of(distance):
+    return 2 * jnp.bitwise_and(distance, 3) + lax.shift_right_logical(distance, 2)
 
 
 def dot(left, right, dims):
     return lax.dot_general(left, right, (dims, ((), ())), preferred_element_type=F32)
+
+
+def join_keys(pieces, resp_latent, resp_rope):
+    piece_rows = pieces[0].shape[0]
+    prompt_count = piece_rows * len(pieces)
+    key_count = prompt_count + resp_latent.shape[0]
+
+    def kernel(piece_0, piece_1, piece_2, piece_3, lat_ref, rot_ref, keys_ref):
+        for j, piece in enumerate((piece_0, piece_1, piece_2, piece_3)):
+            keys_ref[j * piece_rows:(j + 1) * piece_rows] = piece[...]
+        keys_ref[prompt_count:, :LAT] = lat_ref[...]
+        turned = rot_ref[...].astype(F32)
+        turned = jnp.concatenate([turned, turned], axis=0)
+        keys_ref[prompt_count:, LAT:] = jnp.swapaxes(turned, 0, 1).astype(BF)
+
+    return pl.pallas_call(
+        kernel,
+        in_specs=[pl.BlockSpec(memory_space=pltpu.VMEM)] * 6,
+        out_specs=pl.BlockSpec(memory_space=pltpu.VMEM),
+        out_shape=jax.ShapeDtypeStruct((key_count, WIDE), BF),
+        compiler_params=pltpu.CompilerParams(vmem_limit_bytes=4 * 2**20),
+        name="join_keys",
+    )(*pieces, resp_latent, resp_rope.T)
 
 
 def attention(facts, q_nope, q_rope, out_grad, keys, w_own, w_other):
@@ -59,12 +86,13 @@
     w_rows = two_rows // 2
     ctx_count = 8
     owned = prompt_count // ctx_count
-    resp_owned = row_count // ctx_count
+    resp_owned = row_count // 4
     scale = 1.0 / math.sqrt(192.0)
     exp_scale = scale * math.log2(math.e)
 
     def kernel(facts_ref, qn_ref, qr_ref, og_ref, keys_ref, wk_own, wv_own, wk_oth, wv_oth,
-               out_ref, gqn_ref, gqr_ref, prompt_ref, resp_ref, w_all, bias, live, acc, acc_rope):
+               out_ref, gqn_ref, gqr_ref, terms_ref,
+               w_all, bias, live, acc, acc_rope):
         step = pl.program_id(0)
         length, offset, ctx, core = facts_ref[0], facts_ref[1], facts_ref[2], facts_ref[3]
 
@@ -73,7 +101,8 @@
             key = lax.broadcasted_iota(jnp.int32, (key_count, row_count), 0)
             slot = lax.broadcasted_iota(jnp.int32, (key_count, row_count), 1)
             block = lax.shift_right_logical(key, 5)
-            place = jnp.bitwise_xor(turn3(block), ctx) * owned + jnp.bitwise_and(key, owned - 1)
+            distance = lax.shift_right_logical(block, 1) + 4 * jnp.bitwise_and(block, 1)
+            place = jnp.bitwise_xor(distance, ctx) * owned + jnp.bitwise_and(key, owned - 1)
             bias[...] = jnp.where(
                 key < prompt_count,
                 jnp.where(place < offset, 0.0, NEG_FILL),
@@ -139,12 +168,13 @@
         @pl.when(step == steps - 1)
         def _():
             for owner in range(ctx_count):
-                at = pl.ds(pl.multiple_of(turn3(jnp.bitwise_xor(ctx, owner)) * owned, owned), owned)
-                prompt_ref[owner, :, :LAT] = acc[at, :].astype(BF)
-                prompt_ref[owner, :, LAT:] = acc_rope[at, :].astype(BF)
-                at = slice(prompt_count + owner * resp_owned, prompt_count + (owner + 1) * resp_owned)
-                resp_ref[owner, :, :LAT] = acc[at, :].astype(BF)
-                resp_ref[owner, :, LAT:] = acc_rope[at, :].astype(BF)
+                at = pl.ds(pl.multiple_of(block_of(jnp.bitwise_xor(ctx, owner)) * owned, owned), owned)
+                terms_ref[owner, :owned, :LAT] = acc[at, :].astype(BF)
+                terms_ref[owner, :owned, LAT:] = acc_rope[at, :].astype(BF)
+                first = prompt_count + (owner % 4) * resp_owned
+                at = slice(first, first + resp_owned)
+                terms_ref[owner, owned:, :LAT] = acc[at, :].astype(BF)
+                terms_ref[owner, owned:, LAT:] = acc_rope[at, :].astype(BF)
 
     wide = 128 * hps
     return pl.pallas_call(
@@ -165,15 +195,13 @@
             pl.BlockSpec((row_count, wide), lambda i: (0, i)),
             pl.BlockSpec((row_count, wide), lambda i: (0, i)),
             pl.BlockSpec((row_count, wide // 2), lambda i: (0, i)),
-            pl.BlockSpec((ctx_count, owned, WIDE), lambda i: (0, 0, 0)),
-            pl.BlockSpec((ctx_count, resp_owned, WIDE), lambda i: (0, 0, 0)),
+            pl.BlockSpec((ctx_count, owned + resp_owned, WIDE), lambda i: (0, 0, 0)),
         ],
         out_shape=[
             jax.ShapeDtypeStruct(q_nope.shape, BF),
             jax.ShapeDtypeStruct(q_nope.shape, BF),
             jax.ShapeDtypeStruct(q_rope.shape, BF),
-            pltpu.HBM((ctx_count, owned, WIDE), BF),
-            pltpu.HBM((ctx_count, resp_owned, WIDE), BF),
+            pltpu.HBM((ctx_count, owned + resp_owned, WIDE), BF),
         ],
         scratch_shapes=[
             pltpu.VMEM((LAT, 256 * hps), BF),
@@ -188,78 +216,62 @@
     )(facts, q_nope, q_rope, out_grad, keys, w_own, w_own, w_other, w_other)
 
 
-def add_resp(terms, prompt_terms):
-    def kernel(terms_ref, through_ref, resp_ref, out_ref):
-        del through_ref, out_ref
-        total = terms_ref[0].astype(F32)
-        for j in range(1, terms.shape[0]):
-            total = total + terms_ref[j].astype(F32)
-        resp_ref[...] = total.astype(BF)
-
-    return pl.pallas_call(
-        kernel,
-        in_specs=[pl.BlockSpec(memory_space=pltpu.VMEM), pl.BlockSpec(memory_space=pl.ANY)],
-        out_specs=[pl.BlockSpec(memory_space=pltpu.VMEM), pl.BlockSpec(memory_space=pl.ANY)],
+def add_heads(terms, owned, copies):
+    resp_owned = terms.shape[1] - owned
+
+    def kernel(terms_ref, prompt_ref, resp_ref, held, sems):
+        def total(at):
+            result = terms_ref[0, at].astype(F32)
+            for j in range(1, terms.shape[0]):
+                result = result + terms_ref[j, at].astype(F32)
+            return result.astype(BF)
+
+        held[...] = total(slice(0, owned))
+        moves = [pltpu.make_async_copy(held, prompt_ref.at[j], sems.at[j]) for j in range(copies)]
+        for move in moves:
+            move.start()
+        resp_ref[...] = total(slice(owned, owned + resp_owned))
+        for move in moves:
+            move.wait()
+
+    return pl.pallas_call(
+        kernel,
+        in_specs=[pl.BlockSpec(memory_space=pltpu.VMEM)],
+        out_specs=[pl.BlockSpec(memory_space=pl.ANY), pl.BlockSpec(memory_space=pltpu.VMEM)],
         out_shape=[
-            jax.ShapeDtypeStruct(terms.shape[1:], BF),
-            pltpu.HBM(prompt_terms.shape, BF),
-        ],
-        input_output_aliases={1: 1},
-        compiler_params=pltpu.CompilerParams(vmem_limit_bytes=4 * 2**20),
-        name="add_resp",
-    )(terms, prompt_terms)
-
-
-def add_prompt(terms, copies):
-    owned = terms.shape[1]
-
-    def kernel(terms_ref, prompt_ref, held, sems):
-        total = terms_ref[0].astype(F32)
-        for j in range(1, terms.shape[0]):
-            total = total + terms_ref[j].astype(F32)
-        held[...] = total.astype(BF)
-        moves = [pltpu.make_async_copy(held, prompt_ref.at[j], sems.at[j]) for j in range(copies)]
-        for move in moves:
-            move.start()
-        for move in moves:
-            move.wait()
-
-    return pl.pallas_call(
-        kernel,
-        in_specs=[pl.BlockSpec(memory_space=pltpu.VMEM)],
-        out_specs=pl.BlockSpec(memory_space=pl.ANY),
-        out_shape=pltpu.HBM((copies, owned, WIDE), BF),
+            pltpu.HBM((copies, owned, WIDE), BF),
+            jax.ShapeDtypeStruct((resp_owned, WIDE), BF),
+        ],
         scratch_shapes=[pltpu.VMEM((owned, WIDE), BF), pltpu.SemaphoreType.DMA((copies,))],
         compiler_params=pltpu.CompilerParams(vmem_limit_bytes=4 * 2**20),
-        name="add_prompt",
+        name="add_heads",
     )(terms)
 
 
-def finish(facts, prompt_terms, resp_sum):
+def finish(facts, prompt_terms, resp_pieces):
     samples, owned, _ = prompt_terms.shape
-    row_count = resp_sum.shape[0]
-    resp_owned = row_count // 8
-
-    def kernel(facts_ref, prompt_ref, resp_ref, plat_ref, prot_ref, rlat_ref, rrot_ref, held):
+    piece_rows = resp_pieces[0].shape[0]
+    row_count = piece_rows * len(resp_pieces)
+    def kernel(facts_ref, prompt_ref, piece_0, piece_1, piece_2, piece_3, plat_ref, prot_ref, rlat_ref, rrot_ref, held):
         ctx = facts_ref[2]
         total = prompt_ref[0].astype(F32)
         for j in range(1, samples):
             total = total + prompt_ref[j].astype(F32)
         plat_ref[...] = total[:, :LAT]
         prot_ref[...] = total[:, LAT:LAT + 64] + total[:, LAT + 64:]
-        for owner in range(8):
-            at = pl.ds(pl.multiple_of(turn3(jnp.bitwise_xor(ctx, owner)) * resp_owned, resp_owned), resp_owned)
-            rows = resp_ref[at, :].astype(F32)
-            to = slice(owner * resp_owned, (owner + 1) * resp_owned)
-            rlat_ref[to, :] = rows[:, :LAT]
-            held[to, :] = rows[:, LAT:]
+        for distance, piece in enumerate((piece_0, piece_1, piece_2, piece_3)):
+            start = jnp.bitwise_xor(jnp.bitwise_and(ctx, 3), distance) * piece_rows
+            at = pl.ds(pl.multiple_of(start, piece_rows), piece_rows)
+            rows = piece[...].astype(F32)
+            rlat_ref[at, :] = rows[:, :LAT]
+            held[at, :] = rows[:, LAT:]
         turned = jnp.swapaxes(held[...], 0, 1)
         rrot_ref[...] = turned[:64] + turned[64:]
 
     vm = pl.BlockSpec(memory_space=pltpu.VMEM)
     return pl.pallas_call(
         kernel,
-        in_specs=[pl.BlockSpec(memory_space=pltpu.SMEM), vm, vm],
+        in_specs=[pl.BlockSpec(memory_space=pltpu.SMEM)] + [vm] * 5,
         out_specs=[vm] * 4,
         out_shape=[
             jax.ShapeDtypeStruct((owned, LAT), F32),
@@ -270,13 +282,19 @@
         scratch_shapes=[pltpu.VMEM((row_count, 128), F32)],
         compiler_params=pltpu.CompilerParams(vmem_limit_bytes=4 * 2**20),
         name="finish",
-    )(facts, prompt_terms, resp_sum)
-
-
-def butterfly(block, distances=(4, 2, 1)):
-    for k in distances:
-        block = jnp.concatenate([block, lax.ppermute(block, "ctx", [(i, i ^ k) for i in range(8)])], axis=0)
-    return block
+    )(facts, prompt_terms, *resp_pieces)
+
+
+def from_distance(block, distance):
+    return lax.ppermute(block, "ctx", [(i, i ^ distance) for i in range(8)])
+
+
+def meet(block):
+    return jnp.concatenate([block, from_distance(block, 4)], axis=0)
+
+
+def share(block):
+    return [block] + [from_distance(block, distance) for distance in (3, 2, 1)][::-1]
 
 
 def per_device(
@@ -298,20 +316,17 @@
     same_core = [[2 * chip + c for chip in range(8)] for c in range(2)]
     w_own = lax.all_to_all(
         spread_weights(w_key, w_value, 8), "sample", 0, 0, tiled=True, axis_index_groups=same_core)
-    prompt_keys = butterfly(jnp.concatenate([prompt_latent, prompt_rope, prompt_rope], axis=1))
-    keys = jnp.concatenate(
-        [prompt_keys, jnp.concatenate([resp_latent, resp_rope, resp_rope], axis=1)], axis=0)
+    prompt_pieces = share(meet(jnp.concatenate([prompt_latent, prompt_rope, prompt_rope], axis=1)))
+    keys = join_keys(prompt_pieces, resp_latent, resp_rope)
     w_own, keys = lax.optimization_barrier((w_own, keys))
     w_other = lax.ppermute(w_own, "sample", [(i, i ^ 1) for i in range(16)])
-    attn_out, grad_query_nope, grad_query_rope, prompt_terms, resp_terms = attention(
+    attn_out, grad_query_nope, grad_query_rope, terms = attention(
         facts, q_nope, q_rope, out_grad, keys, w_own, w_other)
-    resp_terms = lax.all_to_all(resp_terms, "ctx", 0, 0, tiled=True)
-    resp_part, prompt_terms = add_resp(resp_terms, prompt_terms)
-    prompt_terms = lax.all_to_all(prompt_terms, "ctx", 0, 0, tiled=True)
-    resp_half, prompt_terms = lax.optimization_barrier((butterfly(resp_part, (4,)), prompt_terms))
-    resp_sum = butterfly(resp_half, (2, 1))
-    prompt_part = lax.all_to_all(add_prompt(prompt_terms, 16), "sample", 0, 0, tiled=True)
-    prompt_lat, prompt_rot, resp_lat, resp_rot = finish(facts, prompt_part, resp_sum)
+    terms = lax.all_to_all(terms, "ctx", 0, 0, tiled=True)
+    prompt_part, resp_part = add_heads(terms, prompt_latent.shape[0], 16)
+    prompt_part = lax.all_to_all(prompt_part, "sample", 0, 0, tiled=True)
+    resp_pieces = share(resp_part)
+    prompt_lat, prompt_rot, resp_lat, resp_rot = finish(facts, prompt_part, resp_pieces)
     return (attn_out, grad_query_nope, grad_query_rope, prompt_lat, prompt_rot, resp_lat, resp_rot.T)
 
 

time: 113 us -> 102 us (0.903)
  blocking collectives: 13.6 us -> 26.3 us
  waiting for transfers between devices: 23.7 us -> 12.6 us
  starting transfers between devices: 51 us -> 42 us
  local copies, waits for them, and re-layouts: 3.65 us -> 1.08 us
  other arithmetic: 2.02 us -> 0.24 us
    ppermute x6 -> x7, waiting for transfers between devices: 20.9 us -> 7.57 us  [from_distance(): return lax.ppermute(block, 'ctx', [(i, i ^ distance) for i in range(8)])]
    all_to_all x1, blocking collectives: 13.6 us -> 26.3 us  [per_device(): terms = lax.all_to_all(terms, 'ctx', 0, 0, tiled=True)]
    all_to_all x2 -> x1, starting transfers between devices: 12.3 us -> 5.47 us  [per_device(): prompt_part = lax.all_to_all(prompt_part, 'sample', 0, 0, tiled=True)]
    ppermute x1, starting transfers between devices: 6.95 us -> 3.7 us  [per_device(): w_other = lax.ppermute(w_own, 'sample', [(i, i ^ 1) for i in range(16)])]
    unnamed x20 -> x14, local copies, waits for them, and re-layouts: 3.65 us -> 1.08 us
    all_to_all x1, waiting for transfers between devices: 0.33 us -> 2.24 us  [per_device(): lax.all_to_all(spread_weights(w_key, w_value, 8), 'sample', 0, 0, tiled=T...]
    concatenate x6 -> x1, other arithmetic: 1.86 us -> 0.08 us  [meet(): return jnp.concatenate([block, from_distance(block, 4)], axis=0)]
    ppermute x6 -> x7, starting transfers between devices: 25 us -> 26 us  [from_distance(): return lax.ppermute(block, 'ctx', [(i, i ^ distance) for i in range(8)])]
  transfers between devices with their start and end apart: 10 -> 10, of which waited for: 8 -> 7; matrix products, arithmetic and copies ran while one was open for 3% -> 0% of each run, Pallas kernels for 0% -> 0%
where the time goes in v3:
time: 102 us; the launch traced here: 101 us
  starting transfers between devices  42 us (41%)
  blocking collectives  26.3 us (26%)
  Pallas kernels  16.5 us (16%)
  waiting for transfers between devices  12.6 us (12%)
  between operations  2.11 us (2%)
  local copies, waits for them, and re-layouts  1.08 us (1%)
    all_to_all x1, blocking collectives, per_device(): terms = lax.all_to_all(terms, 'ctx', 0, 0, tiled=True)  26.3 us
    ppermute x7, starting transfers between devices, from_distance(): return lax.ppermute(block, 'ctx', [(i, i ^ distance) for i in range(8)])  26 us
    pallas_call x1, Pallas kernels, attention(): pl.pallas_call(kernel, grid=(steps,), in_specs=[pl.BlockSpec(memory_space...  11.6 us
    ppermute x7, waiting for transfers between devices, from_distance(): return lax.ppermute(block, 'ctx', [(i, i ^ distance) for i in range(8)])  7.57 us
    all_to_all x1, starting transfers between devices, per_device(): lax.all_to_all(spread_weights(w_key, w_value, 8), 'sample', 0, 0, tiled=T...  6.8 us
    all_to_all x1, starting transfers between devices, per_device(): prompt_part = lax.all_to_all(prompt_part, 'sample', 0, 0, tiled=True)  5.47 us
    ppermute x1, starting transfers between devices, per_device(): w_other = lax.ppermute(w_own, 'sample', [(i, i ^ 1) for i in range(16)])  3.7 us
    ppermute x1, waiting for transfers between devices, per_device(): w_other = lax.ppermute(w_own, 'sample', [(i, i ^ 1) for i in range(16)])  2.52 us
  transfers between devices with their start and end apart: 10, of which 7 were waited for; matrix products, arithmetic and copies ran while one was open for 0% of the time, Pallas kernels for 0%

profile of v3, /device:TPU:1, one launch (start us, length us, event | category | flops | bytes accessed | tf_op | source)
XLA Modules:
  0.0 100.8 jit_solution(9414012403099893665)
XLA Ops:
  0.6 2.4 %spread_weights.1 = bf16[8,64,2048]{2,1,0:T(8,128)(2,1)} custom-call(bf16[32,2048]{1,0:T(8,128)(2,1)} %key_ref.1, bf16[32,2048]{1,0:T(8,128)(2,1)} %value_ref.1), custom_call_target="tpu_custom_call" | custom-call | tf_op jit(solution)/shard_map/spread_weights/pallas_call | solution.py:36
  3.1 6.8 %all-to-all-start = ((bf16[8,64,2048]{2,1,0:T(8,128)(2,1)}), bf16[8,64,2048]{2,1,0:T(8,128)(2,1)S(1)}, u32[]{:S(2)}, u32[]{:S(2)}) async-start(bf16[8,64,2048]{2,1,0:T(8,128)(2,1)} %spread_weights.1), calls=%async_computation | async-start | bytes 4194304 | tf_op jit(solution)/shard_map/all_to_all | solution.py:317
  10.0 7.4 %collective-permute-start = (bf16[32,640]{1,0:T(8,128)(2,1)S(1)}, bf16[32,640]{1,0:T(8,128)(2,1)S(1)}, u32[]{:S(2)}, u32[]{:S(2)}) collective-permute-start(bf16[32,640]{1,0:T(8,128)(2,1)S(1)} %pad_maximum_fusion.1), channel_id=1, source_target_pairs={{0,64},{16,80},{32,96},{48,112},{64,0},{80,16},{96,32},{112,48},{1... | collective-permute-start | bytes 122888 | tf_op jit(solution)/shard_map/ppermute | solution.py:289
  17.4 1.4 %collective-permute-done = bf16[32,640]{1,0:T(8,128)(2,1)S(1)} collective-permute-done((bf16[32,640]{1,0:T(8,128)(2,1)S(1)}, bf16[32,640]{1,0:T(8,128)(2,1)S(1)}, u32[]{:S(2)}, u32[]{:S(2)}) %collective-permute-start) | collective-permute-done | bytes 40992 | tf_op jit(solution)/shard_map/ppermute | solution.py:289
  18.9 5.0 %collective-permute-start.3 = (bf16[64,640]{1,0:T(8,128)(2,1)S(1)}, bf16[64,640]{1,0:T(8,128)(2,1)S(1)}, u32[]{:S(2)}, u32[]{:S(2)}) collective-permute-start(bf16[64,640]{1,0:T(8,128)(2,1)S(1)} %pad_maximum_fusion.piece_0), channel_id=1, source_target_pairs={{0,48},{16,32},{32,16},{48,0},{64,112},{80,96},{96,80},{112,64},{1... | collective-permute-start | bytes 245768 | tf_op jit(solution)/shard_map/ppermute | solution.py:289
  23.9 1.9 %collective-permute-start.2 = (bf16[64,640]{1,0:T(8,128)(2,1)S(1)}, bf16[64,640]{1,0:T(8,128)(2,1)S(1)}, u32[]{:S(2)}, u32[]{:S(2)}) collective-permute-start(bf16[64,640]{1,0:T(8,128)(2,1)S(1)} %pad_maximum_fusion.piece_0), channel_id=1, source_target_pairs={{0,32},{16,48},{32,0},{48,16},{64,96},{80,112},{96,64},{112,80},{1... | collective-permute-start | bytes 245768 | tf_op jit(solution)/shard_map/ppermute | solution.py:289
  25.9 2.3 %collective-permute-start.1 = (bf16[64,640]{1,0:T(8,128)(2,1)S(1)}, bf16[64,640]{1,0:T(8,128)(2,1)S(1)}, u32[]{:S(2)}, u32[]{:S(2)}) collective-permute-start(bf16[64,640]{1,0:T(8,128)(2,1)S(1)} %pad_maximum_fusion.piece_0), channel_id=1, source_target_pairs={{0,16},{16,0},{32,48},{48,32},{64,80},{80,64},{96,112},{112,96},{1... | collective-permute-start | bytes 245768 | tf_op jit(solution)/shard_map/ppermute | solution.py:289
  28.2 3.3 %collective-permute-done.2.piece_2 = bf16[64,640]{1,0:T(8,128)(2,1)S(1)} collective-permute-done((bf16[64,640]{1,0:T(8,128)(2,1)S(1)}, bf16[64,640]{1,0:T(8,128)(2,1)S(1)}, u32[]{:S(2)}, u32[]{:S(2)}) %collective-permute-start.2) | collective-permute-done | bytes 81952 | tf_op jit(solution)/shard_map/ppermute | solution.py:289
  31.5 1.2 %collective-permute-done.1.piece_1 = bf16[64,640]{1,0:T(8,128)(2,1)S(1)} collective-permute-done((bf16[64,640]{1,0:T(8,128)(2,1)S(1)}, bf16[64,640]{1,0:T(8,128)(2,1)S(1)}, u32[]{:S(2)}, u32[]{:S(2)}) %collective-permute-start.1) | collective-permute-done | bytes 81952 | tf_op jit(solution)/shard_map/ppermute | solution.py:289
  32.7 0.1 join_keys.1.keys_ref
  32.8 2.2 %all-to-all-done.wk_own.wv_own = bf16[8,64,2048]{2,1,0:T(8,128)(2,1)S(1)} async-done(((bf16[8,64,2048]{2,1,0:T(8,128)(2,1)}), bf16[8,64,2048]{2,1,0:T(8,128)(2,1)S(1)}, u32[]{:S(2)}, u32[]{:S(2)}) %all-to-all-start) | async-done | bytes 2097184 | tf_op jit(solution)/shard_map/all_to_all | solution.py:317
  35.1 3.7 %collective-permute-start.4 = (bf16[8,64,2048]{2,1,0:T(8,128)(2,1)S(1)}, bf16[8,64,2048]{2,1,0:T(8,128)(2,1)}, u32[]{:S(2)}, u32[]{:S(2)}) collective-permute-start(bf16[8,64,2048]{2,1,0:T(8,128)(2,1)S(1)} %all-to-all-done.wk_own.wv_own), channel_id=1, source_target_pairs={{0,1},{1,0},{2,3},{3,2},{4,5},{5,4},{6,7},{7,6},{8,9},{9,8},{10,11... | collective-permute-start | bytes 6291464 | tf_op jit(solution)/shard_map/ppermute | solution.py:322
  40.2 2.5 %collective-permute-done.4.wk_oth.wv_oth = bf16[8,64,2048]{2,1,0:T(8,128)(2,1)} collective-permute-done((bf16[8,64,2048]{2,1,0:T(8,128)(2,1)S(1)}, bf16[8,64,2048]{2,1,0:T(8,128)(2,1)}, u32[]{:S(2)}, u32[]{:S(2)}) %collective-permute-start.4) | collective-permute-done | bytes 2097184 | tf_op jit(solution)/shard_map/ppermute | solution.py:322
  42.7 1.0 %copy-done.3 = bf16[128,2048]{1,0:T(8,128)(2,1)S(1)} copy-done((bf16[128,2048]{1,0:T(8,128)(2,1)S(1)}, bf16[128,2048]{1,0:T(8,128)(2,1)}, u32[]{:S(2)}) %copy-start.3) | copy-done | bytes 524312
  43.7 11.6 %attention.1 = (bf16[128,2048]{1,0:T(8,128)(2,1)}, bf16[128,2048]{1,0:T(8,128)(2,1)}, bf16[128,1024]{1,0:T(8,128)(2,1)}, bf16[8,64,640]{2,1,0:T(8,128)(2,1)}) custom-call(s32[4]{0:T(128)S(1)} %pad_add_fusion.facts_ref, bf16[128,2048]{1,0:T(8,128)(2,1)S(1)} %copy-done.2, bf16[128,1024]{1,0:T(8,128)(2,1)S(1)} %copy-done.4, bf16[128,2048]{1,0:T(8,128)(2,1)S(1)} %copy-done.3, ...), custom_call_target="tpu_custom_call" | custom-call | flops 6000000000 | bytes 8388608 | tf_op jit(solution)/shard_map/attention/pallas_call | solution.py:180
  55.3 26.3 %all_to_all.15.terms_ref = bf16[8,64,640]{2,1,0:T(8,128)(2,1)S(1)} all-to-all(bf16[8,64,640]{2,1,0:T(8,128)(2,1)} %get-tuple-element.24), channel_id=1, replica_groups=mesh['group'=4,'ctx'=8,'sample'=16] {'ctx'}, dimensions={0} | all-to-all | bytes 1310720 | tf_op jit(solution)/shard_map/all_to_all | solution.py:325
  81.6 1.0 %add_heads.1 = (bf16[16,32,640]{2,1,0:T(8,128)(2,1)}, bf16[32,640]{1,0:T(8,128)(2,1)S(1)}) custom-call(bf16[8,64,640]{2,1,0:T(8,128)(2,1)S(1)} %all_to_all.15.terms_ref), custom_call_target="tpu_custom_call" | custom-call | tf_op jit(solution)/shard_map/add_heads/pallas_call | solution.py:237
  82.7 5.5 %all-to-all-start.2 = ((bf16[16,32,640]{2,1,0:T(8,128)(2,1)}), bf16[16,32,640]{2,1,0:T(8,128)(2,1)S(1)}, u32[]{:S(2)}, u32[]{:S(2)}) async-start(bf16[16,32,640]{2,1,0:T(8,128)(2,1)} %get-tuple-element.25), calls=%async_computation.2 | async-start | bytes 1310720 | tf_op jit(solution)/shard_map/all_to_all | solution.py:327
  88.1 2.0 %collective-permute-start.7 = (bf16[32,640]{1,0:T(8,128)(2,1)S(1)}, bf16[32,640]{1,0:T(8,128)(2,1)S(1)}, u32[]{:S(2)}, u32[]{:S(2)}) collective-permute-start(bf16[32,640]{1,0:T(8,128)(2,1)S(1)} %get-tuple-element.26.piece_0), channel_id=1, source_target_pairs={{0,48},{16,32},{32,16},{48,0},{64,112},{80,96},{96,80},{112,64},{1... | collective-permute-start | bytes 122888 | tf_op jit(solution)/shard_map/ppermute | solution.py:289
  90.2 3.3 %collective-permute-start.6 = (bf16[32,640]{1,0:T(8,128)(2,1)S(1)}, bf16[32,640]{1,0:T(8,128)(2,1)S(1)}, u32[]{:S(2)}, u32[]{:S(2)}) collective-permute-start(bf16[32,640]{1,0:T(8,128)(2,1)S(1)} %get-tuple-element.26.piece_0), channel_id=1, source_target_pairs={{0,32},{16,48},{32,0},{48,16},{64,96},{80,112},{96,64},{112,80},{1... | collective-permute-start | bytes 122888 | tf_op jit(solution)/shard_map/ppermute | solution.py:289
  93.5 4.0 %collective-permute-start.5 = (bf16[32,640]{1,0:T(8,128)(2,1)S(1)}, bf16[32,640]{1,0:T(8,128)(2,1)S(1)}, u32[]{:S(2)}, u32[]{:S(2)}) collective-permute-start(bf16[32,640]{1,0:T(8,128)(2,1)S(1)} %get-tuple-element.26.piece_0), channel_id=1, source_target_pairs={{0,16},{16,0},{32,48},{48,32},{64,80},{80,64},{96,112},{112,96},{1... | collective-permute-start | bytes 122888 | tf_op jit(solution)/shard_map/ppermute | solution.py:289
  97.5 1.6 %collective-permute-done.5.piece_1 = bf16[32,640]{1,0:T(8,128)(2,1)S(1)} collective-permute-done((bf16[32,640]{1,0:T(8,128)(2,1)S(1)}, bf16[32,640]{1,0:T(8,128)(2,1)S(1)}, u32[]{:S(2)}, u32[]{:S(2)}) %collective-permute-start.5) | collective-permute-done | bytes 40992 | tf_op jit(solution)/shard_map/ppermute | solution.py:289
  99.1 0.3 all-to-all-done.2.prompt_ref
  99.4 1.4 %finish.1 = (f32[32,512]{1,0:T(8,128)}, f32[32,64]{1,0:T(8,128)}, f32[128,512]{1,0:T(8,128)}, f32[64,128]{1,0:T(8,128)}) custom-call(s32[4]{0:T(128)S(1)} %pad_add_fusion.facts_ref, bf16[16,32,640]{2,1,0:T(8,128)(2,1)S(1)} %all-to-all-done.2.prompt_ref, bf16[32,640]{1,0:T(8,128)(2,1)S(1)} %get-tuple-element.26.piece_0, ...), custom_call_target="tpu_custom_call" | custom-call | tf_op jit(solution)/shard_map/finish/pallas_call | solution.py:272
  (19 shorter events, 0.3 us)
Async XLA Ops:
  3.0 6.9 %copy-start.5 = (bf16[32,512]{1,0:T(8,128)(2,1)S(1)}, bf16[32,512]{1,0:T(8,128)(2,1)}, u32[]{:S(2)}) copy-start(bf16[32,512]{1,0:T(8,128)(2,1)} %param.13) | copy-start | bytes 98308
  3.0 6.9 %copy-start.6 = (bf16[32,64]{1,0:T(8,128)(2,1)S(1)}, bf16[32,64]{1,0:T(8,128)(2,1)}, u32[]{:S(2)}) copy-start(bf16[32,64]{1,0:T(8,128)(2,1)} %param.14) | copy-start | bytes 12292
  3.0 29.7 %copy-start = (bf16[128,512]{1,0:T(8,128)(2,1)S(1)}, bf16[128,512]{1,0:T(8,128)(2,1)}, u32[]{:S(2)}) copy-start(bf16[128,512]{1,0:T(8,128)(2,1)} %lat_ref.1) | copy-start | bytes 393220
  3.0 29.7 %copy-start.1 = (bf16[128,64]{0,1:T(8,128)(2,1)S(1)}, bf16[128,64]{0,1:T(8,128)(2,1)}, u32[]{:S(2)}) copy-start(bf16[128,64]{0,1:T(8,128)(2,1)} %param.16) | copy-start | bytes 49156
  3.1 39.6 %copy-start.2 = (bf16[128,2048]{1,0:T(8,128)(2,1)S(1)}, bf16[128,2048]{1,0:T(8,128)(2,1)}, u32[]{:S(2)}) copy-start(bf16[128,2048]{1,0:T(8,128)(2,1)} %qn_ref.1) | copy-start | bytes 1572868
  3.1 39.6 %copy-start.4 = (bf16[128,1024]{1,0:T(8,128)(2,1)S(1)}, bf16[128,1024]{1,0:T(8,128)(2,1)}, u32[]{:S(2)}) copy-start(bf16[128,1024]{1,0:T(8,128)(2,1)} %qr_ref.1) | copy-start | bytes 786436
  3.1 32.0 %all-to-all-start = ((bf16[8,64,2048]{2,1,0:T(8,128)(2,1)}), bf16[8,64,2048]{2,1,0:T(8,128)(2,1)S(1)}, u32[]{:S(2)}, u32[]{:S(2)}) async-start(bf16[8,64,2048]{2,1,0:T(8,128)(2,1)} %spread_weights.1), calls=%async_computation | async-start | bytes 4194304 | tf_op jit(solution)/shard_map/all_to_all | solution.py:317
  10.0 8.9 %collective-permute-start = (bf16[32,640]{1,0:T(8,128)(2,1)S(1)}, bf16[32,640]{1,0:T(8,128)(2,1)S(1)}, u32[]{:S(2)}, u32[]{:S(2)}) collective-permute-start(bf16[32,640]{1,0:T(8,128)(2,1)S(1)} %pad_maximum_fusion.1), channel_id=1, source_target_pairs={{0,64},{16,80},{32,96},{48,112},{64,0},{80,16},{96,32},{112,48},{1... | collective-permute-start | bytes 122888 | tf_op jit(solution)/shard_map/ppermute | solution.py:289
  18.9 9.3 %collective-permute-start.3 = (bf16[64,640]{1,0:T(8,128)(2,1)S(1)}, bf16[64,640]{1,0:T(8,128)(2,1)S(1)}, u32[]{:S(2)}, u32[]{:S(2)}) collective-permute-start(bf16[64,640]{1,0:T(8,128)(2,1)S(1)} %pad_maximum_fusion.piece_0), channel_id=1, source_target_pairs={{0,48},{16,32},{32,16},{48,0},{64,112},{80,96},{96,80},{112,64},{1... | collective-permute-start | bytes 245768 | tf_op jit(solution)/shard_map/ppermute | solution.py:289
  23.9 7.6 %collective-permute-start.2 = (bf16[64,640]{1,0:T(8,128)(2,1)S(1)}, bf16[64,640]{1,0:T(8,128)(2,1)S(1)}, u32[]{:S(2)}, u32[]{:S(2)}) collective-permute-start(bf16[64,640]{1,0:T(8,128)(2,1)S(1)} %pad_maximum_fusion.piece_0), channel_id=1, source_target_pairs={{0,32},{16,48},{32,0},{48,16},{64,96},{80,112},{96,64},{112,80},{1... | collective-permute-start | bytes 245768 | tf_op jit(solution)/shard_map/ppermute | solution.py:289
  25.9 6.9 %collective-permute-start.1 = (bf16[64,640]{1,0:T(8,128)(2,1)S(1)}, bf16[64,640]{1,0:T(8,128)(2,1)S(1)}, u32[]{:S(2)}, u32[]{:S(2)}) collective-permute-start(bf16[64,640]{1,0:T(8,128)(2,1)S(1)} %pad_maximum_fusion.piece_0), channel_id=1, source_target_pairs={{0,16},{16,0},{32,48},{48,32},{64,80},{80,64},{96,112},{112,96},{1... | collective-permute-start | bytes 245768 | tf_op jit(solution)/shard_map/ppermute | solution.py:289
  35.1 7.6 %collective-permute-start.4 = (bf16[8,64,2048]{2,1,0:T(8,128)(2,1)S(1)}, bf16[8,64,2048]{2,1,0:T(8,128)(2,1)}, u32[]{:S(2)}, u32[]{:S(2)}) collective-permute-start(bf16[8,64,2048]{2,1,0:T(8,128)(2,1)S(1)} %all-to-all-done.wk_own.wv_own), channel_id=1, source_target_pairs={{0,1},{1,0},{2,3},{3,2},{4,5},{5,4},{6,7},{7,6},{8,9},{9,8},{10,11... | collective-permute-start | bytes 6291464 | tf_op jit(solution)/shard_map/ppermute | solution.py:322
  42.7 1.0 %copy-start.3 = (bf16[128,2048]{1,0:T(8,128)(2,1)S(1)}, bf16[128,2048]{1,0:T(8,128)(2,1)}, u32[]{:S(2)}) copy-start(bf16[128,2048]{1,0:T(8,128)(2,1)} %og_ref.1) | copy-start | bytes 1572868
  82.7 16.7 %all-to-all-start.2 = ((bf16[16,32,640]{2,1,0:T(8,128)(2,1)}), bf16[16,32,640]{2,1,0:T(8,128)(2,1)S(1)}, u32[]{:S(2)}, u32[]{:S(2)}) async-start(bf16[16,32,640]{2,1,0:T(8,128)(2,1)} %get-tuple-element.25), calls=%async_computation.2 | async-start | bytes 1310720 | tf_op jit(solution)/shard_map/all_to_all | solution.py:327
  88.1 9.3 %collective-permute-start.7 = (bf16[32,640]{1,0:T(8,128)(2,1)S(1)}, bf16[32,640]{1,0:T(8,128)(2,1)S(1)}, u32[]{:S(2)}, u32[]{:S(2)}) collective-permute-start(bf16[32,640]{1,0:T(8,128)(2,1)S(1)} %get-tuple-element.26.piece_0), channel_id=1, source_target_pairs={{0,48},{16,32},{32,16},{48,0},{64,112},{80,96},{96,80},{112,64},{1... | collective-permute-start | bytes 122888 | tf_op jit(solution)/shard_map/ppermute | solution.py:289
  90.2 7.3 %collective-permute-start.6 = (bf16[32,640]{1,0:T(8,128)(2,1)S(1)}, bf16[32,640]{1,0:T(8,128)(2,1)S(1)}, u32[]{:S(2)}, u32[]{:S(2)}) collective-permute-start(bf16[32,640]{1,0:T(8,128)(2,1)S(1)} %get-tuple-element.26.piece_0), channel_id=1, source_target_pairs={{0,32},{16,48},{32,0},{48,16},{64,96},{80,112},{96,64},{112,80},{1... | collective-permute-start | bytes 122888 | tf_op jit(solution)/shard_map/ppermute | solution.py:289
  93.5 5.7 %collective-permute-start.5 = (bf16[32,640]{1,0:T(8,128)(2,1)S(1)}, bf16[32,640]{1,0:T(8,128)(2,1)S(1)}, u32[]{:S(2)}, u32[]{:S(2)}) collective-permute-start(bf16[32,640]{1,0:T(8,128)(2,1)S(1)} %get-tuple-element.26.piece_0), channel_id=1, source_target_pairs={{0,16},{16,0},{32,48},{48,32},{64,80},{80,64},{96,112},{112,96},{1... | collective-permute-start | bytes 122888 | tf_op jit(solution)/shard_map/ppermute | solution.py:289

commit v4 on v3

--- a/solution.py
+++ b/solution.py
@@ -75,7 +75,7 @@
     )(*pieces, resp_latent, resp_rope.T)
 
 
-def attention(facts, q_nope, q_rope, out_grad, keys, w_own, w_other):
+def attention(for_keys, facts, q_nope, q_rope, out_grad, keys, w_own, w_other):
     row_count = q_nope.shape[0]
     key_count = keys.shape[0]
     prompt_count = key_count - row_count
@@ -90,9 +90,11 @@
     scale = 1.0 / math.sqrt(192.0)
     exp_scale = scale * math.log2(math.e)
 
-    def kernel(facts_ref, qn_ref, qr_ref, og_ref, keys_ref, wk_own, wv_own, wk_oth, wv_oth,
-               out_ref, gqn_ref, gqr_ref, terms_ref,
-               w_all, bias, live, acc, acc_rope):
+    def kernel(facts_ref, qn_ref, qr_ref, og_ref, keys_ref, wk_own, wv_own, wk_oth, wv_oth, *refs):
+        if for_keys:
+            terms_ref, w_all, bias, live, acc, acc_rope = refs
+        else:
+            out_ref, gqn_ref, gqr_ref, w_all, bias, live = refs
         step = pl.program_id(0)
         length, offset, ctx, core = facts_ref[0], facts_ref[1], facts_ref[2], facts_ref[3]
 
@@ -109,8 +111,9 @@
                 jnp.where(key - prompt_count <= slot, 0.0, NEG_FILL))
             row = lax.broadcasted_iota(jnp.int32, (row_count, 128), 0)
             live[...] = jnp.where(row < length, 1.0, 0.0)
-            acc[...] = jnp.zeros_like(acc)
-            acc_rope[...] = jnp.zeros_like(acc_rope)
+            if for_keys:
+                acc[...] = jnp.zeros_like(acc)
+                acc_rope[...] = jnp.zeros_like(acc_rope)
 
         for j in range(chips):
             own_at = pl.ds(pl.multiple_of(j * 2 * w_rows + core * w_rows, w_rows), w_rows)
@@ -148,18 +151,21 @@
             weighed = prob * grad_prob[h]
             inner = jnp.sum(weighed, axis=0, keepdims=True)
             grad_score.append(((weighed - prob * inner) * scale).astype(BF))
-        attn = [dot(prob_half[h], value[h], ((0,), (0,))) for h in heads]
-        grad_query = [dot(grad_score[h], key_full[h], ((0,), (0,))) for h in heads]
+        if not for_keys:
+            attn = [dot(prob_half[h], value[h], ((0,), (0,))) for h in heads]
+            grad_query = [dot(grad_score[h], key_full[h], ((0,), (0,))) for h in heads]
+            for h in heads:
+                out_ref[:, cols[h]] = (attn[h] * alive).astype(BF)
+                gqn_ref[:, cols[h]] = grad_query[h][:, :128].astype(BF)
+                if h % 2 == 1:
+                    gqr_ref[:, cols[h // 2]] = jnp.where(
+                        lane < 64, grad_query[h - 1][:, 128:], grad_query[h][:, 128:]).astype(BF)
+            return
         grad_key = [dot(grad_score[h], query[h], ((1,), (0,))) for h in heads]
         grad_value = [dot(prob_half[h], grad_out[h], ((1,), (0,))) for h in heads]
         grads = []
         rope_sum = None
         for h in heads:
-            out_ref[:, cols[h]] = (attn[h] * alive).astype(BF)
-            gqn_ref[:, cols[h]] = grad_query[h][:, :128].astype(BF)
-            if h % 2 == 1:
-                gqr_ref[:, cols[h // 2]] = jnp.where(
-                    lane < 64, grad_query[h - 1][:, 128:], grad_query[h][:, 128:]).astype(BF)
             grads += [grad_key[h][:, :128].astype(BF), grad_value[h].astype(BF)]
             rope_sum = grad_key[h][:, 128:] if rope_sum is None else rope_sum + grad_key[h][:, 128:]
         acc[...] += dot(jnp.concatenate(grads, axis=1), w_all[...], ((1,), (1,)))
@@ -167,14 +173,16 @@
 
         @pl.when(step == steps - 1)
         def _():
+            rope = acc_rope[...]
+            acc_rope[...] = rope + pltpu.roll(rope, 64, 1)
+            low = lax.broadcasted_iota(jnp.int32, (owned, 128), 1) < 64
             for owner in range(ctx_count):
                 at = pl.ds(pl.multiple_of(block_of(jnp.bitwise_xor(ctx, owner)) * owned, owned), owned)
-                terms_ref[owner, :owned, :LAT] = acc[at, :].astype(BF)
-                terms_ref[owner, :owned, LAT:] = acc_rope[at, :].astype(BF)
                 first = prompt_count + (owner % 4) * resp_owned
-                at = slice(first, first + resp_owned)
-                terms_ref[owner, owned:, :LAT] = acc[at, :].astype(BF)
-                terms_ref[owner, owned:, LAT:] = acc_rope[at, :].astype(BF)
+                resp_at = slice(first, first + resp_owned)
+                terms_ref[owner, :, :LAT] = acc[at, :].astype(BF)
+                terms_ref[owner, :, LAT:2 * LAT] = acc[resp_at, :].astype(BF)
+                terms_ref[owner, :, 2 * LAT:] = jnp.where(low, acc_rope[at, :], acc_rope[resp_at, :]).astype(BF)
 
     wide = 128 * hps
     return pl.pallas_call(
@@ -191,46 +199,45 @@
             pl.BlockSpec((chips, w_rows, wide), lambda i: (0, 0, i)),
             pl.BlockSpec((chips, w_rows, wide), lambda i: (0, 1, i)),
         ],
-        out_specs=[
+        out_specs=pl.BlockSpec((ctx_count, owned, 2 * LAT + 128), lambda i: (0, 0, 0)) if for_keys else [
             pl.BlockSpec((row_count, wide), lambda i: (0, i)),
             pl.BlockSpec((row_count, wide), lambda i: (0, i)),
             pl.BlockSpec((row_count, wide // 2), lambda i: (0, i)),
-            pl.BlockSpec((ctx_count, owned + resp_owned, WIDE), lambda i: (0, 0, 0)),
-        ],
-        out_shape=[
+        ],
+        out_shape=pltpu.HBM((ctx_count, owned, 2 * LAT + 128), BF) if for_keys else [
             jax.ShapeDtypeStruct(q_nope.shape, BF),
             jax.ShapeDtypeStruct(q_nope.shape, BF),
             jax.ShapeDtypeStruct(q_rope.shape, BF),
-            pltpu.HBM((ctx_count, owned + resp_owned, WIDE), BF),
         ],
         scratch_shapes=[
             pltpu.VMEM((LAT, 256 * hps), BF),
             pltpu.VMEM((key_count, row_count), F32),
             pltpu.VMEM((row_count, 128), F32),
-            pltpu.VMEM((key_count, LAT), F32),
-            pltpu.VMEM((key_count, 128), F32),
-        ],
-        compiler_params=pltpu.CompilerParams(vmem_limit_bytes=28 * 2**20),
+        ] + ([pltpu.VMEM((key_count, LAT), F32), pltpu.VMEM((key_count, 128), F32)] if for_keys else []),
+        compiler_params=pltpu.CompilerParams(vmem_limit_bytes=(58 if for_keys else 28) * 2**20),
         cost_estimate=pl.CostEstimate(flops=6 * 10**9, bytes_accessed=8 * 2**20, transcendentals=2048 * 384),
-        name="attention",
+        name="key_terms" if for_keys else "attention",
     )(facts, q_nope, q_rope, out_grad, keys, w_own, w_own, w_other, w_other)
 
 
-def add_heads(terms, owned, copies):
-    resp_owned = terms.shape[1] - owned
+def add_heads(terms, copies):
+    owned = terms.shape[1]
 
     def kernel(terms_ref, prompt_ref, resp_ref, held, sems):
         def total(at):
-            result = terms_ref[0, at].astype(F32)
+            result = terms_ref[0, :, at].astype(F32)
             for j in range(1, terms.shape[0]):
-                result = result + terms_ref[j, at].astype(F32)
+                result = result + terms_ref[j, :, at].astype(F32)
             return result.astype(BF)
 
-        held[...] = total(slice(0, owned))
+        rope = total(slice(2 * LAT, 2 * LAT + 128))
+        held[:, :LAT] = total(slice(0, LAT))
+        held[:, LAT:] = rope
         moves = [pltpu.make_async_copy(held, prompt_ref.at[j], sems.at[j]) for j in range(copies)]
         for move in moves:
             move.start()
-        resp_ref[...] = total(slice(owned, owned + resp_owned))
+        resp_ref[:, :LAT] = total(slice(LAT, 2 * LAT))
+        resp_ref[:, LAT:] = rope
         for move in moves:
             move.wait()
 
@@ -240,7 +247,7 @@
         out_specs=[pl.BlockSpec(memory_space=pl.ANY), pl.BlockSpec(memory_space=pltpu.VMEM)],
         out_shape=[
             pltpu.HBM((copies, owned, WIDE), BF),
-            jax.ShapeDtypeStruct((resp_owned, WIDE), BF),
+            jax.ShapeDtypeStruct((owned, WIDE), BF),
         ],
         scratch_shapes=[pltpu.VMEM((owned, WIDE), BF), pltpu.SemaphoreType.DMA((copies,))],
         compiler_params=pltpu.CompilerParams(vmem_limit_bytes=4 * 2**20),
@@ -258,7 +265,7 @@
         for j in range(1, samples):
             total = total + prompt_ref[j].astype(F32)
         plat_ref[...] = total[:, :LAT]
-        prot_ref[...] = total[:, LAT:LAT + 64] + total[:, LAT + 64:]
+        prot_ref[...] = total[:, LAT:LAT + 64]
         for distance, piece in enumerate((piece_0, piece_1, piece_2, piece_3)):
             start = jnp.bitwise_xor(jnp.bitwise_and(ctx, 3), distance) * piece_rows
             at = pl.ds(pl.multiple_of(start, piece_rows), piece_rows)
@@ -266,7 +273,7 @@
             rlat_ref[at, :] = rows[:, :LAT]
             held[at, :] = rows[:, LAT:]
         turned = jnp.swapaxes(held[...], 0, 1)
-        rrot_ref[...] = turned[:64] + turned[64:]
+        rrot_ref[...] = turned[64:]
 
     vm = pl.BlockSpec(memory_space=pltpu.VMEM)
     return pl.pallas_call(
@@ -320,10 +327,12 @@
     keys = join_keys(prompt_pieces, resp_latent, resp_rope)
     w_own, keys = lax.optimization_barrier((w_own, keys))
     w_other = lax.ppermute(w_own, "sample", [(i, i ^ 1) for i in range(16)])
-    attn_out, grad_query_nope, grad_query_rope, terms = attention(
-        facts, q_nope, q_rope, out_grad, keys, w_own, w_other)
-    terms = lax.all_to_all(terms, "ctx", 0, 0, tiled=True)
-    prompt_part, resp_part = add_heads(terms, prompt_latent.shape[0], 16)
+    held = (q_nope, q_rope, out_grad, keys, w_own, w_other)
+    terms, later_facts = lax.optimization_barrier((attention(True, facts, *held), facts))
+    attn_out, grad_query_nope, grad_query_rope = attention(False, later_facts, *held)
+    terms, attn_out, grad_query_nope, grad_query_rope = lax.optimization_barrier(
+        (lax.all_to_all(terms, "ctx", 0, 0, tiled=True), attn_out, grad_query_nope, grad_query_rope))
+    prompt_part, resp_part = add_heads(terms, 16)
     prompt_part = lax.all_to_all(prompt_part, "sample", 0, 0, tiled=True)
     resp_pieces = share(resp_part)
     prompt_lat, prompt_rot, resp_lat, resp_rot = finish(facts, prompt_part, resp_pieces)

time: 102 us -> 98.8 us (0.969)
  blocking collectives: 26.3 us -> 0 us
  Pallas kernels: 16.5 us -> 23.6 us
  starting transfers between devices: 42 us -> 48.4 us
  waiting for transfers between devices: 12.6 us -> 18.6 us
  local copies, waits for them, and re-layouts: 1.08 us -> 4.48 us
    all_to_all x1 -> x0, blocking collectives: 26.3 us -> none  [per_device(): terms = lax.all_to_all(terms, 'ctx', 0, 0, tiled=True)]
    all_to_all x0 -> x1, waiting for transfers between devices: none -> 7.44 us  [per_device(): lax.all_to_all(terms, 'ctx', 0, 0, tiled=True)]
    pallas_call x1 -> x2, Pallas kernels: 11.6 us -> 18.7 us  [attention(): pl.pallas_call(kernel, grid=(steps,), in_specs=[pl.BlockSpec(memory_space...]
    all_to_all x0 -> x1, starting transfers between devices: none -> 5.86 us  [per_device(): lax.all_to_all(terms, 'ctx', 0, 0, tiled=True)]
    unnamed x14 -> x24, local copies, waits for them, and re-layouts: 1.08 us -> 4.48 us
    all_to_all x1, waiting for transfers between devices: 2.24 us -> 0.26 us  [per_device(): lax.all_to_all(spread_weights(w_key, w_value, 8), 'sample', 0, 0, tiled=T...]
  transfers between devices with their start and end apart: 10 -> 11, of which waited for: 7 -> 8; matrix products, arithmetic and copies ran while one was open for 0% -> 1% of each run, Pallas kernels for 0% -> 8%
where the time goes in v4:
time: 98.8 us; the launch traced here: 98 us
  starting transfers between devices  48.4 us (49%)
  Pallas kernels  23.6 us (24%)
  waiting for transfers between devices  18.6 us (19%)
  local copies, waits for them, and re-layouts  4.48 us (5%)
  between operations  2.13 us (2%)
    ppermute x7, starting transfers between devices, from_distance(): return lax.ppermute(block, 'ctx', [(i, i ^ distance) for i in range(8)])  26.2 us
    pallas_call x2, Pallas kernels, attention(): pl.pallas_call(kernel, grid=(steps,), in_specs=[pl.BlockSpec(memory_space...  18.7 us
    ppermute x7, waiting for transfers between devices, from_distance(): return lax.ppermute(block, 'ctx', [(i, i ^ distance) for i in range(8)])  8.35 us
    all_to_all x1, waiting for transfers between devices, per_device(): lax.all_to_all(terms, 'ctx', 0, 0, tiled=True)  7.44 us
    all_to_all x1, starting transfers between devices, per_device(): lax.all_to_all(spread_weights(w_key, w_value, 8), 'sample', 0, 0, tiled=T...  6.8 us
    all_to_all x1, starting transfers between devices, per_device(): lax.all_to_all(terms, 'ctx', 0, 0, tiled=True)  5.86 us
    all_to_all x1, starting transfers between devices, per_device(): prompt_part = lax.all_to_all(prompt_part, 'sample', 0, 0, tiled=True)  4.9 us
    ppermute x1, starting transfers between devices, per_device(): w_other = lax.ppermute(w_own, 'sample', [(i, i ^ 1) for i in range(16)])  4.65 us
  transfers between devices with their start and end apart: 11, of which 8 were waited for; matrix products, arithmetic and copies ran while one was open for 1% of the time, Pallas kernels for 8%

profile of v4, /device:TPU:1, one launch (start us, length us, event | category | flops | bytes accessed | tf_op | source)
XLA Modules:
  0.0 98.0 jit_solution(14827628626637973854)
XLA Ops:
  0.6 2.4 %spread_weights.1 = bf16[8,64,2048]{2,1,0:T(8,128)(2,1)} custom-call(bf16[32,2048]{1,0:T(8,128)(2,1)} %key_ref.1, bf16[32,2048]{1,0:T(8,128)(2,1)} %value_ref.1), custom_call_target="tpu_custom_call" | custom-call | tf_op jit(solution)/shard_map/spread_weights/pallas_call | solution.py:36
  3.1 6.8 %all-to-all-start = ((bf16[8,64,2048]{2,1,0:T(8,128)(2,1)}), bf16[8,64,2048]{2,1,0:T(8,128)(2,1)S(1)}, u32[]{:S(2)}, u32[]{:S(2)}) async-start(bf16[8,64,2048]{2,1,0:T(8,128)(2,1)} %spread_weights.1), calls=%async_computation | async-start | bytes 4194304 | tf_op jit(solution)/shard_map/all_to_all | solution.py:324
  10.0 7.4 %collective-permute-start = (bf16[32,640]{1,0:T(8,128)(2,1)S(1)}, bf16[32,640]{1,0:T(8,128)(2,1)S(1)}, u32[]{:S(2)}, u32[]{:S(2)}) collective-permute-start(bf16[32,640]{1,0:T(8,128)(2,1)S(1)} %pad_maximum_fusion.1), channel_id=1, source_target_pairs={{0,64},{16,80},{32,96},{48,112},{64,0},{80,16},{96,32},{112,48},{1... | collective-permute-start | bytes 122888 | tf_op jit(solution)/shard_map/ppermute | solution.py:296
  17.4 1.4 %collective-permute-done = bf16[32,640]{1,0:T(8,128)(2,1)S(1)} collective-permute-done((bf16[32,640]{1,0:T(8,128)(2,1)S(1)}, bf16[32,640]{1,0:T(8,128)(2,1)S(1)}, u32[]{:S(2)}, u32[]{:S(2)}) %collective-permute-start) | collective-permute-done | bytes 40992 | tf_op jit(solution)/shard_map/ppermute | solution.py:296
  18.9 3.1 %collective-permute-start.1 = (bf16[64,640]{1,0:T(8,128)(2,1)S(1)}, bf16[64,640]{1,0:T(8,128)(2,1)S(1)}, u32[]{:S(2)}, u32[]{:S(2)}) collective-permute-start(bf16[64,640]{1,0:T(8,128)(2,1)S(1)} %pad_maximum_fusion.piece_0), channel_id=1, source_target_pairs={{0,16},{16,0},{32,48},{48,32},{64,80},{80,64},{96,112},{112,96},{1... | collective-permute-start | bytes 245768 | tf_op jit(solution)/shard_map/ppermute | solution.py:296
  22.0 4.1 %collective-permute-start.2 = (bf16[64,640]{1,0:T(8,128)(2,1)S(1)}, bf16[64,640]{1,0:T(8,128)(2,1)S(1)}, u32[]{:S(2)}, u32[]{:S(2)}) collective-permute-start(bf16[64,640]{1,0:T(8,128)(2,1)S(1)} %pad_maximum_fusion.piece_0), channel_id=1, source_target_pairs={{0,32},{16,48},{32,0},{48,16},{64,96},{80,112},{96,64},{112,80},{1... | collective-permute-start | bytes 245768 | tf_op jit(solution)/shard_map/ppermute | solution.py:296
  26.1 2.3 %collective-permute-start.3 = (bf16[64,640]{1,0:T(8,128)(2,1)S(1)}, bf16[64,640]{1,0:T(8,128)(2,1)S(1)}, u32[]{:S(2)}, u32[]{:S(2)}) collective-permute-start(bf16[64,640]{1,0:T(8,128)(2,1)S(1)} %pad_maximum_fusion.piece_0), channel_id=1, source_target_pairs={{0,48},{16,32},{32,16},{48,0},{64,112},{80,96},{96,80},{112,64},{1... | collective-permute-start | bytes 245768 | tf_op jit(solution)/shard_map/ppermute | solution.py:296
  29.2 4.7 %collective-permute-done.3.piece_3 = bf16[64,640]{1,0:T(8,128)(2,1)S(1)} collective-permute-done((bf16[64,640]{1,0:T(8,128)(2,1)S(1)}, bf16[64,640]{1,0:T(8,128)(2,1)S(1)}, u32[]{:S(2)}, u32[]{:S(2)}) %collective-permute-start.3) | collective-permute-done | bytes 81952 | tf_op jit(solution)/shard_map/ppermute | solution.py:296
  35.1 4.7 %collective-permute-start.4 = (bf16[8,64,2048]{2,1,0:T(8,128)(2,1)S(1)}, bf16[8,64,2048]{2,1,0:T(8,128)(2,1)}, u32[]{:S(2)}, u32[]{:S(2)}) collective-permute-start(bf16[8,64,2048]{2,1,0:T(8,128)(2,1)S(1)} %all-to-all-done.wk_own.wv_own), channel_id=1, source_target_pairs={{0,1},{1,0},{2,3},{3,2},{4,5},{5,4},{6,7},{7,6},{8,9},{9,8},{10,11... | collective-permute-start | bytes 6291464 | tf_op jit(solution)/shard_map/ppermute | solution.py:329
  41.6 2.0 %collective-permute-done.4.wk_oth.wv_oth = bf16[8,64,2048]{2,1,0:T(8,128)(2,1)} collective-permute-done((bf16[8,64,2048]{2,1,0:T(8,128)(2,1)S(1)}, bf16[8,64,2048]{2,1,0:T(8,128)(2,1)}, u32[]{:S(2)}, u32[]{:S(2)}) %collective-permute-start.4) | collective-permute-done | bytes 2097184 | tf_op jit(solution)/shard_map/ppermute | solution.py:329
  43.6 10.5 %key_terms.1 = bf16[8,32,1152]{2,1,0:T(8,128)(2,1)} custom-call(s32[4]{0:T(128)} %pad_add_fusion.facts_ref, bf16[128,2048]{1,0:T(8,128)(2,1)} %qn_ref.3, bf16[128,1024]{1,0:T(8,128)(2,1)} %qr_ref.3, bf16[128,2048]{1,0:T(8,128)(2,1)} %og_ref.3, bf16[384,640]{1,0:T(8,128)(2,1)} %copy-done.2, bf16[8,64,2048]{2,1,0:T(8,128)(2,1)} %copy-done, ...), custom_call_target="tpu_custom_call" | custom-call | flops 6000000000 | bytes 8388608 | tf_op jit(solution)/shard_map/key_terms/pallas_call | solution.py:188
  54.1 5.9 %all-to-all-start.1 = ((bf16[8,32,1152]{2,1,0:T(8,128)(2,1)}), bf16[8,32,1152]{2,1,0:T(8,128)(2,1)S(1)}, u32[]{:S(2)}, u32[]{:S(2)}) async-start(bf16[8,32,1152]{2,1,0:T(8,128)(2,1)} %key_terms.1), calls=%async_computation.1 | async-start | bytes 1179648 | tf_op jit(solution)/shard_map/all_to_all | solution.py:334
  60.0 1.6 %copy-done.1 = bf16[8,64,2048]{2,1,0:T(8,128)(2,1)S(1)} copy-done((bf16[8,64,2048]{2,1,0:T(8,128)(2,1)S(1)}, bf16[8,64,2048]{2,1,0:T(8,128)(2,1)}, u32[]{:S(2)}) %copy-start.1) | copy-done | bytes 2097176
  61.6 1.0 %copy-done.7 = bf16[128,2048]{1,0:T(8,128)(2,1)S(1)} copy-done((bf16[128,2048]{1,0:T(8,128)(2,1)S(1)}, bf16[128,2048]{1,0:T(8,128)(2,1)}, u32[]{:S(2)}) %copy-start.7) | copy-done | bytes 524312
  62.7 1.0 %copy-done.8 = bf16[128,2048]{1,0:T(8,128)(2,1)S(1)} copy-done((bf16[128,2048]{1,0:T(8,128)(2,1)S(1)}, bf16[128,2048]{1,0:T(8,128)(2,1)}, u32[]{:S(2)}) %copy-start.8) | copy-done | bytes 524312
  63.7 8.2 %attention.1 = (bf16[128,2048]{1,0:T(8,128)(2,1)}, bf16[128,2048]{1,0:T(8,128)(2,1)}, bf16[128,1024]{1,0:T(8,128)(2,1)}) custom-call(s32[4]{0:T(128)S(1)} %copy-done.6, bf16[128,2048]{1,0:T(8,128)(2,1)S(1)} %copy-done.7, bf16[128,1024]{1,0:T(8,128)(2,1)S(1)} %copy-done.9, bf16[128,2048]{1,0:T(8,128)(2,1)S(1)} %copy-done.8, bf16[384,640]{1,0:T(8,128)(2,1)S(1)} %copy-done.3, ...), custom_call_target="tpu_custom_call" | custom-call | flops 6000000000 | bytes 8388608 | tf_op jit(solution)/shard_map/attention/pallas_call | solution.py:188
  71.9 7.4 %all-to-all-done.1.terms_ref = bf16[8,32,1152]{2,1,0:T(8,128)(2,1)S(1)} async-done(((bf16[8,32,1152]{2,1,0:T(8,128)(2,1)}), bf16[8,32,1152]{2,1,0:T(8,128)(2,1)S(1)}, u32[]{:S(2)}, u32[]{:S(2)}) %all-to-all-start.1) | async-done | bytes 589856 | tf_op jit(solution)/shard_map/all_to_all | solution.py:334
  79.4 1.0 %add_heads.1 = (bf16[16,32,640]{2,1,0:T(8,128)(2,1)}, bf16[32,640]{1,0:T(8,128)(2,1)S(1)}) custom-call(bf16[8,32,1152]{2,1,0:T(8,128)(2,1)S(1)} %all-to-all-done.1.terms_ref), custom_call_target="tpu_custom_call" | custom-call | tf_op jit(solution)/shard_map/add_heads/pallas_call | solution.py:244
  80.4 4.9 %all-to-all-start.2 = ((bf16[16,32,640]{2,1,0:T(8,128)(2,1)}), bf16[16,32,640]{2,1,0:T(8,128)(2,1)S(1)}, u32[]{:S(2)}, u32[]{:S(2)}) async-start(bf16[16,32,640]{2,1,0:T(8,128)(2,1)} %get-tuple-element.35), calls=%async_computation.2 | async-start | bytes 1310720 | tf_op jit(solution)/shard_map/all_to_all | solution.py:336
  85.3 2.2 %collective-permute-start.5 = (bf16[32,640]{1,0:T(8,128)(2,1)S(1)}, bf16[32,640]{1,0:T(8,128)(2,1)S(1)}, u32[]{:S(2)}, u32[]{:S(2)}) collective-permute-start(bf16[32,640]{1,0:T(8,128)(2,1)S(1)} %get-tuple-element.36.piece_0), channel_id=1, source_target_pairs={{0,16},{16,0},{32,48},{48,32},{64,80},{80,64},{96,112},{112,96},{1... | collective-permute-start | bytes 122888 | tf_op jit(solution)/shard_map/ppermute | solution.py:296
  87.5 1.9 %collective-permute-start.6 = (bf16[32,640]{1,0:T(8,128)(2,1)S(1)}, bf16[32,640]{1,0:T(8,128)(2,1)S(1)}, u32[]{:S(2)}, u32[]{:S(2)}) collective-permute-start(bf16[32,640]{1,0:T(8,128)(2,1)S(1)} %get-tuple-element.36.piece_0), channel_id=1, source_target_pairs={{0,32},{16,48},{32,0},{48,16},{64,96},{80,112},{96,64},{112,80},{1... | collective-permute-start | bytes 122888 | tf_op jit(solution)/shard_map/ppermute | solution.py:296
  89.5 5.2 %collective-permute-start.7 = (bf16[32,640]{1,0:T(8,128)(2,1)S(1)}, bf16[32,640]{1,0:T(8,128)(2,1)S(1)}, u32[]{:S(2)}, u32[]{:S(2)}) collective-permute-start(bf16[32,640]{1,0:T(8,128)(2,1)S(1)} %get-tuple-element.36.piece_0), channel_id=1, source_target_pairs={{0,48},{16,32},{32,16},{48,0},{64,112},{80,96},{96,80},{112,64},{1... | collective-permute-start | bytes 122888 | tf_op jit(solution)/shard_map/ppermute | solution.py:296
  94.7 1.5 %collective-permute-done.7.piece_3 = bf16[32,640]{1,0:T(8,128)(2,1)S(1)} collective-permute-done((bf16[32,640]{1,0:T(8,128)(2,1)S(1)}, bf16[32,640]{1,0:T(8,128)(2,1)S(1)}, u32[]{:S(2)}, u32[]{:S(2)}) %collective-permute-start.7) | collective-permute-done | bytes 40992 | tf_op jit(solution)/shard_map/ppermute | solution.py:296
  96.7 1.3 %finish.1 = (f32[32,512]{1,0:T(8,128)}, f32[32,64]{1,0:T(8,128)}, f32[128,512]{1,0:T(8,128)}, f32[64,128]{1,0:T(8,128)}) custom-call(s32[4]{0:T(128)S(1)} %copy-done.6, bf16[16,32,640]{2,1,0:T(8,128)(2,1)S(1)} %all-to-all-done.2.prompt_ref, bf16[32,640]{1,0:T(8,128)(2,1)S(1)} %get-tuple-element.36.piece_0, ...), custom_call_target="tpu_custom_call" | custom-call | tf_op jit(solution)/shard_map/finish/pallas_call | solution.py:279
  (31 shorter events, 3.2 us)
Async XLA Ops:
  3.0 6.9 %copy-start.10 = (bf16[32,512]{1,0:T(8,128)(2,1)S(1)}, bf16[32,512]{1,0:T(8,128)(2,1)}, u32[]{:S(2)}) copy-start(bf16[32,512]{1,0:T(8,128)(2,1)} %param.13) | copy-start | bytes 98308
  3.0 6.8 %copy-start.11 = (bf16[32,64]{1,0:T(8,128)(2,1)S(1)}, bf16[32,64]{1,0:T(8,128)(2,1)}, u32[]{:S(2)}) copy-start(bf16[32,64]{1,0:T(8,128)(2,1)} %param.14) | copy-start | bytes 12292
  3.0 30.9 %copy-start.4 = (bf16[128,512]{1,0:T(8,128)(2,1)S(1)}, bf16[128,512]{1,0:T(8,128)(2,1)}, u32[]{:S(2)}) copy-start(bf16[128,512]{1,0:T(8,128)(2,1)} %lat_ref.1) | copy-start | bytes 393220
  3.1 30.9 %copy-start.5 = (bf16[128,64]{0,1:T(8,128)(2,1)S(1)}, bf16[128,64]{0,1:T(8,128)(2,1)}, u32[]{:S(2)}) copy-start(bf16[128,64]{0,1:T(8,128)(2,1)} %param.16) | copy-start | bytes 49156
  3.1 32.0 %all-to-all-start = ((bf16[8,64,2048]{2,1,0:T(8,128)(2,1)}), bf16[8,64,2048]{2,1,0:T(8,128)(2,1)S(1)}, u32[]{:S(2)}, u32[]{:S(2)}) async-start(bf16[8,64,2048]{2,1,0:T(8,128)(2,1)} %spread_weights.1), calls=%async_computation | async-start | bytes 4194304 | tf_op jit(solution)/shard_map/all_to_all | solution.py:324
  10.0 8.9 %collective-permute-start = (bf16[32,640]{1,0:T(8,128)(2,1)S(1)}, bf16[32,640]{1,0:T(8,128)(2,1)S(1)}, u32[]{:S(2)}, u32[]{:S(2)}) collective-permute-start(bf16[32,640]{1,0:T(8,128)(2,1)S(1)} %pad_maximum_fusion.1), channel_id=1, source_target_pairs={{0,64},{16,80},{32,96},{48,112},{64,0},{80,16},{96,32},{112,48},{1... | collective-permute-start | bytes 122888 | tf_op jit(solution)/shard_map/ppermute | solution.py:296
  18.9 9.5 %collective-permute-start.1 = (bf16[64,640]{1,0:T(8,128)(2,1)S(1)}, bf16[64,640]{1,0:T(8,128)(2,1)S(1)}, u32[]{:S(2)}, u32[]{:S(2)}) collective-permute-start(bf16[64,640]{1,0:T(8,128)(2,1)S(1)} %pad_maximum_fusion.piece_0), channel_id=1, source_target_pairs={{0,16},{16,0},{32,48},{48,32},{64,80},{80,64},{96,112},{112,96},{1... | collective-permute-start | bytes 245768 | tf_op jit(solution)/shard_map/ppermute | solution.py:296
  22.0 7.2 %collective-permute-start.2 = (bf16[64,640]{1,0:T(8,128)(2,1)S(1)}, bf16[64,640]{1,0:T(8,128)(2,1)S(1)}, u32[]{:S(2)}, u32[]{:S(2)}) collective-permute-start(bf16[64,640]{1,0:T(8,128)(2,1)S(1)} %pad_maximum_fusion.piece_0), channel_id=1, source_target_pairs={{0,32},{16,48},{32,0},{48,16},{64,96},{80,112},{96,64},{112,80},{1... | collective-permute-start | bytes 245768 | tf_op jit(solution)/shard_map/ppermute | solution.py:296
  26.1 7.8 %collective-permute-start.3 = (bf16[64,640]{1,0:T(8,128)(2,1)S(1)}, bf16[64,640]{1,0:T(8,128)(2,1)S(1)}, u32[]{:S(2)}, u32[]{:S(2)}) collective-permute-start(bf16[64,640]{1,0:T(8,128)(2,1)S(1)} %pad_maximum_fusion.piece_0), channel_id=1, source_target_pairs={{0,48},{16,32},{32,16},{48,0},{64,112},{80,96},{96,80},{112,64},{1... | collective-permute-start | bytes 245768 | tf_op jit(solution)/shard_map/ppermute | solution.py:296
  34.0 0.8 copy-start.2
  35.1 8.6 %copy-start = (bf16[8,64,2048]{2,1,0:T(8,128)(2,1)}, bf16[8,64,2048]{2,1,0:T(8,128)(2,1)S(1)}, u32[]{:S(2)}) copy-start(bf16[8,64,2048]{2,1,0:T(8,128)(2,1)S(1)} %all-to-all-done.wk_own.wv_own) | copy-start | bytes 6291460
  35.1 8.6 %collective-permute-start.4 = (bf16[8,64,2048]{2,1,0:T(8,128)(2,1)S(1)}, bf16[8,64,2048]{2,1,0:T(8,128)(2,1)}, u32[]{:S(2)}, u32[]{:S(2)}) collective-permute-start(bf16[8,64,2048]{2,1,0:T(8,128)(2,1)S(1)} %all-to-all-done.wk_own.wv_own), channel_id=1, source_target_pairs={{0,1},{1,0},{2,3},{3,2},{4,5},{5,4},{6,7},{7,6},{8,9},{9,8},{10,11... | collective-permute-start | bytes 6291464 | tf_op jit(solution)/shard_map/ppermute | solution.py:329
  41.6 18.4 %copy-start.3 = (bf16[384,640]{1,0:T(8,128)(2,1)S(1)}, bf16[384,640]{1,0:T(8,128)(2,1)}, u32[]{:S(2)}) copy-start(bf16[384,640]{1,0:T(8,128)(2,1)} %copy-done.2) | copy-start | bytes 1474564
  41.6 18.4 %copy-start.6 = (s32[4]{0:T(128)S(1)}, s32[4]{0:T(128)}, u32[]{:S(2)}) copy-start(s32[4]{0:T(128)} %pad_add_fusion.facts_ref) | copy-start | bytes 52
  41.6 18.4 %copy-start.9 = (bf16[128,1024]{1,0:T(8,128)(2,1)S(1)}, bf16[128,1024]{1,0:T(8,128)(2,1)}, u32[]{:S(2)}) copy-start(bf16[128,1024]{1,0:T(8,128)(2,1)} %qr_ref.3) | copy-start | bytes 786436
  54.1 25.2 %all-to-all-start.1 = ((bf16[8,32,1152]{2,1,0:T(8,128)(2,1)}), bf16[8,32,1152]{2,1,0:T(8,128)(2,1)S(1)}, u32[]{:S(2)}, u32[]{:S(2)}) async-start(bf16[8,32,1152]{2,1,0:T(8,128)(2,1)} %key_terms.1), calls=%async_computation.1 | async-start | bytes 1179648 | tf_op jit(solution)/shard_map/all_to_all | solution.py:334
  60.0 1.6 %copy-start.1 = (bf16[8,64,2048]{2,1,0:T(8,128)(2,1)S(1)}, bf16[8,64,2048]{2,1,0:T(8,128)(2,1)}, u32[]{:S(2)}) copy-start(bf16[8,64,2048]{2,1,0:T(8,128)(2,1)} %copy-done) | copy-start | bytes 6291460
  61.6 1.0 %copy-start.7 = (bf16[128,2048]{1,0:T(8,128)(2,1)S(1)}, bf16[128,2048]{1,0:T(8,128)(2,1)}, u32[]{:S(2)}) copy-start(bf16[128,2048]{1,0:T(8,128)(2,1)} %qn_ref.3) | copy-start | bytes 1572868
  62.7 1.0 %copy-start.8 = (bf16[128,2048]{1,0:T(8,128)(2,1)S(1)}, bf16[128,2048]{1,0:T(8,128)(2,1)}, u32[]{:S(2)}) copy-start(bf16[128,2048]{1,0:T(8,128)(2,1)} %og_ref.3) | copy-start | bytes 1572868
  80.4 16.3 %all-to-all-start.2 = ((bf16[16,32,640]{2,1,0:T(8,128)(2,1)}), bf16[16,32,640]{2,1,0:T(8,128)(2,1)S(1)}, u32[]{:S(2)}, u32[]{:S(2)}) async-start(bf16[16,32,640]{2,1,0:T(8,128)(2,1)} %get-tuple-element.35), calls=%async_computation.2 | async-start | bytes 1310720 | tf_op jit(solution)/shard_map/all_to_all | solution.py:336
  85.3 9.3 %collective-permute-start.5 = (bf16[32,640]{1,0:T(8,128)(2,1)S(1)}, bf16[32,640]{1,0:T(8,128)(2,1)S(1)}, u32[]{:S(2)}, u32[]{:S(2)}) collective-permute-start(bf16[32,640]{1,0:T(8,128)(2,1)S(1)} %get-tuple-element.36.piece_0), channel_id=1, source_target_pairs={{0,16},{16,0},{32,48},{48,32},{64,80},{80,64},{96,112},{112,96},{1... | collective-permute-start | bytes 122888 | tf_op jit(solution)/shard_map/ppermute | solution.py:296
  87.5 7.1 %collective-permute-start.6 = (bf16[32,640]{1,0:T(8,128)(2,1)S(1)}, bf16[32,640]{1,0:T(8,128)(2,1)S(1)}, u32[]{:S(2)}, u32[]{:S(2)}) collective-permute-start(bf16[32,640]{1,0:T(8,128)(2,1)S(1)} %get-tuple-element.36.piece_0), channel_id=1, source_target_pairs={{0,32},{16,48},{32,0},{48,16},{64,96},{80,112},{96,64},{112,80},{1... | collective-permute-start | bytes 122888 | tf_op jit(solution)/shard_map/ppermute | solution.py:296
  89.5 6.7 %collective-permute-start.7 = (bf16[32,640]{1,0:T(8,128)(2,1)S(1)}, bf16[32,640]{1,0:T(8,128)(2,1)S(1)}, u32[]{:S(2)}, u32[]{:S(2)}) collective-permute-start(bf16[32,640]{1,0:T(8,128)(2,1)S(1)} %get-tuple-element.36.piece_0), channel_id=1, source_target_pairs={{0,48},{16,32},{32,16},{48,0},{64,112},{80,96},{96,80},{112,64},{1... | collective-permute-start | bytes 122888 | tf_op jit(solution)/shard_map/ppermute | solution.py:296

commit v5 on v4

--- a/solution.py
+++ b/solution.py
@@ -25,12 +25,14 @@
         ]
         for move in moves:
             move.start()
-        for move in moves:
+        sent = []
+        for k, move in enumerate(moves):
             move.wait()
-        moves = [pltpu.make_async_copy(held, out_ref.at[j], sems.at[j]) for j in range(copies)]
-        for move in moves:
-            move.start()
-        for move in moves:
+            at = pl.ds(k * rows, rows)
+            for j in range(copies):
+                sent.append(pltpu.make_async_copy(held.at[at], out_ref.at[j, at], sems.at[2 + k * copies + j]))
+                sent[-1].start()
+        for move in sent:
             move.wait()
 
     return pl.pallas_call(
@@ -38,7 +40,7 @@
         out_shape=pltpu.HBM((copies, 2 * rows, cols), BF),
         in_specs=[pl.BlockSpec(memory_space=pltpu.HBM)] * 2,
         out_specs=pl.BlockSpec(memory_space=pl.ANY),
-        scratch_shapes=[pltpu.VMEM((2 * rows, cols), BF), pltpu.SemaphoreType.DMA((copies,))],
+        scratch_shapes=[pltpu.VMEM((2 * rows, cols), BF), pltpu.SemaphoreType.DMA((2 + 2 * copies,))],
         compiler_params=pltpu.CompilerParams(vmem_limit_bytes=58 * 2**20),
         name="spread_weights",
     )(w_key, w_value)
@@ -69,7 +71,7 @@
         kernel,
         in_specs=[pl.BlockSpec(memory_space=pltpu.VMEM)] * 6,
         out_specs=pl.BlockSpec(memory_space=pltpu.VMEM),
-        out_shape=jax.ShapeDtypeStruct((key_count, WIDE), BF),
+        out_shape=pltpu.HBM((key_count, WIDE), BF),
         compiler_params=pltpu.CompilerParams(vmem_limit_bytes=4 * 2**20),
         name="join_keys",
     )(*pieces, resp_latent, resp_rope.T)
@@ -141,7 +143,15 @@
             query.append(jnp.concatenate([qn_ref[:, cols[h]], rope], axis=1))
         grad_out = [(og_ref[:, c].astype(F32) * alive).astype(BF) for c in cols]
         scores = [dot(key_full[h], query[h], ((1,), (1,))) + bias[...] for h in heads]
-        grad_prob = [dot(value[h], grad_out[h], ((1,), (1,))) for h in heads]
+        blank = jnp.zeros((row_count, 128), BF)
+        grad_pair = [
+            jnp.concatenate(
+                [jnp.concatenate([grad_out[h], blank], axis=1), jnp.concatenate([blank, grad_out[h + 1]], axis=1)], axis=0)
+            for h in heads[::2]]
+        grad_prob = []
+        for h in heads[::2]:
+            pair = dot(jnp.concatenate(value[h:h + 2], axis=1), grad_pair[h // 2], ((1,), (1,)))
+            grad_prob += [pair[:, :row_count], pair[:, row_count:]]
         prob_half, grad_score = [], []
         for h in heads:
             top = jnp.max(scores[h], axis=0, keepdims=True)
@@ -162,7 +172,10 @@
                         lane < 64, grad_query[h - 1][:, 128:], grad_query[h][:, 128:]).astype(BF)
             return
         grad_key = [dot(grad_score[h], query[h], ((1,), (0,))) for h in heads]
-        grad_value = [dot(prob_half[h], grad_out[h], ((1,), (0,))) for h in heads]
+        grad_value = []
+        for h in heads[::2]:
+            pair = dot(jnp.concatenate(prob_half[h:h + 2], axis=1), grad_pair[h // 2], ((1,), (0,)))
+            grad_value += [pair[:, :128], pair[:, 128:]]
         grads = []
         rope_sum = None
         for h in heads:

time: 98.8 us -> 98.7 us (level)
    unnamed x24 -> x22, local copies, waits for them, and re-layouts: 4.48 us -> 3.71 us
  transfers between devices with their start and end apart: 11 -> 11, of which waited for: 8 -> 8; matrix products, arithmetic and copies ran while one was open for 1% -> 1% of each run, Pallas kernels for 8% -> 9%
where the time goes in v5:
time: 98.7 us; the launch traced here: 97.9 us
  starting transfers between devices  48.4 us (49%)
  Pallas kernels  24.3 us (25%)
  waiting for transfers between devices  18.6 us (19%)
  local copies, waits for them, and re-layouts  3.71 us (4%)
  between operations  2.12 us (2%)
    ppermute x7, starting transfers between devices, from_distance(): return lax.ppermute(block, 'ctx', [(i, i ^ distance) for i in range(8)])  26.2 us
    pallas_call x2, Pallas kernels, attention(): pl.pallas_call(kernel, grid=(steps,), in_specs=[pl.BlockSpec(memory_space...  18.6 us
    ppermute x7, waiting for transfers between devices, from_distance(): return lax.ppermute(block, 'ctx', [(i, i ^ distance) for i in range(8)])  8.35 us
    all_to_all x1, waiting for transfers between devices, per_device(): lax.all_to_all(terms, 'ctx', 0, 0, tiled=True)  7.42 us
    all_to_all x1, starting transfers between devices, per_device(): lax.all_to_all(spread_weights(w_key, w_value, 8), 'sample', 0, 0, tiled=T...  6.8 us
    all_to_all x1, starting transfers between devices, per_device(): lax.all_to_all(terms, 'ctx', 0, 0, tiled=True)  5.87 us
    all_to_all x1, starting transfers between devices, per_device(): prompt_part = lax.all_to_all(prompt_part, 'sample', 0, 0, tiled=True)  4.89 us
    ppermute x1, starting transfers between devices, per_device(): w_other = lax.ppermute(w_own, 'sample', [(i, i ^ 1) for i in range(16)])  4.65 us
  transfers between devices with their start and end apart: 11, of which 8 were waited for; matrix products, arithmetic and copies ran while one was open for 1% of the time, Pallas kernels for 9%

profile of v5, /device:TPU:1, one launch (start us, length us, event | category | flops | bytes accessed | tf_op | source)
XLA Modules:
  0.0 97.9 jit_solution(16638711484591374051)
XLA Ops:
  0.6 2.4 %spread_weights.1 = bf16[8,64,2048]{2,1,0:T(8,128)(2,1)} custom-call(bf16[32,2048]{1,0:T(8,128)(2,1)} %key_ref.1, bf16[32,2048]{1,0:T(8,128)(2,1)} %value_ref.1), custom_call_target="tpu_custom_call" | custom-call | tf_op jit(solution)/shard_map/spread_weights/pallas_call | solution.py:38
  3.1 6.8 %all-to-all-start = ((bf16[8,64,2048]{2,1,0:T(8,128)(2,1)}), bf16[8,64,2048]{2,1,0:T(8,128)(2,1)S(1)}, u32[]{:S(2)}, u32[]{:S(2)}) async-start(bf16[8,64,2048]{2,1,0:T(8,128)(2,1)} %spread_weights.1), calls=%async_computation | async-start | bytes 4194304 | tf_op jit(solution)/shard_map/all_to_all | solution.py:337
  10.0 7.4 %collective-permute-start = (bf16[32,640]{1,0:T(8,128)(2,1)S(1)}, bf16[32,640]{1,0:T(8,128)(2,1)S(1)}, u32[]{:S(2)}, u32[]{:S(2)}) collective-permute-start(bf16[32,640]{1,0:T(8,128)(2,1)S(1)} %pad_maximum_fusion.1), channel_id=1, source_target_pairs={{0,64},{16,80},{32,96},{48,112},{64,0},{80,16},{96,32},{112,48},{1... | collective-permute-start | bytes 122888 | tf_op jit(solution)/shard_map/ppermute | solution.py:309
  17.4 1.4 %collective-permute-done = bf16[32,640]{1,0:T(8,128)(2,1)S(1)} collective-permute-done((bf16[32,640]{1,0:T(8,128)(2,1)S(1)}, bf16[32,640]{1,0:T(8,128)(2,1)S(1)}, u32[]{:S(2)}, u32[]{:S(2)}) %collective-permute-start) | collective-permute-done | bytes 40992 | tf_op jit(solution)/shard_map/ppermute | solution.py:309
  18.9 3.1 %collective-permute-start.1 = (bf16[64,640]{1,0:T(8,128)(2,1)S(1)}, bf16[64,640]{1,0:T(8,128)(2,1)S(1)}, u32[]{:S(2)}, u32[]{:S(2)}) collective-permute-start(bf16[64,640]{1,0:T(8,128)(2,1)S(1)} %pad_maximum_fusion.piece_0), channel_id=1, source_target_pairs={{0,16},{16,0},{32,48},{48,32},{64,80},{80,64},{96,112},{112,96},{1... | collective-permute-start | bytes 245768 | tf_op jit(solution)/shard_map/ppermute | solution.py:309
  22.0 4.1 %collective-permute-start.2 = (bf16[64,640]{1,0:T(8,128)(2,1)S(1)}, bf16[64,640]{1,0:T(8,128)(2,1)S(1)}, u32[]{:S(2)}, u32[]{:S(2)}) collective-permute-start(bf16[64,640]{1,0:T(8,128)(2,1)S(1)} %pad_maximum_fusion.piece_0), channel_id=1, source_target_pairs={{0,32},{16,48},{32,0},{48,16},{64,96},{80,112},{96,64},{112,80},{1... | collective-permute-start | bytes 245768 | tf_op jit(solution)/shard_map/ppermute | solution.py:309
  26.1 2.3 %collective-permute-start.3 = (bf16[64,640]{1,0:T(8,128)(2,1)S(1)}, bf16[64,640]{1,0:T(8,128)(2,1)S(1)}, u32[]{:S(2)}, u32[]{:S(2)}) collective-permute-start(bf16[64,640]{1,0:T(8,128)(2,1)S(1)} %pad_maximum_fusion.piece_0), channel_id=1, source_target_pairs={{0,48},{16,32},{32,16},{48,0},{64,112},{80,96},{96,80},{112,64},{1... | collective-permute-start | bytes 245768 | tf_op jit(solution)/shard_map/ppermute | solution.py:309
  29.2 4.7 %collective-permute-done.3.piece_3 = bf16[64,640]{1,0:T(8,128)(2,1)S(1)} collective-permute-done((bf16[64,640]{1,0:T(8,128)(2,1)S(1)}, bf16[64,640]{1,0:T(8,128)(2,1)S(1)}, u32[]{:S(2)}, u32[]{:S(2)}) %collective-permute-start.3) | collective-permute-done | bytes 81952 | tf_op jit(solution)/shard_map/ppermute | solution.py:309
  35.1 4.6 %collective-permute-start.4 = (bf16[8,64,2048]{2,1,0:T(8,128)(2,1)S(1)}, bf16[8,64,2048]{2,1,0:T(8,128)(2,1)}, u32[]{:S(2)}, u32[]{:S(2)}) collective-permute-start(bf16[8,64,2048]{2,1,0:T(8,128)(2,1)S(1)} %all-to-all-done.wk_own.wv_own), channel_id=1, source_target_pairs={{0,1},{1,0},{2,3},{3,2},{4,5},{5,4},{6,7},{7,6},{8,9},{9,8},{10,11... | collective-permute-start | bytes 6291464 | tf_op jit(solution)/shard_map/ppermute | solution.py:342
  41.6 2.0 %collective-permute-done.4.wk_oth.wv_oth = bf16[8,64,2048]{2,1,0:T(8,128)(2,1)} collective-permute-done((bf16[8,64,2048]{2,1,0:T(8,128)(2,1)S(1)}, bf16[8,64,2048]{2,1,0:T(8,128)(2,1)}, u32[]{:S(2)}, u32[]{:S(2)}) %collective-permute-start.4) | collective-permute-done | bytes 2097184 | tf_op jit(solution)/shard_map/ppermute | solution.py:342
  43.6 10.4 %key_terms.1 = bf16[8,32,1152]{2,1,0:T(8,128)(2,1)} custom-call(s32[4]{0:T(128)} %pad_add_fusion.facts_ref, bf16[128,2048]{1,0:T(8,128)(2,1)} %qn_ref.3, bf16[128,1024]{1,0:T(8,128)(2,1)} %qr_ref.3, bf16[128,2048]{1,0:T(8,128)(2,1)} %og_ref.3, bf16[384,640]{1,0:T(8,128)(2,1)} %join_keys.1.keys_ref, bf16[8,64,2048]{2,1,0:T(8,128)(2,1)} %copy-done, ...), custom_call_target="tpu_custom_call" | custom-call | flops 6000000000 | bytes 8388608 | tf_op jit(solution)/shard_map/key_terms/pallas_call | solution.py:201
  54.0 5.9 %all-to-all-start.1 = ((bf16[8,32,1152]{2,1,0:T(8,128)(2,1)}), bf16[8,32,1152]{2,1,0:T(8,128)(2,1)S(1)}, u32[]{:S(2)}, u32[]{:S(2)}) async-start(bf16[8,32,1152]{2,1,0:T(8,128)(2,1)} %key_terms.1), calls=%async_computation.1 | async-start | bytes 1179648 | tf_op jit(solution)/shard_map/all_to_all | solution.py:347
  60.0 1.6 %copy-done.1 = bf16[8,64,2048]{2,1,0:T(8,128)(2,1)S(1)} copy-done((bf16[8,64,2048]{2,1,0:T(8,128)(2,1)S(1)}, bf16[8,64,2048]{2,1,0:T(8,128)(2,1)}, u32[]{:S(2)}) %copy-start.1) | copy-done | bytes 2097176
  61.5 1.0 %copy-done.6 = bf16[128,2048]{1,0:T(8,128)(2,1)S(1)} copy-done((bf16[128,2048]{1,0:T(8,128)(2,1)S(1)}, bf16[128,2048]{1,0:T(8,128)(2,1)}, u32[]{:S(2)}) %copy-start.6) | copy-done | bytes 524312
  62.6 1.0 %copy-done.7 = bf16[128,2048]{1,0:T(8,128)(2,1)S(1)} copy-done((bf16[128,2048]{1,0:T(8,128)(2,1)S(1)}, bf16[128,2048]{1,0:T(8,128)(2,1)}, u32[]{:S(2)}) %copy-start.7) | copy-done | bytes 524312
  63.6 8.2 %attention.1 = (bf16[128,2048]{1,0:T(8,128)(2,1)}, bf16[128,2048]{1,0:T(8,128)(2,1)}, bf16[128,1024]{1,0:T(8,128)(2,1)}) custom-call(s32[4]{0:T(128)S(1)} %copy-done.5, bf16[128,2048]{1,0:T(8,128)(2,1)S(1)} %copy-done.6, bf16[128,1024]{1,0:T(8,128)(2,1)S(1)} %copy-done.8, bf16[128,2048]{1,0:T(8,128)(2,1)S(1)} %copy-done.7, bf16[384,640]{1,0:T(8,128)(2,1)S(1)} %copy-done.2, ...), custom_call_target="tpu_custom_call" | custom-call | flops 6000000000 | bytes 8388608 | tf_op jit(solution)/shard_map/attention/pallas_call | solution.py:201
  71.9 7.4 %all-to-all-done.1.terms_ref = bf16[8,32,1152]{2,1,0:T(8,128)(2,1)S(1)} async-done(((bf16[8,32,1152]{2,1,0:T(8,128)(2,1)}), bf16[8,32,1152]{2,1,0:T(8,128)(2,1)S(1)}, u32[]{:S(2)}, u32[]{:S(2)}) %all-to-all-start.1) | async-done | bytes 589856 | tf_op jit(solution)/shard_map/all_to_all | solution.py:347
  79.3 1.0 %add_heads.1 = (bf16[16,32,640]{2,1,0:T(8,128)(2,1)}, bf16[32,640]{1,0:T(8,128)(2,1)S(1)}) custom-call(bf16[8,32,1152]{2,1,0:T(8,128)(2,1)S(1)} %all-to-all-done.1.terms_ref), custom_call_target="tpu_custom_call" | custom-call | tf_op jit(solution)/shard_map/add_heads/pallas_call | solution.py:257
  80.3 4.9 %all-to-all-start.2 = ((bf16[16,32,640]{2,1,0:T(8,128)(2,1)}), bf16[16,32,640]{2,1,0:T(8,128)(2,1)S(1)}, u32[]{:S(2)}, u32[]{:S(2)}) async-start(bf16[16,32,640]{2,1,0:T(8,128)(2,1)} %get-tuple-element.35), calls=%async_computation.2 | async-start | bytes 1310720 | tf_op jit(solution)/shard_map/all_to_all | solution.py:349
  85.2 2.2 %collective-permute-start.5 = (bf16[32,640]{1,0:T(8,128)(2,1)S(1)}, bf16[32,640]{1,0:T(8,128)(2,1)S(1)}, u32[]{:S(2)}, u32[]{:S(2)}) collective-permute-start(bf16[32,640]{1,0:T(8,128)(2,1)S(1)} %get-tuple-element.36.piece_0), channel_id=1, source_target_pairs={{0,16},{16,0},{32,48},{48,32},{64,80},{80,64},{96,112},{112,96},{1... | collective-permute-start | bytes 122888 | tf_op jit(solution)/shard_map/ppermute | solution.py:309
  87.4 1.9 %collective-permute-start.6 = (bf16[32,640]{1,0:T(8,128)(2,1)S(1)}, bf16[32,640]{1,0:T(8,128)(2,1)S(1)}, u32[]{:S(2)}, u32[]{:S(2)}) collective-permute-start(bf16[32,640]{1,0:T(8,128)(2,1)S(1)} %get-tuple-element.36.piece_0), channel_id=1, source_target_pairs={{0,32},{16,48},{32,0},{48,16},{64,96},{80,112},{96,64},{112,80},{1... | collective-permute-start | bytes 122888 | tf_op jit(solution)/shard_map/ppermute | solution.py:309
  89.4 5.2 %collective-permute-start.7 = (bf16[32,640]{1,0:T(8,128)(2,1)S(1)}, bf16[32,640]{1,0:T(8,128)(2,1)S(1)}, u32[]{:S(2)}, u32[]{:S(2)}) collective-permute-start(bf16[32,640]{1,0:T(8,128)(2,1)S(1)} %get-tuple-element.36.piece_0), channel_id=1, source_target_pairs={{0,48},{16,32},{32,16},{48,0},{64,112},{80,96},{96,80},{112,64},{1... | collective-permute-start | bytes 122888 | tf_op jit(solution)/shard_map/ppermute | solution.py:309
  94.6 1.5 %collective-permute-done.7.piece_3 = bf16[32,640]{1,0:T(8,128)(2,1)S(1)} collective-permute-done((bf16[32,640]{1,0:T(8,128)(2,1)S(1)}, bf16[32,640]{1,0:T(8,128)(2,1)S(1)}, u32[]{:S(2)}, u32[]{:S(2)}) %collective-permute-start.7) | collective-permute-done | bytes 40992 | tf_op jit(solution)/shard_map/ppermute | solution.py:309
  96.6 1.3 %finish.1 = (f32[32,512]{1,0:T(8,128)}, f32[32,64]{1,0:T(8,128)}, f32[128,512]{1,0:T(8,128)}, f32[64,128]{1,0:T(8,128)}) custom-call(s32[4]{0:T(128)S(1)} %copy-done.5, bf16[16,32,640]{2,1,0:T(8,128)(2,1)S(1)} %all-to-all-done.2.prompt_ref, bf16[32,640]{1,0:T(8,128)(2,1)S(1)} %get-tuple-element.36.piece_0, ...), custom_call_target="tpu_custom_call" | custom-call | tf_op jit(solution)/shard_map/finish/pallas_call | solution.py:292
  (29 shorter events, 3.3 us)
Async XLA Ops:
  3.0 6.9 %copy-start.9 = (bf16[32,512]{1,0:T(8,128)(2,1)S(1)}, bf16[32,512]{1,0:T(8,128)(2,1)}, u32[]{:S(2)}) copy-start(bf16[32,512]{1,0:T(8,128)(2,1)} %param.13) | copy-start | bytes 98308
  3.1 6.8 %copy-start.10 = (bf16[32,64]{1,0:T(8,128)(2,1)S(1)}, bf16[32,64]{1,0:T(8,128)(2,1)}, u32[]{:S(2)}) copy-start(bf16[32,64]{1,0:T(8,128)(2,1)} %param.14) | copy-start | bytes 12292
  3.1 30.9 %copy-start.3 = (bf16[128,512]{1,0:T(8,128)(2,1)S(1)}, bf16[128,512]{1,0:T(8,128)(2,1)}, u32[]{:S(2)}) copy-start(bf16[128,512]{1,0:T(8,128)(2,1)} %lat_ref.1) | copy-start | bytes 393220
  3.1 30.9 %copy-start.4 = (bf16[128,64]{0,1:T(8,128)(2,1)S(1)}, bf16[128,64]{0,1:T(8,128)(2,1)}, u32[]{:S(2)}) copy-start(bf16[128,64]{0,1:T(8,128)(2,1)} %param.16) | copy-start | bytes 49156
  3.1 32.0 %all-to-all-start = ((bf16[8,64,2048]{2,1,0:T(8,128)(2,1)}), bf16[8,64,2048]{2,1,0:T(8,128)(2,1)S(1)}, u32[]{:S(2)}, u32[]{:S(2)}) async-start(bf16[8,64,2048]{2,1,0:T(8,128)(2,1)} %spread_weights.1), calls=%async_computation | async-start | bytes 4194304 | tf_op jit(solution)/shard_map/all_to_all | solution.py:337
  10.0 8.9 %collective-permute-start = (bf16[32,640]{1,0:T(8,128)(2,1)S(1)}, bf16[32,640]{1,0:T(8,128)(2,1)S(1)}, u32[]{:S(2)}, u32[]{:S(2)}) collective-permute-start(bf16[32,640]{1,0:T(8,128)(2,1)S(1)} %pad_maximum_fusion.1), channel_id=1, source_target_pairs={{0,64},{16,80},{32,96},{48,112},{64,0},{80,16},{96,32},{112,48},{1... | collective-permute-start | bytes 122888 | tf_op jit(solution)/shard_map/ppermute | solution.py:309
  18.9 9.5 %collective-permute-start.1 = (bf16[64,640]{1,0:T(8,128)(2,1)S(1)}, bf16[64,640]{1,0:T(8,128)(2,1)S(1)}, u32[]{:S(2)}, u32[]{:S(2)}) collective-permute-start(bf16[64,640]{1,0:T(8,128)(2,1)S(1)} %pad_maximum_fusion.piece_0), channel_id=1, source_target_pairs={{0,16},{16,0},{32,48},{48,32},{64,80},{80,64},{96,112},{112,96},{1... | collective-permute-start | bytes 245768 | tf_op jit(solution)/shard_map/ppermute | solution.py:309
  22.0 7.2 %collective-permute-start.2 = (bf16[64,640]{1,0:T(8,128)(2,1)S(1)}, bf16[64,640]{1,0:T(8,128)(2,1)S(1)}, u32[]{:S(2)}, u32[]{:S(2)}) collective-permute-start(bf16[64,640]{1,0:T(8,128)(2,1)S(1)} %pad_maximum_fusion.piece_0), channel_id=1, source_target_pairs={{0,32},{16,48},{32,0},{48,16},{64,96},{80,112},{96,64},{112,80},{1... | collective-permute-start | bytes 245768 | tf_op jit(solution)/shard_map/ppermute | solution.py:309
  26.1 7.8 %collective-permute-start.3 = (bf16[64,640]{1,0:T(8,128)(2,1)S(1)}, bf16[64,640]{1,0:T(8,128)(2,1)S(1)}, u32[]{:S(2)}, u32[]{:S(2)}) collective-permute-start(bf16[64,640]{1,0:T(8,128)(2,1)S(1)} %pad_maximum_fusion.piece_0), channel_id=1, source_target_pairs={{0,48},{16,32},{32,16},{48,0},{64,112},{80,96},{96,80},{112,64},{1... | collective-permute-start | bytes 245768 | tf_op jit(solution)/shard_map/ppermute | solution.py:309
  35.1 8.6 %copy-start = (bf16[8,64,2048]{2,1,0:T(8,128)(2,1)}, bf16[8,64,2048]{2,1,0:T(8,128)(2,1)S(1)}, u32[]{:S(2)}) copy-start(bf16[8,64,2048]{2,1,0:T(8,128)(2,1)S(1)} %all-to-all-done.wk_own.wv_own) | copy-start | bytes 6291460
  35.1 8.6 %collective-permute-start.4 = (bf16[8,64,2048]{2,1,0:T(8,128)(2,1)S(1)}, bf16[8,64,2048]{2,1,0:T(8,128)(2,1)}, u32[]{:S(2)}, u32[]{:S(2)}) collective-permute-start(bf16[8,64,2048]{2,1,0:T(8,128)(2,1)S(1)} %all-to-all-done.wk_own.wv_own), channel_id=1, source_target_pairs={{0,1},{1,0},{2,3},{3,2},{4,5},{5,4},{6,7},{7,6},{8,9},{9,8},{10,11... | collective-permute-start | bytes 6291464 | tf_op jit(solution)/shard_map/ppermute | solution.py:342
  41.6 18.3 %copy-start.2 = (bf16[384,640]{1,0:T(8,128)(2,1)S(1)}, bf16[384,640]{1,0:T(8,128)(2,1)}, u32[]{:S(2)}) copy-start(bf16[384,640]{1,0:T(8,128)(2,1)} %join_keys.1.keys_ref) | copy-start | bytes 1474564
  41.6 18.3 %copy-start.5 = (s32[4]{0:T(128)S(1)}, s32[4]{0:T(128)}, u32[]{:S(2)}) copy-start(s32[4]{0:T(128)} %pad_add_fusion.facts_ref) | copy-start | bytes 52
  41.6 18.3 %copy-start.8 = (bf16[128,1024]{1,0:T(8,128)(2,1)S(1)}, bf16[128,1024]{1,0:T(8,128)(2,1)}, u32[]{:S(2)}) copy-start(bf16[128,1024]{1,0:T(8,128)(2,1)} %qr_ref.3) | copy-start | bytes 786436
  54.0 25.2 %all-to-all-start.1 = ((bf16[8,32,1152]{2,1,0:T(8,128)(2,1)}), bf16[8,32,1152]{2,1,0:T(8,128)(2,1)S(1)}, u32[]{:S(2)}, u32[]{:S(2)}) async-start(bf16[8,32,1152]{2,1,0:T(8,128)(2,1)} %key_terms.1), calls=%async_computation.1 | async-start | bytes 1179648 | tf_op jit(solution)/shard_map/all_to_all | solution.py:347
  59.9 1.6 %copy-start.1 = (bf16[8,64,2048]{2,1,0:T(8,128)(2,1)S(1)}, bf16[8,64,2048]{2,1,0:T(8,128)(2,1)}, u32[]{:S(2)}) copy-start(bf16[8,64,2048]{2,1,0:T(8,128)(2,1)} %copy-done) | copy-start | bytes 6291460
  61.5 1.0 %copy-start.6 = (bf16[128,2048]{1,0:T(8,128)(2,1)S(1)}, bf16[128,2048]{1,0:T(8,128)(2,1)}, u32[]{:S(2)}) copy-start(bf16[128,2048]{1,0:T(8,128)(2,1)} %qn_ref.3) | copy-start | bytes 1572868
  62.6 1.0 %copy-start.7 = (bf16[128,2048]{1,0:T(8,128)(2,1)S(1)}, bf16[128,2048]{1,0:T(8,128)(2,1)}, u32[]{:S(2)}) copy-start(bf16[128,2048]{1,0:T(8,128)(2,1)} %og_ref.3) | copy-start | bytes 1572868
  80.3 16.3 %all-to-all-start.2 = ((bf16[16,32,640]{2,1,0:T(8,128)(2,1)}), bf16[16,32,640]{2,1,0:T(8,128)(2,1)S(1)}, u32[]{:S(2)}, u32[]{:S(2)}) async-start(bf16[16,32,640]{2,1,0:T(8,128)(2,1)} %get-tuple-element.35), calls=%async_computation.2 | async-start | bytes 1310720 | tf_op jit(solution)/shard_map/all_to_all | solution.py:349
  85.2 9.3 %collective-permute-start.5 = (bf16[32,640]{1,0:T(8,128)(2,1)S(1)}, bf16[32,640]{1,0:T(8,128)(2,1)S(1)}, u32[]{:S(2)}, u32[]{:S(2)}) collective-permute-start(bf16[32,640]{1,0:T(8,128)(2,1)S(1)} %get-tuple-element.36.piece_0), channel_id=1, source_target_pairs={{0,16},{16,0},{32,48},{48,32},{64,80},{80,64},{96,112},{112,96},{1... | collective-permute-start | bytes 122888 | tf_op jit(solution)/shard_map/ppermute | solution.py:309
  87.4 7.1 %collective-permute-start.6 = (bf16[32,640]{1,0:T(8,128)(2,1)S(1)}, bf16[32,640]{1,0:T(8,128)(2,1)S(1)}, u32[]{:S(2)}, u32[]{:S(2)}) collective-permute-start(bf16[32,640]{1,0:T(8,128)(2,1)S(1)} %get-tuple-element.36.piece_0), channel_id=1, source_target_pairs={{0,32},{16,48},{32,0},{48,16},{64,96},{80,112},{96,64},{112,80},{1... | collective-permute-start | bytes 122888 | tf_op jit(solution)/shard_map/ppermute | solution.py:309
  89.4 6.7 %collective-permute-start.7 = (bf16[32,640]{1,0:T(8,128)(2,1)S(1)}, bf16[32,640]{1,0:T(8,128)(2,1)S(1)}, u32[]{:S(2)}, u32[]{:S(2)}) collective-permute-start(bf16[32,640]{1,0:T(8,128)(2,1)S(1)} %get-tuple-element.36.piece_0), channel_id=1, source_target_pairs={{0,48},{16,32},{32,16},{48,0},{64,112},{80,96},{96,80},{112,64},{1... | collective-permute-start | bytes 122888 | tf_op jit(solution)/shard_map/ppermute | solution.py:309

commit v6 on v5

--- a/solution.py
+++ b/solution.py
@@ -337,9 +337,9 @@
     w_own = lax.all_to_all(
         spread_weights(w_key, w_value, 8), "sample", 0, 0, tiled=True, axis_index_groups=same_core)
     prompt_pieces = share(meet(jnp.concatenate([prompt_latent, prompt_rope, prompt_rope], axis=1)))
+    w_own, *prompt_pieces = lax.optimization_barrier((w_own, *prompt_pieces))
+    w_other = lax.ppermute(w_own, "sample", [(i, i ^ 1) for i in range(16)])
     keys = join_keys(prompt_pieces, resp_latent, resp_rope)
-    w_own, keys = lax.optimization_barrier((w_own, keys))
-    w_other = lax.ppermute(w_own, "sample", [(i, i ^ 1) for i in range(16)])
     held = (q_nope, q_rope, out_grad, keys, w_own, w_other)
     terms, later_facts = lax.optimization_barrier((attention(True, facts, *held), facts))
     attn_out, grad_query_nope, grad_query_rope = attention(False, later_facts, *held)

time: 98.7 us -> 98 us (level)
  no operation moved by 1% of the time
where the time goes in v6:
time: 98 us; the launch traced here: 97.2 us
  starting transfers between devices  47.7 us (49%)
  Pallas kernels  24.3 us (25%)
  waiting for transfers between devices  18.6 us (19%)
  local copies, waits for them, and re-layouts  3.71 us (4%)
  between operations  2.12 us (2%)
    ppermute x7, starting transfers between devices, from_distance(): return lax.ppermute(block, 'ctx', [(i, i ^ distance) for i in range(8)])  26.2 us
    pallas_call x2, Pallas kernels, attention(): pl.pallas_call(kernel, grid=(steps,), in_specs=[pl.BlockSpec(memory_space...  18.6 us
    ppermute x7, waiting for transfers between devices, from_distance(): return lax.ppermute(block, 'ctx', [(i, i ^ distance) for i in range(8)])  8.35 us
    all_to_all x1, waiting for transfers between devices, per_device(): lax.all_to_all(terms, 'ctx', 0, 0, tiled=True)  7.42 us
    all_to_all x1, starting transfers between devices, per_device(): lax.all_to_all(spread_weights(w_key, w_value, 8), 'sample', 0, 0, tiled=T...  6.8 us
    all_to_all x1, starting transfers between devices, per_device(): lax.all_to_all(terms, 'ctx', 0, 0, tiled=True)  6.76 us
    all_to_all x1, starting transfers between devices, per_device(): prompt_part = lax.all_to_all(prompt_part, 'sample', 0, 0, tiled=True)  4.15 us
    ppermute x1, starting transfers between devices, per_device(): w_other = lax.ppermute(w_own, 'sample', [(i, i ^ 1) for i in range(16)])  3.76 us
  transfers between devices with their start and end apart: 11, of which 8 were waited for; matrix products, arithmetic and copies ran while one was open for 1% of the time, Pallas kernels for 9%

profile of v6, /device:TPU:1, one launch (start us, length us, event | category | flops | bytes accessed | tf_op | source)
XLA Modules:
  0.0 97.2 jit_solution(16783560879392728517)
XLA Ops:
  0.6 2.4 %spread_weights.1 = bf16[8,64,2048]{2,1,0:T(8,128)(2,1)} custom-call(bf16[32,2048]{1,0:T(8,128)(2,1)} %key_ref.1, bf16[32,2048]{1,0:T(8,128)(2,1)} %value_ref.1), custom_call_target="tpu_custom_call" | custom-call | tf_op jit(solution)/shard_map/spread_weights/pallas_call | solution.py:38
  3.1 6.8 %all-to-all-start = ((bf16[8,64,2048]{2,1,0:T(8,128)(2,1)}), bf16[8,64,2048]{2,1,0:T(8,128)(2,1)S(1)}, u32[]{:S(2)}, u32[]{:S(2)}) async-start(bf16[8,64,2048]{2,1,0:T(8,128)(2,1)} %spread_weights.1), calls=%async_computation | async-start | bytes 4194304 | tf_op jit(solution)/shard_map/all_to_all | solution.py:337
  10.0 7.4 %collective-permute-start = (bf16[32,640]{1,0:T(8,128)(2,1)S(1)}, bf16[32,640]{1,0:T(8,128)(2,1)S(1)}, u32[]{:S(2)}, u32[]{:S(2)}) collective-permute-start(bf16[32,640]{1,0:T(8,128)(2,1)S(1)} %pad_maximum_fusion.1), channel_id=1, source_target_pairs={{0,64},{16,80},{32,96},{48,112},{64,0},{80,16},{96,32},{112,48},{1... | collective-permute-start | bytes 122888 | tf_op jit(solution)/shard_map/ppermute | solution.py:309
  17.4 1.4 %collective-permute-done = bf16[32,640]{1,0:T(8,128)(2,1)S(1)} collective-permute-done((bf16[32,640]{1,0:T(8,128)(2,1)S(1)}, bf16[32,640]{1,0:T(8,128)(2,1)S(1)}, u32[]{:S(2)}, u32[]{:S(2)}) %collective-permute-start) | collective-permute-done | bytes 40992 | tf_op jit(solution)/shard_map/ppermute | solution.py:309
  18.9 3.1 %collective-permute-start.1 = (bf16[64,640]{1,0:T(8,128)(2,1)S(1)}, bf16[64,640]{1,0:T(8,128)(2,1)S(1)}, u32[]{:S(2)}, u32[]{:S(2)}) collective-permute-start(bf16[64,640]{1,0:T(8,128)(2,1)S(1)} %pad_maximum_fusion.piece_0), channel_id=1, source_target_pairs={{0,16},{16,0},{32,48},{48,32},{64,80},{80,64},{96,112},{112,96},{1... | collective-permute-start | bytes 245768 | tf_op jit(solution)/shard_map/ppermute | solution.py:309
  22.0 4.1 %collective-permute-start.2 = (bf16[64,640]{1,0:T(8,128)(2,1)S(1)}, bf16[64,640]{1,0:T(8,128)(2,1)S(1)}, u32[]{:S(2)}, u32[]{:S(2)}) collective-permute-start(bf16[64,640]{1,0:T(8,128)(2,1)S(1)} %pad_maximum_fusion.piece_0), channel_id=1, source_target_pairs={{0,32},{16,48},{32,0},{48,16},{64,96},{80,112},{96,64},{112,80},{1... | collective-permute-start | bytes 245768 | tf_op jit(solution)/shard_map/ppermute | solution.py:309
  26.1 2.3 %collective-permute-start.3 = (bf16[64,640]{1,0:T(8,128)(2,1)S(1)}, bf16[64,640]{1,0:T(8,128)(2,1)S(1)}, u32[]{:S(2)}, u32[]{:S(2)}) collective-permute-start(bf16[64,640]{1,0:T(8,128)(2,1)S(1)} %pad_maximum_fusion.piece_0), channel_id=1, source_target_pairs={{0,48},{16,32},{32,16},{48,0},{64,112},{80,96},{96,80},{112,64},{1... | collective-permute-start | bytes 245768 | tf_op jit(solution)/shard_map/ppermute | solution.py:309
  29.2 4.7 %collective-permute-done.3.piece_3 = bf16[64,640]{1,0:T(8,128)(2,1)S(1)} collective-permute-done((bf16[64,640]{1,0:T(8,128)(2,1)S(1)}, bf16[64,640]{1,0:T(8,128)(2,1)S(1)}, u32[]{:S(2)}, u32[]{:S(2)}) %collective-permute-start.3) | collective-permute-done | bytes 81952 | tf_op jit(solution)/shard_map/ppermute | solution.py:309
  33.9 1.1 %all-to-all-done.wk_own.wv_own = bf16[8,64,2048]{2,1,0:T(8,128)(2,1)S(1)} async-done(((bf16[8,64,2048]{2,1,0:T(8,128)(2,1)}), bf16[8,64,2048]{2,1,0:T(8,128)(2,1)S(1)}, u32[]{:S(2)}, u32[]{:S(2)}) %all-to-all-start) | async-done | bytes 2097184 | tf_op jit(solution)/shard_map/all_to_all | solution.py:337
  35.1 3.8 %collective-permute-start.4 = (bf16[8,64,2048]{2,1,0:T(8,128)(2,1)S(1)}, bf16[8,64,2048]{2,1,0:T(8,128)(2,1)}, u32[]{:S(2)}, u32[]{:S(2)}) collective-permute-start(bf16[8,64,2048]{2,1,0:T(8,128)(2,1)S(1)} %all-to-all-done.wk_own.wv_own), channel_id=1, source_target_pairs={{0,1},{1,0},{2,3},{3,2},{4,5},{5,4},{6,7},{7,6},{8,9},{9,8},{10,11... | collective-permute-start | bytes 6291464 | tf_op jit(solution)/shard_map/ppermute | solution.py:341
  41.6 1.1 %collective-permute-done.4.wk_oth.wv_oth = bf16[8,64,2048]{2,1,0:T(8,128)(2,1)} collective-permute-done((bf16[8,64,2048]{2,1,0:T(8,128)(2,1)S(1)}, bf16[8,64,2048]{2,1,0:T(8,128)(2,1)}, u32[]{:S(2)}, u32[]{:S(2)}) %collective-permute-start.4) | collective-permute-done | bytes 2097184 | tf_op jit(solution)/shard_map/ppermute | solution.py:341
  42.8 10.4 %key_terms.1 = bf16[8,32,1152]{2,1,0:T(8,128)(2,1)} custom-call(s32[4]{0:T(128)} %pad_add_fusion.facts_ref, bf16[128,2048]{1,0:T(8,128)(2,1)} %qn_ref.3, bf16[128,1024]{1,0:T(8,128)(2,1)} %qr_ref.3, bf16[128,2048]{1,0:T(8,128)(2,1)} %og_ref.3, bf16[384,640]{1,0:T(8,128)(2,1)} %join_keys.1.keys_ref, bf16[8,64,2048]{2,1,0:T(8,128)(2,1)} %copy-done, ...), custom_call_target="tpu_custom_call" | custom-call | flops 6000000000 | bytes 8388608 | tf_op jit(solution)/shard_map/key_terms/pallas_call | solution.py:201
  53.2 6.8 %all-to-all-start.1 = ((bf16[8,32,1152]{2,1,0:T(8,128)(2,1)}), bf16[8,32,1152]{2,1,0:T(8,128)(2,1)S(1)}, u32[]{:S(2)}, u32[]{:S(2)}) async-start(bf16[8,32,1152]{2,1,0:T(8,128)(2,1)} %key_terms.1), calls=%async_computation.1 | async-start | bytes 1179648 | tf_op jit(solution)/shard_map/all_to_all | solution.py:347
  60.0 1.6 %copy-done.1 = bf16[8,64,2048]{2,1,0:T(8,128)(2,1)S(1)} copy-done((bf16[8,64,2048]{2,1,0:T(8,128)(2,1)S(1)}, bf16[8,64,2048]{2,1,0:T(8,128)(2,1)}, u32[]{:S(2)}) %copy-start.1) | copy-done | bytes 2097176
  62.6 1.0 %copy-done.7 = bf16[128,2048]{1,0:T(8,128)(2,1)S(1)} copy-done((bf16[128,2048]{1,0:T(8,128)(2,1)S(1)}, bf16[128,2048]{1,0:T(8,128)(2,1)}, u32[]{:S(2)}) %copy-start.7) | copy-done | bytes 524312
  63.6 8.2 %attention.1 = (bf16[128,2048]{1,0:T(8,128)(2,1)}, bf16[128,2048]{1,0:T(8,128)(2,1)}, bf16[128,1024]{1,0:T(8,128)(2,1)}) custom-call(s32[4]{0:T(128)S(1)} %copy-done.5, bf16[128,2048]{1,0:T(8,128)(2,1)S(1)} %copy-done.6, bf16[128,1024]{1,0:T(8,128)(2,1)S(1)} %copy-done.8, bf16[128,2048]{1,0:T(8,128)(2,1)S(1)} %copy-done.7, bf16[384,640]{1,0:T(8,128)(2,1)S(1)} %copy-done.2, ...), custom_call_target="tpu_custom_call" | custom-call | flops 6000000000 | bytes 8388608 | tf_op jit(solution)/shard_map/attention/pallas_call | solution.py:201
  71.9 7.4 %all-to-all-done.1.terms_ref = bf16[8,32,1152]{2,1,0:T(8,128)(2,1)S(1)} async-done(((bf16[8,32,1152]{2,1,0:T(8,128)(2,1)}), bf16[8,32,1152]{2,1,0:T(8,128)(2,1)S(1)}, u32[]{:S(2)}, u32[]{:S(2)}) %all-to-all-start.1) | async-done | bytes 589856 | tf_op jit(solution)/shard_map/all_to_all | solution.py:347
  79.3 1.0 %add_heads.1 = (bf16[16,32,640]{2,1,0:T(8,128)(2,1)}, bf16[32,640]{1,0:T(8,128)(2,1)S(1)}) custom-call(bf16[8,32,1152]{2,1,0:T(8,128)(2,1)S(1)} %all-to-all-done.1.terms_ref), custom_call_target="tpu_custom_call" | custom-call | tf_op jit(solution)/shard_map/add_heads/pallas_call | solution.py:257
  80.3 4.2 %all-to-all-start.2 = ((bf16[16,32,640]{2,1,0:T(8,128)(2,1)}), bf16[16,32,640]{2,1,0:T(8,128)(2,1)S(1)}, u32[]{:S(2)}, u32[]{:S(2)}) async-start(bf16[16,32,640]{2,1,0:T(8,128)(2,1)} %get-tuple-element.41), calls=%async_computation.2 | async-start | bytes 1310720 | tf_op jit(solution)/shard_map/all_to_all | solution.py:349
  84.5 2.2 %collective-permute-start.5 = (bf16[32,640]{1,0:T(8,128)(2,1)S(1)}, bf16[32,640]{1,0:T(8,128)(2,1)S(1)}, u32[]{:S(2)}, u32[]{:S(2)}) collective-permute-start(bf16[32,640]{1,0:T(8,128)(2,1)S(1)} %get-tuple-element.42.piece_0), channel_id=1, source_target_pairs={{0,16},{16,0},{32,48},{48,32},{64,80},{80,64},{96,112},{112,96},{1... | collective-permute-start | bytes 122888 | tf_op jit(solution)/shard_map/ppermute | solution.py:309
  86.7 1.9 %collective-permute-start.6 = (bf16[32,640]{1,0:T(8,128)(2,1)S(1)}, bf16[32,640]{1,0:T(8,128)(2,1)S(1)}, u32[]{:S(2)}, u32[]{:S(2)}) collective-permute-start(bf16[32,640]{1,0:T(8,128)(2,1)S(1)} %get-tuple-element.42.piece_0), channel_id=1, source_target_pairs={{0,32},{16,48},{32,0},{48,16},{64,96},{80,112},{96,64},{112,80},{1... | collective-permute-start | bytes 122888 | tf_op jit(solution)/shard_map/ppermute | solution.py:309
  88.6 5.2 %collective-permute-start.7 = (bf16[32,640]{1,0:T(8,128)(2,1)S(1)}, bf16[32,640]{1,0:T(8,128)(2,1)S(1)}, u32[]{:S(2)}, u32[]{:S(2)}) collective-permute-start(bf16[32,640]{1,0:T(8,128)(2,1)S(1)} %get-tuple-element.42.piece_0), channel_id=1, source_target_pairs={{0,48},{16,32},{32,16},{48,0},{64,112},{80,96},{96,80},{112,64},{1... | collective-permute-start | bytes 122888 | tf_op jit(solution)/shard_map/ppermute | solution.py:309
  93.8 1.5 %collective-permute-done.7.piece_3 = bf16[32,640]{1,0:T(8,128)(2,1)S(1)} collective-permute-done((bf16[32,640]{1,0:T(8,128)(2,1)S(1)}, bf16[32,640]{1,0:T(8,128)(2,1)S(1)}, u32[]{:S(2)}, u32[]{:S(2)}) %collective-permute-start.7) | collective-permute-done | bytes 40992 | tf_op jit(solution)/shard_map/ppermute | solution.py:309
  95.9 1.3 %finish.1 = (f32[32,512]{1,0:T(8,128)}, f32[32,64]{1,0:T(8,128)}, f32[128,512]{1,0:T(8,128)}, f32[64,128]{1,0:T(8,128)}) custom-call(s32[4]{0:T(128)S(1)} %copy-done.5, bf16[16,32,640]{2,1,0:T(8,128)(2,1)S(1)} %all-to-all-done.2.prompt_ref, bf16[32,640]{1,0:T(8,128)(2,1)S(1)} %get-tuple-element.42.piece_0, ...), custom_call_target="tpu_custom_call" | custom-call | tf_op jit(solution)/shard_map/finish/pallas_call | solution.py:292
  (29 shorter events, 4.0 us)
Async XLA Ops:
  3.0 6.9 %copy-start.9 = (bf16[32,512]{1,0:T(8,128)(2,1)S(1)}, bf16[32,512]{1,0:T(8,128)(2,1)}, u32[]{:S(2)}) copy-start(bf16[32,512]{1,0:T(8,128)(2,1)} %param.13) | copy-start | bytes 98308
  3.1 6.8 %copy-start.10 = (bf16[32,64]{1,0:T(8,128)(2,1)S(1)}, bf16[32,64]{1,0:T(8,128)(2,1)}, u32[]{:S(2)}) copy-start(bf16[32,64]{1,0:T(8,128)(2,1)} %param.14) | copy-start | bytes 12292
  3.1 37.7 %copy-start.3 = (bf16[128,512]{1,0:T(8,128)(2,1)S(1)}, bf16[128,512]{1,0:T(8,128)(2,1)}, u32[]{:S(2)}) copy-start(bf16[128,512]{1,0:T(8,128)(2,1)} %lat_ref.1) | copy-start | bytes 393220
  3.1 37.7 %copy-start.4 = (bf16[128,64]{0,1:T(8,128)(2,1)S(1)}, bf16[128,64]{0,1:T(8,128)(2,1)}, u32[]{:S(2)}) copy-start(bf16[128,64]{0,1:T(8,128)(2,1)} %param.16) | copy-start | bytes 49156
  3.1 32.0 %all-to-all-start = ((bf16[8,64,2048]{2,1,0:T(8,128)(2,1)}), bf16[8,64,2048]{2,1,0:T(8,128)(2,1)S(1)}, u32[]{:S(2)}, u32[]{:S(2)}) async-start(bf16[8,64,2048]{2,1,0:T(8,128)(2,1)} %spread_weights.1), calls=%async_computation | async-start | bytes 4194304 | tf_op jit(solution)/shard_map/all_to_all | solution.py:337
  10.0 8.9 %collective-permute-start = (bf16[32,640]{1,0:T(8,128)(2,1)S(1)}, bf16[32,640]{1,0:T(8,128)(2,1)S(1)}, u32[]{:S(2)}, u32[]{:S(2)}) collective-permute-start(bf16[32,640]{1,0:T(8,128)(2,1)S(1)} %pad_maximum_fusion.1), channel_id=1, source_target_pairs={{0,64},{16,80},{32,96},{48,112},{64,0},{80,16},{96,32},{112,48},{1... | collective-permute-start | bytes 122888 | tf_op jit(solution)/shard_map/ppermute | solution.py:309
  18.9 9.5 %collective-permute-start.1 = (bf16[64,640]{1,0:T(8,128)(2,1)S(1)}, bf16[64,640]{1,0:T(8,128)(2,1)S(1)}, u32[]{:S(2)}, u32[]{:S(2)}) collective-permute-start(bf16[64,640]{1,0:T(8,128)(2,1)S(1)} %pad_maximum_fusion.piece_0), channel_id=1, source_target_pairs={{0,16},{16,0},{32,48},{48,32},{64,80},{80,64},{96,112},{112,96},{1... | collective-permute-start | bytes 245768 | tf_op jit(solution)/shard_map/ppermute | solution.py:309
  22.0 7.2 %collective-permute-start.2 = (bf16[64,640]{1,0:T(8,128)(2,1)S(1)}, bf16[64,640]{1,0:T(8,128)(2,1)S(1)}, u32[]{:S(2)}, u32[]{:S(2)}) collective-permute-start(bf16[64,640]{1,0:T(8,128)(2,1)S(1)} %pad_maximum_fusion.piece_0), channel_id=1, source_target_pairs={{0,32},{16,48},{32,0},{48,16},{64,96},{80,112},{96,64},{112,80},{1... | collective-permute-start | bytes 245768 | tf_op jit(solution)/shard_map/ppermute | solution.py:309
  26.1 7.8 %collective-permute-start.3 = (bf16[64,640]{1,0:T(8,128)(2,1)S(1)}, bf16[64,640]{1,0:T(8,128)(2,1)S(1)}, u32[]{:S(2)}, u32[]{:S(2)}) collective-permute-start(bf16[64,640]{1,0:T(8,128)(2,1)S(1)} %pad_maximum_fusion.piece_0), channel_id=1, source_target_pairs={{0,48},{16,32},{32,16},{48,0},{64,112},{80,96},{96,80},{112,64},{1... | collective-permute-start | bytes 245768 | tf_op jit(solution)/shard_map/ppermute | solution.py:309
  35.1 7.7 %copy-start = (bf16[8,64,2048]{2,1,0:T(8,128)(2,1)}, bf16[8,64,2048]{2,1,0:T(8,128)(2,1)S(1)}, u32[]{:S(2)}) copy-start(bf16[8,64,2048]{2,1,0:T(8,128)(2,1)S(1)} %all-to-all-done.wk_own.wv_own) | copy-start | bytes 6291460
  35.1 7.7 %collective-permute-start.4 = (bf16[8,64,2048]{2,1,0:T(8,128)(2,1)S(1)}, bf16[8,64,2048]{2,1,0:T(8,128)(2,1)}, u32[]{:S(2)}, u32[]{:S(2)}) collective-permute-start(bf16[8,64,2048]{2,1,0:T(8,128)(2,1)S(1)} %all-to-all-done.wk_own.wv_own), channel_id=1, source_target_pairs={{0,1},{1,0},{2,3},{3,2},{4,5},{5,4},{6,7},{7,6},{8,9},{9,8},{10,11... | collective-permute-start | bytes 6291464 | tf_op jit(solution)/shard_map/ppermute | solution.py:341
  41.6 18.3 %copy-start.2 = (bf16[384,640]{1,0:T(8,128)(2,1)S(1)}, bf16[384,640]{1,0:T(8,128)(2,1)}, u32[]{:S(2)}) copy-start(bf16[384,640]{1,0:T(8,128)(2,1)} %join_keys.1.keys_ref) | copy-start | bytes 1474564
  41.6 18.3 %copy-start.5 = (s32[4]{0:T(128)S(1)}, s32[4]{0:T(128)}, u32[]{:S(2)}) copy-start(s32[4]{0:T(128)} %pad_add_fusion.facts_ref) | copy-start | bytes 52
  41.6 18.3 %copy-start.8 = (bf16[128,1024]{1,0:T(8,128)(2,1)S(1)}, bf16[128,1024]{1,0:T(8,128)(2,1)}, u32[]{:S(2)}) copy-start(bf16[128,1024]{1,0:T(8,128)(2,1)} %qr_ref.3) | copy-start | bytes 786436
  53.2 26.1 %all-to-all-start.1 = ((bf16[8,32,1152]{2,1,0:T(8,128)(2,1)}), bf16[8,32,1152]{2,1,0:T(8,128)(2,1)S(1)}, u32[]{:S(2)}, u32[]{:S(2)}) async-start(bf16[8,32,1152]{2,1,0:T(8,128)(2,1)} %key_terms.1), calls=%async_computation.1 | async-start | bytes 1179648 | tf_op jit(solution)/shard_map/all_to_all | solution.py:347
  59.9 1.6 %copy-start.1 = (bf16[8,64,2048]{2,1,0:T(8,128)(2,1)S(1)}, bf16[8,64,2048]{2,1,0:T(8,128)(2,1)}, u32[]{:S(2)}) copy-start(bf16[8,64,2048]{2,1,0:T(8,128)(2,1)} %copy-done) | copy-start | bytes 6291460
  61.5 1.0 %copy-start.6 = (bf16[128,2048]{1,0:T(8,128)(2,1)S(1)}, bf16[128,2048]{1,0:T(8,128)(2,1)}, u32[]{:S(2)}) copy-start(bf16[128,2048]{1,0:T(8,128)(2,1)} %qn_ref.3) | copy-start | bytes 1572868
  62.6 1.0 %copy-start.7 = (bf16[128,2048]{1,0:T(8,128)(2,1)S(1)}, bf16[128,2048]{1,0:T(8,128)(2,1)}, u32[]{:S(2)}) copy-start(bf16[128,2048]{1,0:T(8,128)(2,1)} %og_ref.3) | copy-start | bytes 1572868
  80.3 15.5 %all-to-all-start.2 = ((bf16[16,32,640]{2,1,0:T(8,128)(2,1)}), bf16[16,32,640]{2,1,0:T(8,128)(2,1)S(1)}, u32[]{:S(2)}, u32[]{:S(2)}) async-start(bf16[16,32,640]{2,1,0:T(8,128)(2,1)} %get-tuple-element.41), calls=%async_computation.2 | async-start | bytes 1310720 | tf_op jit(solution)/shard_map/all_to_all | solution.py:349
  84.5 9.3 %collective-permute-start.5 = (bf16[32,640]{1,0:T(8,128)(2,1)S(1)}, bf16[32,640]{1,0:T(8,128)(2,1)S(1)}, u32[]{:S(2)}, u32[]{:S(2)}) collective-permute-start(bf16[32,640]{1,0:T(8,128)(2,1)S(1)} %get-tuple-element.42.piece_0), channel_id=1, source_target_pairs={{0,16},{16,0},{32,48},{48,32},{64,80},{80,64},{96,112},{112,96},{1... | collective-permute-start | bytes 122888 | tf_op jit(solution)/shard_map/ppermute | solution.py:309
  86.7 7.1 %collective-permute-start.6 = (bf16[32,640]{1,0:T(8,128)(2,1)S(1)}, bf16[32,640]{1,0:T(8,128)(2,1)S(1)}, u32[]{:S(2)}, u32[]{:S(2)}) collective-permute-start(bf16[32,640]{1,0:T(8,128)(2,1)S(1)} %get-tuple-element.42.piece_0), channel_id=1, source_target_pairs={{0,32},{16,48},{32,0},{48,16},{64,96},{80,112},{96,64},{112,80},{1... | collective-permute-start | bytes 122888 | tf_op jit(solution)/shard_map/ppermute | solution.py:309
  88.6 6.7 %collective-permute-start.7 = (bf16[32,640]{1,0:T(8,128)(2,1)S(1)}, bf16[32,640]{1,0:T(8,128)(2,1)S(1)}, u32[]{:S(2)}, u32[]{:S(2)}) collective-permute-start(bf16[32,640]{1,0:T(8,128)(2,1)S(1)} %get-tuple-element.42.piece_0), channel_id=1, source_target_pairs={{0,48},{16,32},{32,16},{48,0},{64,112},{80,96},{96,80},{112,64},{1... | collective-permute-start | bytes 122888 | tf_op jit(solution)/shard_map/ppermute | solution.py:309
